TPU v7x, 32 devices: a whole 2x2x4 slice. The times are simulated.
32 devices in a mesh: groups: 1, mode: 32 (over z, y, x, core).
Axes of the slice: x: 2, y: 2, z: 4, core: 2. Of those that a mesh axis runs over, the one named last changes fastest.
Arguments:
- basis: bfloat16 [384, 16384], P('groups', 'mode')
- slab_region: int32 [128], P(('groups', 'mode')), may hold values from 0 to 8
- coef_index: int32 [9, 6], P('groups'), may hold values from 0 to 8
- coef_table: float32 [8], P('groups'), may hold values from 0.2 to 5
Outputs:
- gram: float32 [21, 384, 384], P(None, ('groups', 'mode'))
All inputs are finite; a program needn't handle non-finite values.
Results may differ from a plain program's by a relative error of at most 0.0005.
The roundings to bfloat16 on the way count: a program that leaves them out, or rounds other values in their place, can miss the bound.
Values may be sent and summed in bfloat16 or wider, within the bound.
No kernel may reach another device: no remote copies, remote signals or barrier semaphores. Data moves between devices by JAX's collectives and lax.ppermute only.
A program may use at most 128 MiB of HBM per device.

v0:
```python
import jax
import jax.numpy as jnp
from jax import lax
from jax.sharding import PartitionSpec as P


def extended(block, sides, width):
    for axis, dim in sides:
        count = lax.axis_size(axis)
        forward = [(i, i + 1) for i in range(count - 1)]
        forward.append((count - 1, 0))
        backward = [(target, source) for source, target in forward]
        low = lax.ppermute(
            lax.slice_in_dim(block, block.shape[dim] - width, None, axis=dim), axis, forward
        )
        high = lax.ppermute(lax.slice_in_dim(block, 0, width, axis=dim), axis, backward)
        block = jnp.concatenate([low, block, high], axis=dim)
    return block


def slab_weights(slab_region, coef_index, coef_table):
    regions = coef_index.shape[0]
    entries = coef_table.shape[0]
    table_hit = (
        coef_index[:, :, None] == jnp.arange(entries, dtype=jnp.int32)[None, None, :]
    ).astype(jnp.float32)
    kappa = jnp.sum(table_hit * coef_table[None, None, :], axis=2)
    region_hit = (slab_region[:, None] == jnp.arange(regions, dtype=jnp.int32)[None, :]).astype(
        jnp.float32
    )
    return jnp.sum(region_hit[:, :, None] * kappa[None, :, :], axis=1)


def term_actions(padded, slab_kappa):
    rows = padded.shape[0]
    slabs = padded.shape[1] - 2
    width = padded.shape[2]
    terms = slab_kappa.shape[1]
    field = padded[:, 1:-1, :].astype(jnp.float32)
    prev_s = padded[:, :-2, :].astype(jnp.float32)
    next_s = padded[:, 2:, :].astype(jnp.float32)
    zero_col = jnp.zeros((rows, slabs, 1), jnp.float32)
    left_w = jnp.concatenate([zero_col, field[:, :, :-1]], axis=2)
    right_w = jnp.concatenate([field[:, :, 1:], zero_col], axis=2)
    mirror = field[:, :, ::-1]
    stencils = [
        2.0 * field - prev_s - next_s,
        2.0 * field - left_w - right_w,
        field - prev_s,
        field - next_s,
        field - mirror,
        field,
    ]
    result = [
        (slab_kappa[None, :, term, None] * stencils[term])
        .reshape(rows, slabs * width)
        .astype(jnp.bfloat16)
        for term in range(terms)
    ]
    return jnp.stack(result, axis=0)


def per_device(basis, slab_region, coef_index, coef_table):
    terms = coef_index.shape[1]
    rows, cells_dev = basis.shape
    slabs_dev = slab_region.shape[0]
    width = cells_dev // slabs_dev
    devices = lax.axis_size("mode")
    total_cells = cells_dev * devices
    slab_kappa = slab_weights(slab_region, coef_index, coef_table)
    field = basis.reshape(rows, slabs_dev, width)
    padded = extended(field, (("mode", 1),), 1)
    actions = term_actions(padded, slab_kappa)
    pair_list = [(first, second) for first in range(terms) for second in range(first, terms)]
    values = actions.astype(jnp.float32)
    level_sums = lax.psum(jnp.sum(values * values, axis=(1, 2)), "mode")
    pieces = []
    for partial_first in range(terms):
        others = actions[partial_first:].reshape((terms - partial_first) * rows, cells_dev)
        pieces.append(
            lax.dot_general(
                actions[partial_first],
                others,
                (((1,), (1,)), ((), ())),
                preferred_element_type=jnp.float32,
            )
        )
    raw = lax.psum_scatter(
        jnp.concatenate(pieces, axis=1).reshape(rows, len(pair_list), rows),
        "mode",
        scatter_dimension=0,
        tiled=True,
    )
    level = level_sums / (rows * total_cells) + 1e-06
    factors = jnp.stack(
        [
            1.0 / (total_cells * jnp.sqrt(level[first] * level[second]))
            for first, second in pair_list
        ]
    )
    return jnp.transpose(raw * factors[None, :, None], (1, 0, 2))


def solution(mesh):
    return jax.shard_map(
        per_device,
        mesh=mesh,
        in_specs=(P("groups", "mode"), P(("groups", "mode")), P("groups", None), P("groups")),
        out_specs=P(None, ("groups", "mode"), None),
        check_vma=False,
    )
```

profile of v0, /device:TPU:0, one launch (start us, length us, event | category | flops | bytes accessed | tf_op | source)
XLA Modules:
  0.0 243.7 jit_solution(2782310361562966436)
XLA Ops:
  6.5 0.0 copy-start.9
  6.5 0.0 copy-start.8
  6.5 0.0 copy-start.10
  6.5 0.0 reduce-scatter.2.cloned.1.call-start
  6.5 1.1 reshape.267
  7.7 0.3 fusion.20
  8.0 0.5 collective-permute-start
  8.5 6.0 %collective-permute-start.1 = (bf16[384,1,128]{2,1,0:T(2,128)(2,1)S(1)}, bf16[384,1,128]{2,1,0:T(2,128)(2,1)S(1)}, u32[]{:S(2)}, u32[]{:S(2)}) collective-permute-start(bf16[384,1,128]{2,1,0:T(2,128)(2,1)S(1)} %get-tuple-element.23), channel_id=1, source_target_pairs={{1,0},{2,1},{3,2},{4,3},{5,4},{6,5},{7,6},{8,7},{9,8},{10,9},{11,1... | collective-permute-start | bytes 294920 | tf_op jit(solution)/shard_map/ppermute | solution.py:16
  14.5 1.2 fusion.19
  15.6 0.0 copy-done.9
  15.6 0.1 fusion.17
  15.7 0.0 copy-done.8
  15.7 0.0 copy-done.10
  15.7 0.1 select_reduce_fusion
  15.8 0.1 multiply_reduce_fusion.1
  15.9 0.6 slice_bitcast_fusion
  16.5 0.1 broadcast_bitcast_fusion
  16.5 0.9 rev.3
  17.4 0.4 collective-permute-done
  17.8 0.0 collective-permute-done.1
  17.8 3.9 %fusion.5 = (bf16[384,4,128]{2,1,0:T(4,128)(2,1)S(1)}, bf16[384,4,128]{2,1,0:T(4,128)(2,1)S(1)}, bf16[384,4,128]{2,1,0:T(4,128)(2,1)S(1)}, bf16[384,4,128]{2,1,0:T(4,128)(2,1)}, bf16[384,4,128]{2,1,0:T(4,128)(2,1)}) fusion(bf16[384,4,128]{2,1,0:T(4,128)(2,1)S(1)} %reshape.267, bf16[384,1,128]{2,1,0:T(2,128)(2,1)S(1)} %collective-permute-done.1, ...), kind=kLoop, calls=%fused_computation.18 | loop fusion | flops 5308416 | bytes 4902992 | tf_op jit(solution)/shard_map/convert_element_type | solution.py:57
  21.7 0.0 copy-start.3
  21.7 1.0 convert_element_type.112
  22.8 1.0 constant_dynamic-update-slice_fusion.5
  23.8 1.9 convert_element_type.114
  25.7 0.9 convert_element_type.116
  26.6 0.0 copy-done.3
  26.6 0.2 convert_element_type.118
  26.8 0.0 copy-done.1
  26.8 1.1 convert_element_type.120
  27.9 0.0 copy-start.7
  27.9 1.1 constant_dynamic-update-slice_fusion.10
  29.0 0.0 copy-start.5
  29.0 1.1 constant_dynamic-update-slice_fusion.9
  30.2 0.1 constant_dynamic-update-slice_fusion.8
  30.2 0.1 constant_dynamic-update-slice_fusion.7
  30.3 0.0 copy-done.7
  30.3 0.1 constant_dynamic-update-slice_fusion.6
  30.4 0.0 copy-done.5
  30.4 0.2 pad_maximum_fusion
  30.6 0.1 pad_maximum_fusion.1
  30.7 0.1 pad_maximum_fusion.2
  30.9 0.0 copy-start.6
  30.9 2.9 %convolution_dynamic-update-slice_fusion = f32[384,8064]{1,0:T(8,128)} fusion(bf16[2304,512]{1,0:T(8,128)(2,1)S(1)} %bitcast.51, bf16[48,8,4,128]{3,2,1,0:T(4,128)(2,1)S(1)} %bitcast.54), kind=kOutput, calls=%fused_computation | convolution fusion | flops 905969664 | bytes 6291456 | tf_op jit(solution)/shard_map/dot_general | solution.py:81
  33.8 0.0 copy-done.6
  33.8 0.0 copy-start.4
  33.8 2.6 %convolution_dynamic-update-slice_fusion.2 = f32[384,8064]{1,0:T(8,128)} fusion(f32[384,8064]{1,0:T(8,128)} %convolution_dynamic-update-slice_fusion, bf16[1920,512]{1,0:T(8,128)(2,1)S(1)} %bitcast.60, bf16[48,8,4,128]{3,2,1,0:T(4,128)(2,1)S(1)} %bitcast.58), kind=kOutput, calls=%fused_computation.3 | convolution fusion | flops 754974720 | bytes 5308416 | tf_op jit(solution)/shard_map/dot_general | solution.py:81
  36.4 0.0 copy-start.2
  36.4 0.0 copy-done.4
  36.4 2.2 convolution_dynamic-update-slice_fusion.1
  38.6 0.0 copy-done.2
  38.6 2.0 convolution_dynamic-update-slice_fusion.3
  40.6 0.0 copy-done
  40.7 1.6 convolution_dynamic-update-slice_fusion.4
  42.2 1.3 convolution_dynamic-update-slice_fusion.5
  43.5 12.6 %copy.16 = f32[384,8064]{0,1:T(8,128)} copy(f32[384,8064]{1,0:T(8,128)} %convolution_dynamic-update-slice_fusion.5) | data formatting | bytes 24772608 | tf_op jit(solution)/shard_map/concatenate | solution.py:89
  56.1 14.8 %copy.17 = f32[384,21,384]{2,1,0:T(8,128)} copy(f32[384,21,384]{0,2,1:T(8,128)} %bitcast.50) | data formatting | bytes 24772608 | tf_op jit(solution)/shard_map/reshape | solution.py:89
  70.9 0.0 reduce-scatter.2.cloned.1.call-update
  70.9 0.6 multiply_reduce_fusion
  71.6 38.7 %psum.7 = f32[6]{0:T(128)S(1)} all-reduce(f32[6]{0:T(128)S(1)} %multiply_reduce_fusion), channel_id=1, replica_groups=mesh['groups'=1,'mode'=32] {'mode'}, use_global_device_ids=true, to_apply=%region_4.0 | all-reduce | flops 6 | bytes 48 | tf_op jit(solution)/shard_map/psum | solution.py:76
  110.3 0.7 fusion.21
  139.5 0.1 stack.20
  139.6 95.5 %reduce-scatter.2.cloned.1.call-done = f32[12,21,384]{2,1,0:T(8,128)} async-done(((f32[384,21,384]{2,1,0:T(8,128)}), f32[12,21,384]{2,1,0:T(8,128)}) %reduce-scatter.2.cloned.1.call-update) | async-done | bytes 387088 | tf_op jit(solution)/shard_map/reduce_scatter | solution.py:88
  235.0 1.9 multiply_bitcast_fusion
  (4 shorter events, 0.0 us)
Async XLA Ops:
  6.5 9.1 %copy-start.9 = (s32[4]{0:T(128)S(1)}, s32[4]{0:T(128)}, u32[]{:S(2)}) copy-start(s32[4]{0:T(128)} %param.5) | copy-start | bytes 52
  6.5 9.2 %copy-start.8 = (s32[9,6]{0,1:T(8,128)S(1)}, s32[9,6]{0,1:T(8,128)}, u32[]{:S(2)}) copy-start(s32[9,6]{0,1:T(8,128)} %param.6) | copy-start | bytes 652
  6.5 9.2 %copy-start.10 = (f32[8]{0:T(128)S(1)}, f32[8]{0:T(128)}, u32[]{:S(2)}) copy-start(f32[8]{0:T(128)} %param.7) | copy-start | bytes 100
  6.5 228.5 %reduce-scatter.2.cloned.1.call-start = ((), (), s32[]{:S(2)}) async-start(), calls=%async_computation.1 | async-start | bytes 14598144 | tf_op jit(solution)/shard_map/reduce_scatter | solution.py:88
  8.0 9.9 %collective-permute-start = (bf16[384,1,128]{2,1,0:T(2,128)(2,1)S(1)}, bf16[384,1,128]{2,1,0:T(2,128)(2,1)S(1)}, u32[]{:S(2)}, u32[]{:S(2)}) collective-permute-start(bf16[384,1,128]{2,1,0:T(2,128)(2,1)S(1)} %get-tuple-element.22), channel_id=1, source_target_pairs={{0,1},{1,2},{2,3},{3,4},{4,5},{5,6},{6,7},{7,8},{8,9},{9,10},{10,1... | collective-permute-start | bytes 294920 | tf_op jit(solution)/shard_map/ppermute | solution.py:13
  8.5 9.4 %collective-permute-start.1 = (bf16[384,1,128]{2,1,0:T(2,128)(2,1)S(1)}, bf16[384,1,128]{2,1,0:T(2,128)(2,1)S(1)}, u32[]{:S(2)}, u32[]{:S(2)}) collective-permute-start(bf16[384,1,128]{2,1,0:T(2,128)(2,1)S(1)} %get-tuple-element.23), channel_id=1, source_target_pairs={{1,0},{2,1},{3,2},{4,3},{5,4},{6,5},{7,6},{8,7},{9,8},{10,9},{11,1... | collective-permute-start | bytes 294920 | tf_op jit(solution)/shard_map/ppermute | solution.py:16
  21.7 4.9 %copy-start.3 = (bf16[384,4,128]{2,1,0:T(4,128)(2,1)}, bf16[384,4,128]{2,1,0:T(4,128)(2,1)S(1)}, u32[]{:S(2)}) copy-start(bf16[384,4,128]{2,1,0:T(4,128)(2,1)S(1)} %get-tuple-element.9) | copy-start | bytes 1179652
  21.7 5.0 %copy-start.1 = (bf16[384,4,128]{2,1,0:T(4,128)(2,1)}, bf16[384,4,128]{2,1,0:T(4,128)(2,1)S(1)}, u32[]{:S(2)}) copy-start(bf16[384,4,128]{2,1,0:T(4,128)(2,1)S(1)} %get-tuple-element.7) | copy-start | bytes 1179652
  27.9 2.4 copy-start.7
  29.0 1.4 copy-start.5
  30.9 2.9 %copy-start.6 = (bf16[384,4,128]{2,1,0:T(4,128)(2,1)S(1)}, bf16[384,4,128]{2,1,0:T(4,128)(2,1)}, u32[]{:S(2)}) copy-start(bf16[384,4,128]{2,1,0:T(4,128)(2,1)} %get-tuple-element.19) | copy-start | bytes 1179652
  33.8 2.6 %copy-start.4 = (bf16[384,4,128]{2,1,0:T(4,128)(2,1)S(1)}, bf16[384,4,128]{2,1,0:T(4,128)(2,1)}, u32[]{:S(2)}) copy-start(bf16[384,4,128]{2,1,0:T(4,128)(2,1)} %copy-done.3) | copy-start | bytes 1179652
  36.4 2.2 copy-start.2
  38.6 2.0 copy-start
Sparse Core Ops, SparseCore 0:
  71.0 163.9 reduce-scatter.1
where the time goes:
time: 245 us; the launch traced here: 244 us
  waiting for transfers between devices  95.9 us (39%)
  between operations  42.1 us (17%)
  local copies, waits for them, and re-layouts  40.8 us (17%)
  blocking collectives  38.7 us (16%)
  matrix products  12.6 us (5%)
  other arithmetic  7.13 us (3%)
  starting transfers between devices  6.49 us (3%)
    reduce_scatter x1, waiting for transfers between devices, per_device(): lax.psum_scatter(jnp.concatenate(pieces, axis=1).reshape(rows, len(pair_l...  95.5 us
    psum x1, blocking collectives, per_device(): level_sums = lax.psum(jnp.sum(values * values, axis=(1, 2)), 'mode')  38.7 us
    reshape x1, local copies, waits for them, and re-layouts, per_device(): jnp.concatenate(pieces, axis=1).reshape(rows, len(pair_list), rows)  14.8 us
    dot_general x6, matrix products, per_device(): lax.dot_general(actions[partial_first], others, (((1,), (1,)), ((), ())),...  12.6 us
    concatenate x1, local copies, waits for them, and re-layouts, per_device(): jnp.concatenate(pieces, axis=1).reshape(rows, len(pair_list), rows)  12.6 us
    ppermute x1, starting transfers between devices, extended(): lax.ppermute(lax.slice_in_dim(block, 0, width, axis=dim), axis, backward)  5.99 us
    convert_element_type x5, local copies, waits for them, and re-layouts, term_actions(): result = [(slab_kappa[None, :, term, None] * stencils[term]).reshape(rows...  5.13 us
  transfers between devices with their start and end apart: 3, of which 2 were waited for; matrix products, arithmetic and copies ran while one was open for 2% of the time, Pallas kernels for 0%

commit v1 on v0

v1 whole, which is shorter than its diff:
```python
import functools

import jax
import jax.numpy as jnp
from jax import lax
from jax.experimental import pallas as pl
from jax.experimental.pallas import tpu as pltpu
from jax.sharding import PartitionSpec as P

GROUP = 8
KROWS = 32
LIMIT = 2.0**15
F32 = jnp.float32
BF16 = jnp.bfloat16
VMEM = pl.BlockSpec(memory_space=pltpu.VMEM)
SMEM = pl.BlockSpec(memory_space=pltpu.SMEM)


def params():
    return pltpu.CompilerParams(vmem_limit_bytes=40 * 1024 * 1024)


def shape(dims, dtype=F32):
    return jax.ShapeDtypeStruct(dims, dtype)


def payload_kernel(basis, region, index, table, first, second):
    rows, cells = basis.shape
    slabs = region.shape[0]
    width = cells // slabs
    terms = index.shape[1]
    entries = table.shape[0]
    half = first.shape[0]
    row = lax.broadcasted_iota(jnp.int32, (KROWS, width), 0)
    for s in range(slabs):
        reg = region[s]
        block = jnp.zeros((KROWS, width), F32)
        for q in range(terms):
            at = index[reg, q]
            kappa = jnp.where(at < entries, table[jnp.minimum(at, entries - 1)], 0.0)
            full = jnp.full((KROWS, width), kappa, F32)
            high = full.astype(BF16).astype(F32)
            mid = (full - high).astype(BF16).astype(F32)
            low = (full - high - mid).astype(BF16).astype(F32)
            block = jnp.where(row == 3 * q, high, block)
            block = jnp.where(row == 3 * q + 1, mid, block)
            block = jnp.where(row == 3 * q + 2, low, block)
        first[0:KROWS, s * width : (s + 1) * width] = block.astype(BF16)
    first[KROWS:half, :] = basis[0 : half - KROWS, :]
    second[...] = basis[half - KROWS :, :]


def payload(basis, region, index, table):
    rows, cells = basis.shape
    half = (rows + KROWS) // 2
    return pl.pallas_call(
        payload_kernel,
        out_shape=(shape((half, cells), BF16), shape((half, cells), BF16)),
        in_specs=[VMEM, SMEM, SMEM, SMEM],
        out_specs=(VMEM, VMEM),
        compiler_params=params(),
    )(basis, region, index, table)


def flip(values, mask, count):
    return lax.ppermute(values, "mode", [(i, i ^ mask) for i in range(count)])


def gather(first, second, count):
    x, y, core = 2, 4, 1
    fx, sy = flip(first, x, count), flip(second, y, count)
    fy, sx = flip(first, y, count), flip(second, x, count)
    fxy, sxy = flip(fx, y, count), flip(sy, x, count)
    firsts = {0: first, 2: fx, 4: fy, 6: fxy}
    seconds = {0: second, 2: sx, 4: sy, 6: sxy}
    for mask in (0, 2, 4, 6):
        firsts[mask + 1] = flip(firsts[mask], core, count)
        seconds[mask + 1] = flip(seconds[mask], core, count)
    return [firsts[m] for m in range(GROUP)] + [seconds[m] for m in range(GROUP)]


def place(count):
    me = lax.axis_index("mode")
    return lax.rem(me, GROUP), lax.div(me, GROUP)


def selector(own, rows, planes):
    j, a = place(None)
    line = lax.broadcasted_iota(jnp.int32, (planes * own, rows), 0)
    column = lax.broadcasted_iota(jnp.int32, (planes * own, rows), 1)
    shift = jnp.zeros((planes * own, rows), jnp.int32)
    for k in range(planes):
        start = lax.rem(a + k, planes) * (GROUP * own) + j * own - k * own
        shift = jnp.where(line >= k * own, start, shift)
    return jnp.where(column - line == shift, 1.0, 0.0).astype(BF16)


def assemble_kernel(own, planes, *refs):
    pieces, (field, weights) = refs[: 2 * GROUP], refs[2 * GROUP :]
    j, _ = place(None)
    half, cells = pieces[0].shape
    width = field.shape[2]
    slabs = cells // width
    rows = 2 * half - KROWS
    pick = selector(own, rows, planes)
    for mask in range(GROUP):
        owner = jnp.bitwise_xor(j, mask)
        for s in range(slabs):
            lanes = slice(s * width, (s + 1) * width)
            weights[owner * slabs + s] = pieces[mask][0:KROWS, lanes]
            block = jnp.concatenate(
                [pieces[mask][KROWS:half, lanes], pieces[GROUP + mask][:, lanes]], axis=0
            )
            field[owner * slabs + s, 0:rows] = block
            field[owner * slabs + s, rows:] = jnp.dot(
                pick, block, preferred_element_type=F32
            ).astype(BF16)


def assemble(pieces, own, planes, width):
    half, cells = pieces[0].shape
    slabs = GROUP * (cells // width)
    rows = 2 * half - KROWS
    return pl.pallas_call(
        functools.partial(assemble_kernel, own, planes),
        out_shape=(
            shape((slabs, rows + planes * own, width), BF16),
            shape((slabs, KROWS, width), BF16),
        ),
        in_specs=[VMEM] * (2 * GROUP),
        out_specs=(VMEM, VMEM),
        compiler_params=params(),
    )(*pieces)


def across(width):
    line = lax.broadcasted_iota(jnp.int32, (width, width), 0)
    column = lax.broadcasted_iota(jnp.int32, (width, width), 1)
    same = jnp.where(line == column, 1.0, 0.0)
    beside = jnp.where(jnp.abs(line - column) == 1, 1.0, 0.0)
    mirror = jnp.where(line + column == width - 1, 1.0, 0.0)
    return jnp.concatenate([2.0 * same - beside, same - mirror], axis=1).astype(BF16)


def act(triples, weights, stencil, side, right, left, squares, rows, terms):
    total = triples[0][1].shape[0]
    own = total - rows
    width = triples[0][1].shape[1]
    chunk = own
    for n, (before, here, after, weight) in enumerate(triples):
        lanes = slice(n * width, (n + 1) * width)
        side[...] = jnp.dot(here[...], stencil, preferred_element_type=F32)
        table = weight[...].astype(F32)
        kappas = []
        for q in range(terms):
            one = table[3 * q : 3 * q + 1] + table[3 * q + 1 : 3 * q + 2] + table[3 * q + 2 : 3 * q + 3]
            kappas.append(jnp.broadcast_to(one, (8, width))[None])
        sums = [jnp.zeros((8, width), F32) for _ in range(terms)]
        for start in range(0, total, chunk):
            part = slice(start, start + chunk)
            value = here[part, :].astype(F32)
            back = value - before[part, :].astype(F32)
            ahead = value - after[part, :].astype(F32)
            shapes = (
                back + ahead,
                side[part, 0:width],
                back,
                ahead,
                side[part, width : 2 * width],
                value,
            )
            for q in range(terms):
                action = (shapes[q].reshape(chunk // 8, 8, width) * kappas[q]).reshape(chunk, width)
                action = action.astype(BF16)
                if start < rows:
                    right[q, part, lanes] = action
                    back32 = action.astype(F32)
                    sums[q] += jnp.sum((back32 * back32).reshape(chunk // 8, 8, width), axis=0)
                else:
                    left[q * own : (q + 1) * own, lanes] = action
        for q in range(terms):
            squares[q] += sums[q]


def contract(left, right, total, own, terms):
    offset = 0
    for k in range(terms):
        lines = own * (k + 1)
        total[offset : offset + lines, :] += lax.dot_general(
            left[0:lines, :],
            right[k],
            (((1,), (1,)), ((), ())),
            preferred_element_type=F32,
        )
        offset += lines


def inner_kernel(rows, terms, field, weights, total, squares, side, right, left):
    slabs = field.shape[0]
    own = field.shape[1] - rows
    stencil = across(field.shape[2])
    total[...] = jnp.zeros_like(total)
    squares[...] = jnp.zeros_like(squares)

    @pl.loop(0, (slabs - 2) // 2)
    def _(t):
        s = 2 * t + 1
        triples = [
            (field.at[s + n - 1], field.at[s + n], field.at[s + n + 1], weights.at[s + n])
            for n in range(2)
        ]
        act(triples, weights, stencil, side, right, left, squares, rows, terms)
        contract(left, right, total, own, terms)


def outer_kernel(
    rows, terms, own, planes, field, weights, low, high, total_in, squares_in,
    mine, others, levels, total, squares, ends, side, right, left,
):
    slabs, every, width = field.shape
    lines = every - rows
    stencil = across(width)
    pick = selector(own, rows, planes)
    total[...] = total_in[...]
    squares[...] = squares_in[...]
    for n, halo in enumerate((low, high)):
        ends[n, 0:rows] = halo[...]
        ends[n, rows:] = jnp.dot(pick, halo[...], preferred_element_type=F32).astype(BF16)
    triples = [
        (ends.at[0], field.at[0], field.at[1], weights.at[0]),
        (field.at[slabs - 2], field.at[slabs - 1], ends.at[1], weights.at[slabs - 1]),
    ]
    act(triples, weights, stencil, side, right, left, squares, rows, terms)
    contract(left, right, total, lines, terms)
    norms = []
    for q in range(terms):
        level = jnp.sum(squares[q], keepdims=True)
        levels[q] = jnp.broadcast_to(level, levels.shape[1:])
        norms.append(LIMIT**0.5 * lax.rsqrt(jnp.maximum(level, 1e-30)))
    offset = 0
    for k in range(terms):
        for q in range(k + 1):
            scale = norms[q] * norms[k]
            pair = q * terms - q * (q - 1) // 2 + k - q
            for z in range(planes):
                at = offset + q * lines + z * own
                part = total[at : at + own, :] * scale
                if z == 0:
                    mine[pair * own : (pair + 1) * own, :] = part
                else:
                    others[z - 1, pair * own : (pair + 1) * own, :] = part
        offset += (k + 1) * lines


def products(field, weights, count, rows, own, planes, terms):
    slabs, every, width = field.shape
    lines = every - rows
    pairs = terms * (terms + 1) // 2
    scratch = [
        pltpu.VMEM((every, 2 * width), F32),
        pltpu.VMEM((terms, rows, 2 * width), BF16),
        pltpu.VMEM((terms * lines, 2 * width), BF16),
    ]
    ahead = [(i, (i + GROUP) % count) for i in range(count)]
    behind = [(i, (i - GROUP) % count) for i in range(count)]
    low = lax.ppermute(field[slabs - 1, :rows], "mode", ahead)
    high = lax.ppermute(field[0, :rows], "mode", behind)
    total, squares = pl.pallas_call(
        functools.partial(inner_kernel, rows, terms),
        out_shape=(shape((pairs * lines, rows)), shape((terms, 8, width))),
        in_specs=[VMEM, VMEM],
        out_specs=(VMEM, VMEM),
        scratch_shapes=scratch,
        compiler_params=params(),
        cost_estimate=pl.CostEstimate(flops=20_000_000_000, bytes_accessed=5_000_000, transcendentals=0),
    )(field, weights)
    return pl.pallas_call(
        functools.partial(outer_kernel, rows, terms, own, planes),
        out_shape=(
            shape((pairs * own, rows)),
            shape((planes - 1, pairs * own, rows)),
            shape((terms, 8, width)),
        ),
        in_specs=[VMEM] * 6,
        out_specs=(VMEM, VMEM, VMEM),
        scratch_shapes=[
            pltpu.VMEM((pairs * lines, rows), F32),
            pltpu.VMEM((terms, 8, width), F32),
            pltpu.VMEM((2, every, width), BF16),
            *scratch,
        ],
        compiler_params=params(),
    )(field, weights, low, high, total, squares)


def per_device(basis, slab_region, coef_index, coef_table):
    terms = coef_index.shape[1]
    rows, cells = basis.shape
    width = cells // slab_region.shape[0]
    count = lax.axis_size("mode")
    planes = count // GROUP
    own = rows // count
    pairs = [(q, k) for q in range(terms) for k in range(q, terms)]
    first, second = payload(basis, slab_region, coef_index, coef_table)
    pieces = gather(first, second, count)
    field, weights = assemble(pieces, own, planes, width)
    mine, others, levels = products(field, weights, count, rows, own, planes, terms)
    sums = [levels[:, 0, 0]]
    parts = [mine]
    others = others.astype(jnp.float16)
    for z in range(1, planes):
        there = [(i, (i + z * GROUP) % count) for i in range(count)]
        sums.append(lax.ppermute(levels, "mode", there)[:, 0, 0])
        parts.append(lax.ppermute(others[z - 1], "mode", there).astype(F32))
    level = sum(sums) / (rows * cells * count) + 1e-06
    root = lax.rsqrt(level)
    out = 0.0
    for part, one in zip(parts, sums):
        decode = jnp.sqrt(jnp.maximum(one, 1e-30)) * root
        factor = jnp.stack([decode[q] * decode[k] for q, k in pairs]) / (LIMIT * cells * count)
        out = out + part.reshape(len(pairs), own, rows) * factor[:, None, None]
    return out


def solution(mesh):
    return jax.shard_map(
        per_device,
        mesh=mesh,
        in_specs=(P("groups", "mode"), P(("groups", "mode")), P("groups", None), P("groups")),
        out_specs=P(None, ("groups", "mode"), None),
        check_vma=False,
    )
```

time: 245 us -> 168 us (0.69)
  waiting for transfers between devices: 95.9 us -> 15.9 us
  between operations: 42.1 us -> 105 us
  blocking collectives: 38.7 us -> 0 us
  local copies, waits for them, and re-layouts: 40.8 us -> 6.57 us
  Pallas kernels: 0 us -> 18.2 us
  starting transfers between devices: 6.49 us -> 20.5 us
  matrix products: 12.6 us -> 0 us
  other arithmetic: 7.13 us -> 0.44 us
    reduce_scatter x1 -> x0, waiting for transfers between devices: 95.5 us -> none  [per_device(): lax.psum_scatter(jnp.concatenate(pieces, axis=1).reshape(rows, len(pair_l...]
    psum x1 -> x0, blocking collectives: 38.7 us -> none  [per_device(): level_sums = lax.psum(jnp.sum(values * values, axis=(1, 2)), 'mode')]
    pallas_call x0 -> x4, Pallas kernels: none -> 18.2 us  [the longest x1 14.8 us: products(): pl.pallas_call(functools.partial(inner_kernel, rows, terms), out_shape=(s...]
    reshape x2 -> x4, local copies, waits for them, and re-layouts: 15.9 us -> 0.17 us  [per_device(): out = out + part.reshape(len(pairs), own, rows) * factor[:, None, None]]
    ppermute x2 -> x22, waiting for transfers between devices: 0.42 us -> 15.9 us  [the longest x14 13.1 us: flip(): return lax.ppermute(values, 'mode', [(i, i ^ mask) for i in range(count)])]
    ppermute x2 -> x22, starting transfers between devices: 6.49 us -> 20.5 us  [the longest x14 7.91 us: flip(): return lax.ppermute(values, 'mode', [(i, i ^ mask) for i in range(count)])]
    dot_general x6 -> x0, matrix products: 12.6 us -> none  [per_device(): lax.dot_general(actions[partial_first], others, (((1,), (1,)), ((), ())),...]
    concatenate x1 -> x0, local copies, waits for them, and re-layouts: 12.6 us -> none  [per_device(): jnp.concatenate(pieces, axis=1).reshape(rows, len(pair_list), rows)]
  transfers between devices with their start and end apart: 3 -> 22, of which waited for: 2 -> 8; matrix products, arithmetic and copies ran while one was open for 2% -> 2% of each run, Pallas kernels for 0% -> 9%
where the time goes in v1:
time: 168 us; the launch traced here: 166 us
  between operations  105 us (62%)
  starting transfers between devices  20.5 us (12%)
  Pallas kernels  18.2 us (11%)
  waiting for transfers between devices  15.9 us (9%)
  local copies, waits for them, and re-layouts  6.57 us (4%)
    pallas_call x1, Pallas kernels, products(): pl.pallas_call(functools.partial(inner_kernel, rows, terms), out_shape=(s...  14.8 us
    ppermute x14, waiting for transfers between devices, flip(): return lax.ppermute(values, 'mode', [(i, i ^ mask) for i in range(count)])  13.1 us
    ppermute x14, starting transfers between devices, flip(): return lax.ppermute(values, 'mode', [(i, i ^ mask) for i in range(count)])  7.91 us
    ppermute x3, starting transfers between devices, per_device(): sums.append(lax.ppermute(levels, 'mode', there)[:, 0, 0])  4.52 us
    ppermute x3, starting transfers between devices, per_device(): parts.append(lax.ppermute(others[z - 1], 'mode', there).astype(F32))  4.43 us
    ppermute x1, starting transfers between devices, products(): high = lax.ppermute(field[0, :rows], 'mode', behind)  3.65 us
  transfers between devices with their start and end apart: 22, of which 8 were waited for; matrix products, arithmetic and copies ran while one was open for 2% of the time, Pallas kernels for 9%

profile of v1, /device:TPU:0, one launch (start us, length us, event | category | flops | bytes accessed | tf_op | source)
XLA Modules:
  0.0 166.5 jit_solution(10401365260813464629)
XLA Ops:
  0.0 0.8 copy.10.index
  0.8 0.0 copy-start
  0.8 1.0 copy-done
  1.8 0.7 copy-done.1
  2.4 0.7 copy-done.2
  3.1 0.7 shard_map.46
  3.8 3.0 %collective-permute-start.3 = (bf16[208,512]{1,0:T(8,128)(2,1)S(1)}, bf16[208,512]{1,0:T(8,128)(2,1)S(1)}, u32[]{:S(2)}, u32[]{:S(2)}) collective-permute-start(bf16[208,512]{1,0:T(8,128)(2,1)S(1)} %get-tuple-element.14.refs_0_), channel_id=1, source_target_pairs={{0,4},{1,5},{2,6},{3,7},{4,0},{5,1},{6,2},{7,3},{8,12},{9,13},{10,... | collective-permute-start | bytes 638984 | tf_op jit(solution)/shard_map/ppermute | solution.py:66
  6.9 1.5 collective-permute-start.1
  8.4 0.0 collective-permute-start
  8.4 0.5 collective-permute-start.10
  8.9 0.1 collective-permute-start.8
  9.0 3.7 %collective-permute-done.3.refs_4_ = bf16[208,512]{1,0:T(8,128)(2,1)S(1)} collective-permute-done((bf16[208,512]{1,0:T(8,128)(2,1)S(1)}, bf16[208,512]{1,0:T(8,128)(2,1)S(1)}, u32[]{:S(2)}, u32[]{:S(2)}) %collective-permute-start.3) | collective-permute-done | bytes 213024 | tf_op jit(solution)/shard_map/ppermute | solution.py:66
  12.7 0.0 collective-permute-start.7
  12.7 2.3 %collective-permute-done.1.refs_2_ = bf16[208,512]{1,0:T(8,128)(2,1)S(1)} collective-permute-done((bf16[208,512]{1,0:T(8,128)(2,1)S(1)}, bf16[208,512]{1,0:T(8,128)(2,1)S(1)}, u32[]{:S(2)}, u32[]{:S(2)}) %collective-permute-start.1) | collective-permute-done | bytes 213024 | tf_op jit(solution)/shard_map/ppermute | solution.py:66
  15.0 0.0 collective-permute-start.4
  15.1 0.0 collective-permute-done.refs_1_
  15.1 0.5 collective-permute-start.5
  15.5 1.2 collective-permute-done.10.refs_12_
  16.7 1.7 %collective-permute-start.12 = (bf16[208,512]{1,0:T(8,128)(2,1)S(1)}, bf16[208,512]{1,0:T(8,128)(2,1)S(1)}, u32[]{:S(2)}, u32[]{:S(2)}) collective-permute-start(bf16[208,512]{1,0:T(8,128)(2,1)S(1)} %collective-permute-done.10.refs_12_), channel_id=1, source_target_pairs={{0,2},{1,3},{2,0},{3,1},{4,6},{5,7},{6,4},{7,5},{8,10},{9,11},{10,... | collective-permute-start | bytes 638984 | tf_op jit(solution)/shard_map/ppermute | solution.py:66
  18.4 0.0 collective-permute-done.8.refs_10_
  18.4 0.0 collective-permute-start.2
  18.4 0.0 collective-permute-done.7.refs_9_
  18.4 0.5 collective-permute-start.11
  18.9 0.0 collective-permute-done.4.refs_5_
  18.9 0.1 collective-permute-start.9
  19.0 3.7 %collective-permute-done.5.refs_6_ = bf16[208,512]{1,0:T(8,128)(2,1)S(1)} collective-permute-done((bf16[208,512]{1,0:T(8,128)(2,1)S(1)}, bf16[208,512]{1,0:T(8,128)(2,1)S(1)}, u32[]{:S(2)}, u32[]{:S(2)}) %collective-permute-start.5) | collective-permute-done | bytes 213024 | tf_op jit(solution)/shard_map/ppermute | solution.py:66
  22.7 0.0 collective-permute-start.6
  22.7 0.6 collective-permute-done.12.refs_14_
  23.4 0.0 collective-permute-start.13
  23.4 0.0 collective-permute-done.2.refs_3_
  23.4 0.0 collective-permute-done.11.refs_13_
  23.4 0.0 collective-permute-done.9.refs_11_
  23.4 0.8 collective-permute-done.6.refs_7_
  24.2 0.6 collective-permute-done.13.refs_15_
  24.8 1.4 shard_map.47
  26.2 3.7 %collective-permute-start.15 = (bf16[384,128]{1,0:T(8,128)(2,1)S(1)}, bf16[384,128]{1,0:T(8,128)(2,1)S(1)}, u32[]{:S(2)}, u32[]{:S(2)}) collective-permute-start(bf16[384,128]{1,0:T(8,128)(2,1)S(1)} %get-tuple-element.25), channel_id=1, source_target_pairs={{0,24},{1,25},{2,26},{3,27},{4,28},{5,29},{6,30},{7,31},{8,0},{9,1... | collective-permute-start | bytes 294920 | tf_op jit(solution)/shard_map/ppermute | solution.py:267
  29.9 0.0 collective-permute-start.14
  29.9 14.8 %shard_map.48 = (f32[1008,384]{1,0:T(8,128)S(1)}, f32[6,8,128]{2,1,0:T(8,128)S(1)}) custom-call(bf16[32,432,128]{2,1,0:T(8,128)(2,1)S(1)} %get-tuple-element.16.field, bf16[32,32,128]{2,1,0:T(8,128)(2,1)S(1)} %get-tuple-element.17.weights), custom_call_target="tpu_custom_call" | custom-call | flops 20000000000 | bytes 5000000 | tf_op jit(solution)/shard_map/pallas_call | solution.py:268
  44.7 0.0 collective-permute-done.15.high
  44.8 0.0 collective-permute-done.14.low
  44.8 1.2 shard_map.49
  46.0 3.9 %collective-permute-start.18 = (f32[6,8,128]{2,1,0:T(8,128)S(1)}, f32[6,8,128]{2,1,0:T(8,128)S(1)}, u32[]{:S(2)}, u32[]{:S(2)}) collective-permute-start(f32[6,8,128]{2,1,0:T(8,128)S(1)} %get-tuple-element.21), channel_id=1, source_target_pairs={{0,24},{1,25},{2,26},{3,27},{4,28},{5,29},{6,30},{7,31},{8,0},{9,1... | collective-permute-start | bytes 73736 | tf_op jit(solution)/shard_map/ppermute | solution.py:313
  49.9 0.0 collective-permute-start.17
  49.9 0.6 collective-permute-start.16
  50.5 0.1 convert_element_type.2
  50.6 0.1 slice_bitcast_fusion.2
  50.8 2.9 %collective-permute-start.19 = (f16[252,384]{1,0:T(8,128)(2,1)S(1)}, f16[252,384]{1,0:T(8,128)(2,1)S(1)}, u32[]{:S(2)}, u32[]{:S(2)}) collective-permute-start(f16[252,384]{1,0:T(8,128)(2,1)S(1)} %get-tuple-element.27), channel_id=1, source_target_pairs={{0,8},{1,9},{2,10},{3,11},{4,12},{5,13},{6,14},{7,15},{8,16},{9,17... | collective-permute-start | bytes 580616 | tf_op jit(solution)/shard_map/ppermute | solution.py:314
  53.7 1.0 collective-permute-start.21
  54.7 0.0 collective-permute-done.18
  54.7 0.6 collective-permute-start.20
  55.2 2.8 %collective-permute-done.17 = f32[6,8,128]{2,1,0:T(8,128)S(1)} collective-permute-done((f32[6,8,128]{2,1,0:T(8,128)S(1)}, f32[6,8,128]{2,1,0:T(8,128)S(1)}, u32[]{:S(2)}, u32[]{:S(2)}) %collective-permute-start.17) | collective-permute-done | bytes 24608 | tf_op jit(solution)/shard_map/ppermute | solution.py:313
  58.0 0.0 collective-permute-done.16
  58.0 0.6 fusion
  85.1 0.6 fusion.1
  137.7 0.6 fusion.3
  164.5 0.1 stack.10
  164.7 0.1 stack.8
  164.8 0.1 stack.11
  164.9 0.1 stack.9
  165.1 0.0 collective-permute-done.19
  165.2 0.0 collective-permute-done.21
  165.3 0.0 collective-permute-done.20
  165.4 0.2 multiply_add_fusion
  165.6 0.9 copy.11
  (15 shorter events, 0.3 us)
Async XLA Ops:
  0.8 1.0 copy-start
  1.8 0.7 copy-start.1
  2.4 0.7 copy-start.2
  3.8 8.9 %collective-permute-start.3 = (bf16[208,512]{1,0:T(8,128)(2,1)S(1)}, bf16[208,512]{1,0:T(8,128)(2,1)S(1)}, u32[]{:S(2)}, u32[]{:S(2)}) collective-permute-start(bf16[208,512]{1,0:T(8,128)(2,1)S(1)} %get-tuple-element.14.refs_0_), channel_id=1, source_target_pairs={{0,4},{1,5},{2,6},{3,7},{4,0},{5,1},{6,2},{7,3},{8,12},{9,13},{10,... | collective-permute-start | bytes 638984 | tf_op jit(solution)/shard_map/ppermute | solution.py:66
  6.9 8.2 %collective-permute-start.1 = (bf16[208,512]{1,0:T(8,128)(2,1)S(1)}, bf16[208,512]{1,0:T(8,128)(2,1)S(1)}, u32[]{:S(2)}, u32[]{:S(2)}) collective-permute-start(bf16[208,512]{1,0:T(8,128)(2,1)S(1)} %get-tuple-element.14.refs_0_), channel_id=1, source_target_pairs={{0,2},{1,3},{2,0},{3,1},{4,6},{5,7},{6,4},{7,5},{8,10},{9,11},{10,... | collective-permute-start | bytes 638984 | tf_op jit(solution)/shard_map/ppermute | solution.py:66
  8.4 6.7 %collective-permute-start = (bf16[208,512]{1,0:T(8,128)(2,1)S(1)}, bf16[208,512]{1,0:T(8,128)(2,1)S(1)}, u32[]{:S(2)}, u32[]{:S(2)}) collective-permute-start(bf16[208,512]{1,0:T(8,128)(2,1)S(1)} %get-tuple-element.14.refs_0_), channel_id=1, source_target_pairs={{0,1},{1,0},{2,3},{3,2},{4,5},{5,4},{6,7},{7,6},{8,9},{9,8},{10,11... | collective-permute-start | bytes 638984 | tf_op jit(solution)/shard_map/ppermute | solution.py:66
  8.4 8.3 %collective-permute-start.10 = (bf16[208,512]{1,0:T(8,128)(2,1)S(1)}, bf16[208,512]{1,0:T(8,128)(2,1)S(1)}, u32[]{:S(2)}, u32[]{:S(2)}) collective-permute-start(bf16[208,512]{1,0:T(8,128)(2,1)S(1)} %get-tuple-element.15.refs_8_), channel_id=1, source_target_pairs={{0,4},{1,5},{2,6},{3,7},{4,0},{5,1},{6,2},{7,3},{8,12},{9,13},{10,... | collective-permute-start | bytes 638984 | tf_op jit(solution)/shard_map/ppermute | solution.py:66
  8.9 9.5 %collective-permute-start.8 = (bf16[208,512]{1,0:T(8,128)(2,1)S(1)}, bf16[208,512]{1,0:T(8,128)(2,1)S(1)}, u32[]{:S(2)}, u32[]{:S(2)}) collective-permute-start(bf16[208,512]{1,0:T(8,128)(2,1)S(1)} %get-tuple-element.15.refs_8_), channel_id=1, source_target_pairs={{0,2},{1,3},{2,0},{3,1},{4,6},{5,7},{6,4},{7,5},{8,10},{9,11},{10,... | collective-permute-start | bytes 638984 | tf_op jit(solution)/shard_map/ppermute | solution.py:66
  12.7 5.7 %collective-permute-start.7 = (bf16[208,512]{1,0:T(8,128)(2,1)S(1)}, bf16[208,512]{1,0:T(8,128)(2,1)S(1)}, u32[]{:S(2)}, u32[]{:S(2)}) collective-permute-start(bf16[208,512]{1,0:T(8,128)(2,1)S(1)} %get-tuple-element.15.refs_8_), channel_id=1, source_target_pairs={{0,1},{1,0},{2,3},{3,2},{4,5},{5,4},{6,7},{7,6},{8,9},{9,8},{10,11... | collective-permute-start | bytes 638984 | tf_op jit(solution)/shard_map/ppermute | solution.py:66
  15.0 3.9 %collective-permute-start.4 = (bf16[208,512]{1,0:T(8,128)(2,1)S(1)}, bf16[208,512]{1,0:T(8,128)(2,1)S(1)}, u32[]{:S(2)}, u32[]{:S(2)}) collective-permute-start(bf16[208,512]{1,0:T(8,128)(2,1)S(1)} %collective-permute-done.3.refs_4_), channel_id=1, source_target_pairs={{0,1},{1,0},{2,3},{3,2},{4,5},{5,4},{6,7},{7,6},{8,9},{9,8},{10,11... | collective-permute-start | bytes 638984 | tf_op jit(solution)/shard_map/ppermute | solution.py:66
  15.1 7.7 %collective-permute-start.5 = (bf16[208,512]{1,0:T(8,128)(2,1)S(1)}, bf16[208,512]{1,0:T(8,128)(2,1)S(1)}, u32[]{:S(2)}, u32[]{:S(2)}) collective-permute-start(bf16[208,512]{1,0:T(8,128)(2,1)S(1)} %collective-permute-done.1.refs_2_), channel_id=1, source_target_pairs={{0,4},{1,5},{2,6},{3,7},{4,0},{5,1},{6,2},{7,3},{8,12},{9,13},{10,... | collective-permute-start | bytes 638984 | tf_op jit(solution)/shard_map/ppermute | solution.py:66
  16.7 6.7 %collective-permute-start.12 = (bf16[208,512]{1,0:T(8,128)(2,1)S(1)}, bf16[208,512]{1,0:T(8,128)(2,1)S(1)}, u32[]{:S(2)}, u32[]{:S(2)}) collective-permute-start(bf16[208,512]{1,0:T(8,128)(2,1)S(1)} %collective-permute-done.10.refs_12_), channel_id=1, source_target_pairs={{0,2},{1,3},{2,0},{3,1},{4,6},{5,7},{6,4},{7,5},{8,10},{9,11},{10,... | collective-permute-start | bytes 638984 | tf_op jit(solution)/shard_map/ppermute | solution.py:66
  18.4 5.0 %collective-permute-start.2 = (bf16[208,512]{1,0:T(8,128)(2,1)S(1)}, bf16[208,512]{1,0:T(8,128)(2,1)S(1)}, u32[]{:S(2)}, u32[]{:S(2)}) collective-permute-start(bf16[208,512]{1,0:T(8,128)(2,1)S(1)} %collective-permute-done.1.refs_2_), channel_id=1, source_target_pairs={{0,1},{1,0},{2,3},{3,2},{4,5},{5,4},{6,7},{7,6},{8,9},{9,8},{10,11... | collective-permute-start | bytes 638984 | tf_op jit(solution)/shard_map/ppermute | solution.py:66
  18.4 5.0 %collective-permute-start.11 = (bf16[208,512]{1,0:T(8,128)(2,1)S(1)}, bf16[208,512]{1,0:T(8,128)(2,1)S(1)}, u32[]{:S(2)}, u32[]{:S(2)}) collective-permute-start(bf16[208,512]{1,0:T(8,128)(2,1)S(1)} %collective-permute-done.10.refs_12_), channel_id=1, source_target_pairs={{0,1},{1,0},{2,3},{3,2},{4,5},{5,4},{6,7},{7,6},{8,9},{9,8},{10,11... | collective-permute-start | bytes 638984 | tf_op jit(solution)/shard_map/ppermute | solution.py:66
  18.9 4.5 %collective-permute-start.9 = (bf16[208,512]{1,0:T(8,128)(2,1)S(1)}, bf16[208,512]{1,0:T(8,128)(2,1)S(1)}, u32[]{:S(2)}, u32[]{:S(2)}) collective-permute-start(bf16[208,512]{1,0:T(8,128)(2,1)S(1)} %collective-permute-done.8.refs_10_), channel_id=1, source_target_pairs={{0,1},{1,0},{2,3},{3,2},{4,5},{5,4},{6,7},{7,6},{8,9},{9,8},{10,11... | collective-permute-start | bytes 638984 | tf_op jit(solution)/shard_map/ppermute | solution.py:66
  22.7 1.5 collective-permute-start.6
  23.4 1.5 collective-permute-start.13
  26.2 18.5 %collective-permute-start.15 = (bf16[384,128]{1,0:T(8,128)(2,1)S(1)}, bf16[384,128]{1,0:T(8,128)(2,1)S(1)}, u32[]{:S(2)}, u32[]{:S(2)}) collective-permute-start(bf16[384,128]{1,0:T(8,128)(2,1)S(1)} %get-tuple-element.25), channel_id=1, source_target_pairs={{0,24},{1,25},{2,26},{3,27},{4,28},{5,29},{6,30},{7,31},{8,0},{9,1... | collective-permute-start | bytes 294920 | tf_op jit(solution)/shard_map/ppermute | solution.py:267
  29.9 14.9 %collective-permute-start.14 = (bf16[384,128]{1,0:T(8,128)(2,1)S(1)}, bf16[384,128]{1,0:T(8,128)(2,1)S(1)}, u32[]{:S(2)}, u32[]{:S(2)}) collective-permute-start(bf16[384,128]{1,0:T(8,128)(2,1)S(1)} %get-tuple-element.26), channel_id=1, source_target_pairs={{0,8},{1,9},{2,10},{3,11},{4,12},{5,13},{6,14},{7,15},{8,16},{9,17... | collective-permute-start | bytes 294920 | tf_op jit(solution)/shard_map/ppermute | solution.py:266
  46.0 8.7 %collective-permute-start.18 = (f32[6,8,128]{2,1,0:T(8,128)S(1)}, f32[6,8,128]{2,1,0:T(8,128)S(1)}, u32[]{:S(2)}, u32[]{:S(2)}) collective-permute-start(f32[6,8,128]{2,1,0:T(8,128)S(1)} %get-tuple-element.21), channel_id=1, source_target_pairs={{0,24},{1,25},{2,26},{3,27},{4,28},{5,29},{6,30},{7,31},{8,0},{9,1... | collective-permute-start | bytes 73736 | tf_op jit(solution)/shard_map/ppermute | solution.py:313
  49.9 8.1 %collective-permute-start.17 = (f32[6,8,128]{2,1,0:T(8,128)S(1)}, f32[6,8,128]{2,1,0:T(8,128)S(1)}, u32[]{:S(2)}, u32[]{:S(2)}) collective-permute-start(f32[6,8,128]{2,1,0:T(8,128)S(1)} %get-tuple-element.21), channel_id=1, source_target_pairs={{0,16},{1,17},{2,18},{3,19},{4,20},{5,21},{6,22},{7,23},{8,24},{9,... | collective-permute-start | bytes 73736 | tf_op jit(solution)/shard_map/ppermute | solution.py:313
  49.9 8.1 %collective-permute-start.16 = (f32[6,8,128]{2,1,0:T(8,128)S(1)}, f32[6,8,128]{2,1,0:T(8,128)S(1)}, u32[]{:S(2)}, u32[]{:S(2)}) collective-permute-start(f32[6,8,128]{2,1,0:T(8,128)S(1)} %get-tuple-element.21), channel_id=1, source_target_pairs={{0,8},{1,9},{2,10},{3,11},{4,12},{5,13},{6,14},{7,15},{8,16},{9,17... | collective-permute-start | bytes 73736 | tf_op jit(solution)/shard_map/ppermute | solution.py:313
  50.8 114.3 %collective-permute-start.19 = (f16[252,384]{1,0:T(8,128)(2,1)S(1)}, f16[252,384]{1,0:T(8,128)(2,1)S(1)}, u32[]{:S(2)}, u32[]{:S(2)}) collective-permute-start(f16[252,384]{1,0:T(8,128)(2,1)S(1)} %get-tuple-element.27), channel_id=1, source_target_pairs={{0,8},{1,9},{2,10},{3,11},{4,12},{5,13},{6,14},{7,15},{8,16},{9,17... | collective-permute-start | bytes 580616 | tf_op jit(solution)/shard_map/ppermute | solution.py:314
  53.7 111.5 %collective-permute-start.21 = (f16[252,384]{1,0:T(8,128)(2,1)S(1)}, f16[252,384]{1,0:T(8,128)(2,1)S(1)}, u32[]{:S(2)}, u32[]{:S(2)}) collective-permute-start(f16[252,384]{1,0:T(8,128)(2,1)S(1)} %get-tuple-element.28), channel_id=1, source_target_pairs={{0,24},{1,25},{2,26},{3,27},{4,28},{5,29},{6,30},{7,31},{8,0},{9,1... | collective-permute-start | bytes 580616 | tf_op jit(solution)/shard_map/ppermute | solution.py:314
  54.7 110.6 %collective-permute-start.20 = (f16[252,384]{1,0:T(8,128)(2,1)S(1)}, f16[252,384]{1,0:T(8,128)(2,1)S(1)}, u32[]{:S(2)}, u32[]{:S(2)}) collective-permute-start(f16[252,384]{1,0:T(8,128)(2,1)S(1)} %get-tuple-element.29), channel_id=1, source_target_pairs={{0,16},{1,17},{2,18},{3,19},{4,20},{5,21},{6,22},{7,23},{8,24},{9,... | collective-permute-start | bytes 580616 | tf_op jit(solution)/shard_map/ppermute | solution.py:314

commit v2 on v1

--- a/solution.py
+++ b/solution.py
@@ -293,6 +293,26 @@
     )(field, weights, low, high, total, squares)
 
 
+def finish_kernel(own, terms, cells, *refs):
+    planes = (len(refs) - 1) // 2
+    parts, levels, out = refs[:planes], refs[planes : 2 * planes], refs[-1]
+    rows = parts[0].shape[1]
+    decodes = []
+    for q in range(terms):
+        sums = [level[q, 0:1, 0:1] for level in levels]
+        root = lax.rsqrt(sum(sums) / (rows * cells) + 1e-06) * (LIMIT * cells) ** -0.5
+        decodes.append([jnp.sqrt(jnp.maximum(one, 1e-30)) * root for one in sums])
+    pair = 0
+    for q in range(terms):
+        for k in range(q, terms):
+            here = slice(pair * own, (pair + 1) * own)
+            total = 0.0
+            for z in range(planes):
+                total = total + parts[z][here, :] * (decodes[q][z] * decodes[k][z])
+            out[:, pair, :] = total
+            pair += 1
+
+
 def per_device(basis, slab_region, coef_index, coef_table):
     terms = coef_index.shape[1]
     rows, cells = basis.shape
@@ -300,26 +320,25 @@
     count = lax.axis_size("mode")
     planes = count // GROUP
     own = rows // count
-    pairs = [(q, k) for q in range(terms) for k in range(q, terms)]
     first, second = payload(basis, slab_region, coef_index, coef_table)
     pieces = gather(first, second, count)
     field, weights = assemble(pieces, own, planes, width)
     mine, others, levels = products(field, weights, count, rows, own, planes, terms)
-    sums = [levels[:, 0, 0]]
+    sums = [levels]
     parts = [mine]
     others = others.astype(jnp.float16)
     for z in range(1, planes):
         there = [(i, (i + z * GROUP) % count) for i in range(count)]
-        sums.append(lax.ppermute(levels, "mode", there)[:, 0, 0])
+        sums.append(lax.ppermute(levels, "mode", there))
         parts.append(lax.ppermute(others[z - 1], "mode", there).astype(F32))
-    level = sum(sums) / (rows * cells * count) + 1e-06
-    root = lax.rsqrt(level)
-    out = 0.0
-    for part, one in zip(parts, sums):
-        decode = jnp.sqrt(jnp.maximum(one, 1e-30)) * root
-        factor = jnp.stack([decode[q] * decode[k] for q, k in pairs]) / (LIMIT * cells * count)
-        out = out + part.reshape(len(pairs), own, rows) * factor[:, None, None]
-    return out
+    out = pl.pallas_call(
+        functools.partial(finish_kernel, own, terms, cells * count),
+        out_shape=shape((own, terms * (terms + 1) // 2, rows)),
+        in_specs=[VMEM] * (2 * planes),
+        out_specs=VMEM,
+        compiler_params=params(),
+    )(*parts, *sums)
+    return jnp.transpose(out, (1, 0, 2))
 
 
 def solution(mesh):

time: 168 us -> 68.9 us (0.41)
  between operations: 105 us -> 0.14 us
  waiting for transfers between devices: 15.9 us -> 25.5 us
  local copies, waits for them, and re-layouts: 6.57 us -> 3.21 us
    ppermute x3, waiting for transfers between devices: 0.01 us -> 12 us  [per_device(): parts.append(lax.ppermute(others[z - 1], 'mode', there).astype(F32))]
    ppermute x3, waiting for transfers between devices: 2.8 us -> 0.44 us  [per_device(): sums.append(lax.ppermute(levels, 'mode', there))]
    slice x3 -> x0, local copies, waits for them, and re-layouts: 1.84 us -> none  [per_device(): decode[k]]
  transfers between devices with their start and end apart: 22 -> 22, of which waited for: 8 -> 10; matrix products, arithmetic and copies ran while one was open for 2% -> 0% of each run, Pallas kernels for 9% -> 22%
where the time goes in v2:
time: 68.9 us; the launch traced here: 68.7 us
  waiting for transfers between devices  25.5 us (37%)
  starting transfers between devices  20.4 us (30%)
  Pallas kernels  19.3 us (28%)
  local copies, waits for them, and re-layouts  3.21 us (5%)
    pallas_call x1, Pallas kernels, products(): pl.pallas_call(functools.partial(inner_kernel, rows, terms), out_shape=(s...  14.8 us
    ppermute x14, waiting for transfers between devices, flip(): return lax.ppermute(values, 'mode', [(i, i ^ mask) for i in range(count)])  13.1 us
    ppermute x3, waiting for transfers between devices, per_device(): parts.append(lax.ppermute(others[z - 1], 'mode', there).astype(F32))  12 us
    ppermute x14, starting transfers between devices, flip(): return lax.ppermute(values, 'mode', [(i, i ^ mask) for i in range(count)])  7.91 us
    ppermute x3, starting transfers between devices, per_device(): parts.append(lax.ppermute(others[z - 1], 'mode', there).astype(F32))  4.52 us
    ppermute x3, starting transfers between devices, per_device(): sums.append(lax.ppermute(levels, 'mode', there))  4.31 us
    ppermute x1, starting transfers between devices, products(): high = lax.ppermute(field[0, :rows], 'mode', behind)  3.65 us
    unnamed x7, local copies, waits for them, and re-layouts  3.08 us
  transfers between devices with their start and end apart: 22, of which 10 were waited for; matrix products, arithmetic and copies ran while one was open for 0% of the time, Pallas kernels for 22%

profile of v2, /device:TPU:0, one launch (start us, length us, event | category | flops | bytes accessed | tf_op | source)
XLA Modules:
  0.0 68.7 jit_solution(15465958869809820843)
XLA Ops:
  0.0 0.8 %copy.5.index = s32[9,6]{1,0:T(8,128)S(1)} copy(s32[9,6]{0,1:T(8,128)} %param.6) | data formatting | bytes 432 | tf_op args[2]
  0.8 0.0 copy-start
  0.8 1.0 %copy-done = bf16[384,512]{1,0:T(8,128)(2,1)S(1)} copy-done((bf16[384,512]{1,0:T(8,128)(2,1)S(1)}, bf16[384,512]{1,0:T(8,128)(2,1)}, u32[]{:S(2)}) %copy-start) | copy-done | bytes 393240
  1.8 0.0 copy-start.1
  1.8 0.7 copy-done.1
  2.4 0.0 copy-start.2
  2.4 0.7 copy-done.2
  3.1 0.7 %shard_map.46 = (bf16[208,512]{1,0:T(8,128)(2,1)S(1)}, bf16[208,512]{1,0:T(8,128)(2,1)S(1)}) custom-call(bf16[384,512]{1,0:T(8,128)(2,1)S(1)} %copy-done, s32[4]{0:T(128)S(1)} %copy-done.1, s32[9,6]{1,0:T(8,128)S(1)} %copy.5.index, f32[8]{0:T(128)S(1)} %copy-done.2), custom_call_target="tpu_custom_call" | custom-call | tf_op jit(solution)/shard_map/pallas_call | solution.py:56
  3.8 3.0 %collective-permute-start.3 = (bf16[208,512]{1,0:T(8,128)(2,1)S(1)}, bf16[208,512]{1,0:T(8,128)(2,1)S(1)}, u32[]{:S(2)}, u32[]{:S(2)}) collective-permute-start(bf16[208,512]{1,0:T(8,128)(2,1)S(1)} %get-tuple-element.14.refs_0_), channel_id=1, source_target_pairs={{0,4},{1,5},{2,6},{3,7},{4,0},{5,1},{6,2},{7,3},{8,12},{9,13},{10,... | collective-permute-start | bytes 638984 | tf_op jit(solution)/shard_map/ppermute | solution.py:66
  6.9 1.5 %collective-permute-start.1 = (bf16[208,512]{1,0:T(8,128)(2,1)S(1)}, bf16[208,512]{1,0:T(8,128)(2,1)S(1)}, u32[]{:S(2)}, u32[]{:S(2)}) collective-permute-start(bf16[208,512]{1,0:T(8,128)(2,1)S(1)} %get-tuple-element.14.refs_0_), channel_id=1, source_target_pairs={{0,2},{1,3},{2,0},{3,1},{4,6},{5,7},{6,4},{7,5},{8,10},{9,11},{10,... | collective-permute-start | bytes 638984 | tf_op jit(solution)/shard_map/ppermute | solution.py:66
  8.4 0.0 collective-permute-start
  8.4 0.5 collective-permute-start.10
  8.9 0.1 collective-permute-start.8
  9.0 3.7 %collective-permute-done.3.refs_4_ = bf16[208,512]{1,0:T(8,128)(2,1)S(1)} collective-permute-done((bf16[208,512]{1,0:T(8,128)(2,1)S(1)}, bf16[208,512]{1,0:T(8,128)(2,1)S(1)}, u32[]{:S(2)}, u32[]{:S(2)}) %collective-permute-start.3) | collective-permute-done | bytes 213024 | tf_op jit(solution)/shard_map/ppermute | solution.py:66
  12.7 0.0 collective-permute-start.7
  12.7 2.3 %collective-permute-done.1.refs_2_ = bf16[208,512]{1,0:T(8,128)(2,1)S(1)} collective-permute-done((bf16[208,512]{1,0:T(8,128)(2,1)S(1)}, bf16[208,512]{1,0:T(8,128)(2,1)S(1)}, u32[]{:S(2)}, u32[]{:S(2)}) %collective-permute-start.1) | collective-permute-done | bytes 213024 | tf_op jit(solution)/shard_map/ppermute | solution.py:66
  15.0 0.0 collective-permute-start.4
  15.1 0.0 collective-permute-done.refs_1_
  15.1 0.5 collective-permute-start.5
  15.5 1.2 %collective-permute-done.10.refs_12_ = bf16[208,512]{1,0:T(8,128)(2,1)S(1)} collective-permute-done((bf16[208,512]{1,0:T(8,128)(2,1)S(1)}, bf16[208,512]{1,0:T(8,128)(2,1)S(1)}, u32[]{:S(2)}, u32[]{:S(2)}) %collective-permute-start.10) | collective-permute-done | bytes 213024 | tf_op jit(solution)/shard_map/ppermute | solution.py:66
  16.7 1.7 %collective-permute-start.12 = (bf16[208,512]{1,0:T(8,128)(2,1)S(1)}, bf16[208,512]{1,0:T(8,128)(2,1)S(1)}, u32[]{:S(2)}, u32[]{:S(2)}) collective-permute-start(bf16[208,512]{1,0:T(8,128)(2,1)S(1)} %collective-permute-done.10.refs_12_), channel_id=1, source_target_pairs={{0,2},{1,3},{2,0},{3,1},{4,6},{5,7},{6,4},{7,5},{8,10},{9,11},{10,... | collective-permute-start | bytes 638984 | tf_op jit(solution)/shard_map/ppermute | solution.py:66
  18.4 0.0 collective-permute-done.8.refs_10_
  18.4 0.0 collective-permute-start.2
  18.4 0.0 collective-permute-done.7.refs_9_
  18.4 0.5 collective-permute-start.11
  18.9 0.0 collective-permute-done.4.refs_5_
  18.9 0.1 collective-permute-start.9
  19.0 3.7 %collective-permute-done.5.refs_6_ = bf16[208,512]{1,0:T(8,128)(2,1)S(1)} collective-permute-done((bf16[208,512]{1,0:T(8,128)(2,1)S(1)}, bf16[208,512]{1,0:T(8,128)(2,1)S(1)}, u32[]{:S(2)}, u32[]{:S(2)}) %collective-permute-start.5) | collective-permute-done | bytes 213024 | tf_op jit(solution)/shard_map/ppermute | solution.py:66
  22.7 0.0 collective-permute-start.6
  22.7 0.6 collective-permute-done.12.refs_14_
  23.4 0.0 collective-permute-start.13
  23.4 0.0 collective-permute-done.2.refs_3_
  23.4 0.0 collective-permute-done.11.refs_13_
  23.4 0.0 collective-permute-done.9.refs_11_
  23.4 0.8 %collective-permute-done.6.refs_7_ = bf16[208,512]{1,0:T(8,128)(2,1)S(1)} collective-permute-done((bf16[208,512]{1,0:T(8,128)(2,1)S(1)}, bf16[208,512]{1,0:T(8,128)(2,1)S(1)}, u32[]{:S(2)}, u32[]{:S(2)}) %collective-permute-start.6) | collective-permute-done | bytes 213024 | tf_op jit(solution)/shard_map/ppermute | solution.py:66
  24.2 0.6 collective-permute-done.13.refs_15_
  24.8 1.4 %shard_map.47 = (bf16[32,432,128]{2,1,0:T(8,128)(2,1)S(1)}, bf16[32,32,128]{2,1,0:T(8,128)(2,1)S(1)}) custom-call(bf16[208,512]{1,0:T(8,128)(2,1)S(1)} %get-tuple-element.14.refs_0_, bf16[208,512]{1,0:T(8,128)(2,1)S(1)} %collective-permute-done.refs_1_, bf16[208,512]{1,0:T(8,128)(2,1)S(1)} %collective-permute-done.1.refs_2_, ...), custom_call_target="tpu_custom_call" | custom-call | tf_op jit(solution)/shard_map/pallas_call | solution.py:124
  26.2 3.7 %collective-permute-start.15 = (bf16[384,128]{1,0:T(8,128)(2,1)S(1)}, bf16[384,128]{1,0:T(8,128)(2,1)S(1)}, u32[]{:S(2)}, u32[]{:S(2)}) collective-permute-start(bf16[384,128]{1,0:T(8,128)(2,1)S(1)} %get-tuple-element.23), channel_id=1, source_target_pairs={{0,24},{1,25},{2,26},{3,27},{4,28},{5,29},{6,30},{7,31},{8,0},{9,1... | collective-permute-start | bytes 294920 | tf_op jit(solution)/shard_map/ppermute | solution.py:267
  29.9 0.0 collective-permute-start.14
  29.9 14.8 %shard_map.48 = (f32[1008,384]{1,0:T(8,128)S(1)}, f32[6,8,128]{2,1,0:T(8,128)S(1)}) custom-call(bf16[32,432,128]{2,1,0:T(8,128)(2,1)S(1)} %get-tuple-element.16.field, bf16[32,32,128]{2,1,0:T(8,128)(2,1)S(1)} %get-tuple-element.17.weights), custom_call_target="tpu_custom_call" | custom-call | flops 20000000000 | bytes 5000000 | tf_op jit(solution)/shard_map/pallas_call | solution.py:268
  44.7 0.0 collective-permute-done.15.high
  44.8 0.0 collective-permute-done.14.low
  44.8 1.2 %shard_map.49 = (f32[252,384]{1,0:T(8,128)S(1)}, f32[3,252,384]{2,1,0:T(8,128)S(1)}, f32[6,8,128]{2,1,0:T(8,128)S(1)}) custom-call(bf16[32,432,128]{2,1,0:T(8,128)(2,1)S(1)} %get-tuple-element.16.field, bf16[32,32,128]{2,1,0:T(8,128)(2,1)S(1)} %get-tuple-element.17.weights, bf16[384,128]{1,0:T(8,128)(2,1)S(1)} %collective-permute-done.14.low, ...), custom_call_target="tpu_custom_call" | custom-call | tf_op jit(solution)/shard_map/pallas_call | solution.py:277
  46.0 0.1 convert_element_type.12
  46.1 0.1 slice_bitcast_fusion
  46.2 3.9 %collective-permute-start.18 = (f16[252,384]{1,0:T(8,128)(2,1)S(1)}, f16[252,384]{1,0:T(8,128)(2,1)S(1)}, u32[]{:S(2)}, u32[]{:S(2)}) collective-permute-start(f16[252,384]{1,0:T(8,128)(2,1)S(1)} %get-tuple-element.25), channel_id=1, source_target_pairs={{0,24},{1,25},{2,26},{3,27},{4,28},{5,29},{6,30},{7,31},{8,0},{9,1... | collective-permute-start | bytes 580616 | tf_op jit(solution)/shard_map/ppermute | solution.py:333
  50.1 0.0 collective-permute-start.17
  50.1 0.6 collective-permute-start.16
  50.7 3.2 %collective-permute-start.21 = (f32[6,8,128]{2,1,0:T(8,128)S(1)}, f32[6,8,128]{2,1,0:T(8,128)S(1)}, u32[]{:S(2)}, u32[]{:S(2)}) collective-permute-start(f32[6,8,128]{2,1,0:T(8,128)S(1)} %get-tuple-element.22.refs_4_), channel_id=1, source_target_pairs={{0,24},{1,25},{2,26},{3,27},{4,28},{5,29},{6,30},{7,31},{8,0},{9,1... | collective-permute-start | bytes 73736 | tf_op jit(solution)/shard_map/ppermute | solution.py:332
  53.9 1.1 %collective-permute-start.20 = (f32[6,8,128]{2,1,0:T(8,128)S(1)}, f32[6,8,128]{2,1,0:T(8,128)S(1)}, u32[]{:S(2)}, u32[]{:S(2)}) collective-permute-start(f32[6,8,128]{2,1,0:T(8,128)S(1)} %get-tuple-element.22.refs_4_), channel_id=1, source_target_pairs={{0,16},{1,17},{2,18},{3,19},{4,20},{5,21},{6,22},{7,23},{8,24},{9,... | collective-permute-start | bytes 73736 | tf_op jit(solution)/shard_map/ppermute | solution.py:332
  55.0 0.4 collective-permute-done.18
  55.5 0.0 collective-permute-start.19
  55.5 11.6 %collective-permute-done.17 = f16[252,384]{1,0:T(8,128)(2,1)S(1)} collective-permute-done((f16[252,384]{1,0:T(8,128)(2,1)S(1)}, f16[252,384]{1,0:T(8,128)(2,1)S(1)}, u32[]{:S(2)}, u32[]{:S(2)}) %collective-permute-start.17) | collective-permute-done | bytes 193568 | tf_op jit(solution)/shard_map/ppermute | solution.py:333
  67.1 0.0 collective-permute-done.16
  67.2 0.0 collective-permute-done.21.refs_7_
  67.2 0.4 collective-permute-done.20.refs_6_
  67.6 0.0 collective-permute-done.19.refs_5_
  67.6 1.1 %shard_map.50 = f32[12,21,384]{2,1,0:T(8,128)} custom-call(f32[252,384]{1,0:T(8,128)S(1)} %get-tuple-element.20.refs_0_, f32[252,384]{1,0:T(8,128)S(1)} %convert_element_type.13.refs_1_, f32[252,384]{1,0:T(8,128)S(1)} %convert_element_type.14.refs_2_, f32[252,384]{1,0:T(8,128)S(1)} %convert_element_type.15.refs_3_, ...), custom_call_target="tpu_custom_call" | custom-call | tf_op jit(solution)/shard_map/pallas_call | solution.py:334
  (4 shorter events, 0.1 us)
Async XLA Ops:
  0.8 1.0 %copy-start = (bf16[384,512]{1,0:T(8,128)(2,1)S(1)}, bf16[384,512]{1,0:T(8,128)(2,1)}, u32[]{:S(2)}) copy-start(bf16[384,512]{1,0:T(8,128)(2,1)} %basis.1) | copy-start | bytes 1179652
  1.8 0.7 copy-start.1
  2.4 0.7 copy-start.2
  3.8 8.9 %collective-permute-start.3 = (bf16[208,512]{1,0:T(8,128)(2,1)S(1)}, bf16[208,512]{1,0:T(8,128)(2,1)S(1)}, u32[]{:S(2)}, u32[]{:S(2)}) collective-permute-start(bf16[208,512]{1,0:T(8,128)(2,1)S(1)} %get-tuple-element.14.refs_0_), channel_id=1, source_target_pairs={{0,4},{1,5},{2,6},{3,7},{4,0},{5,1},{6,2},{7,3},{8,12},{9,13},{10,... | collective-permute-start | bytes 638984 | tf_op jit(solution)/shard_map/ppermute | solution.py:66
  6.9 8.2 %collective-permute-start.1 = (bf16[208,512]{1,0:T(8,128)(2,1)S(1)}, bf16[208,512]{1,0:T(8,128)(2,1)S(1)}, u32[]{:S(2)}, u32[]{:S(2)}) collective-permute-start(bf16[208,512]{1,0:T(8,128)(2,1)S(1)} %get-tuple-element.14.refs_0_), channel_id=1, source_target_pairs={{0,2},{1,3},{2,0},{3,1},{4,6},{5,7},{6,4},{7,5},{8,10},{9,11},{10,... | collective-permute-start | bytes 638984 | tf_op jit(solution)/shard_map/ppermute | solution.py:66
  8.4 6.7 %collective-permute-start = (bf16[208,512]{1,0:T(8,128)(2,1)S(1)}, bf16[208,512]{1,0:T(8,128)(2,1)S(1)}, u32[]{:S(2)}, u32[]{:S(2)}) collective-permute-start(bf16[208,512]{1,0:T(8,128)(2,1)S(1)} %get-tuple-element.14.refs_0_), channel_id=1, source_target_pairs={{0,1},{1,0},{2,3},{3,2},{4,5},{5,4},{6,7},{7,6},{8,9},{9,8},{10,11... | collective-permute-start | bytes 638984 | tf_op jit(solution)/shard_map/ppermute | solution.py:66
  8.4 8.3 %collective-permute-start.10 = (bf16[208,512]{1,0:T(8,128)(2,1)S(1)}, bf16[208,512]{1,0:T(8,128)(2,1)S(1)}, u32[]{:S(2)}, u32[]{:S(2)}) collective-permute-start(bf16[208,512]{1,0:T(8,128)(2,1)S(1)} %get-tuple-element.15.refs_8_), channel_id=1, source_target_pairs={{0,4},{1,5},{2,6},{3,7},{4,0},{5,1},{6,2},{7,3},{8,12},{9,13},{10,... | collective-permute-start | bytes 638984 | tf_op jit(solution)/shard_map/ppermute | solution.py:66
  8.9 9.5 %collective-permute-start.8 = (bf16[208,512]{1,0:T(8,128)(2,1)S(1)}, bf16[208,512]{1,0:T(8,128)(2,1)S(1)}, u32[]{:S(2)}, u32[]{:S(2)}) collective-permute-start(bf16[208,512]{1,0:T(8,128)(2,1)S(1)} %get-tuple-element.15.refs_8_), channel_id=1, source_target_pairs={{0,2},{1,3},{2,0},{3,1},{4,6},{5,7},{6,4},{7,5},{8,10},{9,11},{10,... | collective-permute-start | bytes 638984 | tf_op jit(solution)/shard_map/ppermute | solution.py:66
  12.7 5.7 %collective-permute-start.7 = (bf16[208,512]{1,0:T(8,128)(2,1)S(1)}, bf16[208,512]{1,0:T(8,128)(2,1)S(1)}, u32[]{:S(2)}, u32[]{:S(2)}) collective-permute-start(bf16[208,512]{1,0:T(8,128)(2,1)S(1)} %get-tuple-element.15.refs_8_), channel_id=1, source_target_pairs={{0,1},{1,0},{2,3},{3,2},{4,5},{5,4},{6,7},{7,6},{8,9},{9,8},{10,11... | collective-permute-start | bytes 638984 | tf_op jit(solution)/shard_map/ppermute | solution.py:66
  15.0 3.9 %collective-permute-start.4 = (bf16[208,512]{1,0:T(8,128)(2,1)S(1)}, bf16[208,512]{1,0:T(8,128)(2,1)S(1)}, u32[]{:S(2)}, u32[]{:S(2)}) collective-permute-start(bf16[208,512]{1,0:T(8,128)(2,1)S(1)} %collective-permute-done.3.refs_4_), channel_id=1, source_target_pairs={{0,1},{1,0},{2,3},{3,2},{4,5},{5,4},{6,7},{7,6},{8,9},{9,8},{10,11... | collective-permute-start | bytes 638984 | tf_op jit(solution)/shard_map/ppermute | solution.py:66
  15.1 7.7 %collective-permute-start.5 = (bf16[208,512]{1,0:T(8,128)(2,1)S(1)}, bf16[208,512]{1,0:T(8,128)(2,1)S(1)}, u32[]{:S(2)}, u32[]{:S(2)}) collective-permute-start(bf16[208,512]{1,0:T(8,128)(2,1)S(1)} %collective-permute-done.1.refs_2_), channel_id=1, source_target_pairs={{0,4},{1,5},{2,6},{3,7},{4,0},{5,1},{6,2},{7,3},{8,12},{9,13},{10,... | collective-permute-start | bytes 638984 | tf_op jit(solution)/shard_map/ppermute | solution.py:66
  16.7 6.7 %collective-permute-start.12 = (bf16[208,512]{1,0:T(8,128)(2,1)S(1)}, bf16[208,512]{1,0:T(8,128)(2,1)S(1)}, u32[]{:S(2)}, u32[]{:S(2)}) collective-permute-start(bf16[208,512]{1,0:T(8,128)(2,1)S(1)} %collective-permute-done.10.refs_12_), channel_id=1, source_target_pairs={{0,2},{1,3},{2,0},{3,1},{4,6},{5,7},{6,4},{7,5},{8,10},{9,11},{10,... | collective-permute-start | bytes 638984 | tf_op jit(solution)/shard_map/ppermute | solution.py:66
  18.4 5.0 %collective-permute-start.2 = (bf16[208,512]{1,0:T(8,128)(2,1)S(1)}, bf16[208,512]{1,0:T(8,128)(2,1)S(1)}, u32[]{:S(2)}, u32[]{:S(2)}) collective-permute-start(bf16[208,512]{1,0:T(8,128)(2,1)S(1)} %collective-permute-done.1.refs_2_), channel_id=1, source_target_pairs={{0,1},{1,0},{2,3},{3,2},{4,5},{5,4},{6,7},{7,6},{8,9},{9,8},{10,11... | collective-permute-start | bytes 638984 | tf_op jit(solution)/shard_map/ppermute | solution.py:66
  18.4 5.0 %collective-permute-start.11 = (bf16[208,512]{1,0:T(8,128)(2,1)S(1)}, bf16[208,512]{1,0:T(8,128)(2,1)S(1)}, u32[]{:S(2)}, u32[]{:S(2)}) collective-permute-start(bf16[208,512]{1,0:T(8,128)(2,1)S(1)} %collective-permute-done.10.refs_12_), channel_id=1, source_target_pairs={{0,1},{1,0},{2,3},{3,2},{4,5},{5,4},{6,7},{7,6},{8,9},{9,8},{10,11... | collective-permute-start | bytes 638984 | tf_op jit(solution)/shard_map/ppermute | solution.py:66
  18.9 4.5 %collective-permute-start.9 = (bf16[208,512]{1,0:T(8,128)(2,1)S(1)}, bf16[208,512]{1,0:T(8,128)(2,1)S(1)}, u32[]{:S(2)}, u32[]{:S(2)}) collective-permute-start(bf16[208,512]{1,0:T(8,128)(2,1)S(1)} %collective-permute-done.8.refs_10_), channel_id=1, source_target_pairs={{0,1},{1,0},{2,3},{3,2},{4,5},{5,4},{6,7},{7,6},{8,9},{9,8},{10,11... | collective-permute-start | bytes 638984 | tf_op jit(solution)/shard_map/ppermute | solution.py:66
  22.7 1.5 %collective-permute-start.6 = (bf16[208,512]{1,0:T(8,128)(2,1)S(1)}, bf16[208,512]{1,0:T(8,128)(2,1)S(1)}, u32[]{:S(2)}, u32[]{:S(2)}) collective-permute-start(bf16[208,512]{1,0:T(8,128)(2,1)S(1)} %collective-permute-done.5.refs_6_), channel_id=1, source_target_pairs={{0,1},{1,0},{2,3},{3,2},{4,5},{5,4},{6,7},{7,6},{8,9},{9,8},{10,11... | collective-permute-start | bytes 638984 | tf_op jit(solution)/shard_map/ppermute | solution.py:66
  23.4 1.5 %collective-permute-start.13 = (bf16[208,512]{1,0:T(8,128)(2,1)S(1)}, bf16[208,512]{1,0:T(8,128)(2,1)S(1)}, u32[]{:S(2)}, u32[]{:S(2)}) collective-permute-start(bf16[208,512]{1,0:T(8,128)(2,1)S(1)} %collective-permute-done.12.refs_14_), channel_id=1, source_target_pairs={{0,1},{1,0},{2,3},{3,2},{4,5},{5,4},{6,7},{7,6},{8,9},{9,8},{10,11... | collective-permute-start | bytes 638984 | tf_op jit(solution)/shard_map/ppermute | solution.py:66
  26.2 18.5 %collective-permute-start.15 = (bf16[384,128]{1,0:T(8,128)(2,1)S(1)}, bf16[384,128]{1,0:T(8,128)(2,1)S(1)}, u32[]{:S(2)}, u32[]{:S(2)}) collective-permute-start(bf16[384,128]{1,0:T(8,128)(2,1)S(1)} %get-tuple-element.23), channel_id=1, source_target_pairs={{0,24},{1,25},{2,26},{3,27},{4,28},{5,29},{6,30},{7,31},{8,0},{9,1... | collective-permute-start | bytes 294920 | tf_op jit(solution)/shard_map/ppermute | solution.py:267
  29.9 14.9 %collective-permute-start.14 = (bf16[384,128]{1,0:T(8,128)(2,1)S(1)}, bf16[384,128]{1,0:T(8,128)(2,1)S(1)}, u32[]{:S(2)}, u32[]{:S(2)}) collective-permute-start(bf16[384,128]{1,0:T(8,128)(2,1)S(1)} %get-tuple-element.24), channel_id=1, source_target_pairs={{0,8},{1,9},{2,10},{3,11},{4,12},{5,13},{6,14},{7,15},{8,16},{9,17... | collective-permute-start | bytes 294920 | tf_op jit(solution)/shard_map/ppermute | solution.py:266
  46.2 9.3 %collective-permute-start.18 = (f16[252,384]{1,0:T(8,128)(2,1)S(1)}, f16[252,384]{1,0:T(8,128)(2,1)S(1)}, u32[]{:S(2)}, u32[]{:S(2)}) collective-permute-start(f16[252,384]{1,0:T(8,128)(2,1)S(1)} %get-tuple-element.25), channel_id=1, source_target_pairs={{0,24},{1,25},{2,26},{3,27},{4,28},{5,29},{6,30},{7,31},{8,0},{9,1... | collective-permute-start | bytes 580616 | tf_op jit(solution)/shard_map/ppermute | solution.py:333
  50.1 17.0 %collective-permute-start.17 = (f16[252,384]{1,0:T(8,128)(2,1)S(1)}, f16[252,384]{1,0:T(8,128)(2,1)S(1)}, u32[]{:S(2)}, u32[]{:S(2)}) collective-permute-start(f16[252,384]{1,0:T(8,128)(2,1)S(1)} %get-tuple-element.26), channel_id=1, source_target_pairs={{0,16},{1,17},{2,18},{3,19},{4,20},{5,21},{6,22},{7,23},{8,24},{9,... | collective-permute-start | bytes 580616 | tf_op jit(solution)/shard_map/ppermute | solution.py:333
  50.1 17.0 %collective-permute-start.16 = (f16[252,384]{1,0:T(8,128)(2,1)S(1)}, f16[252,384]{1,0:T(8,128)(2,1)S(1)}, u32[]{:S(2)}, u32[]{:S(2)}) collective-permute-start(f16[252,384]{1,0:T(8,128)(2,1)S(1)} %get-tuple-element.27), channel_id=1, source_target_pairs={{0,8},{1,9},{2,10},{3,11},{4,12},{5,13},{6,14},{7,15},{8,16},{9,17... | collective-permute-start | bytes 580616 | tf_op jit(solution)/shard_map/ppermute | solution.py:333
  50.7 16.5 %collective-permute-start.21 = (f32[6,8,128]{2,1,0:T(8,128)S(1)}, f32[6,8,128]{2,1,0:T(8,128)S(1)}, u32[]{:S(2)}, u32[]{:S(2)}) collective-permute-start(f32[6,8,128]{2,1,0:T(8,128)S(1)} %get-tuple-element.22.refs_4_), channel_id=1, source_target_pairs={{0,24},{1,25},{2,26},{3,27},{4,28},{5,29},{6,30},{7,31},{8,0},{9,1... | collective-permute-start | bytes 73736 | tf_op jit(solution)/shard_map/ppermute | solution.py:332
  53.9 13.7 %collective-permute-start.20 = (f32[6,8,128]{2,1,0:T(8,128)S(1)}, f32[6,8,128]{2,1,0:T(8,128)S(1)}, u32[]{:S(2)}, u32[]{:S(2)}) collective-permute-start(f32[6,8,128]{2,1,0:T(8,128)S(1)} %get-tuple-element.22.refs_4_), channel_id=1, source_target_pairs={{0,16},{1,17},{2,18},{3,19},{4,20},{5,21},{6,22},{7,23},{8,24},{9,... | collective-permute-start | bytes 73736 | tf_op jit(solution)/shard_map/ppermute | solution.py:332
  55.5 12.2 %collective-permute-start.19 = (f32[6,8,128]{2,1,0:T(8,128)S(1)}, f32[6,8,128]{2,1,0:T(8,128)S(1)}, u32[]{:S(2)}, u32[]{:S(2)}) collective-permute-start(f32[6,8,128]{2,1,0:T(8,128)S(1)} %get-tuple-element.22.refs_4_), channel_id=1, source_target_pairs={{0,8},{1,9},{2,10},{3,11},{4,12},{5,13},{6,14},{7,15},{8,16},{9,17... | collective-permute-start | bytes 73736 | tf_op jit(solution)/shard_map/ppermute | solution.py:332

commit v3 on v0

v3 whole, which is shorter than its diff:
```python
import functools

import jax
import jax.numpy as jnp
from jax import lax
from jax.experimental import pallas as pl
from jax.experimental.pallas import tpu as pltpu
from jax.sharding import PartitionSpec as P

GROUP = 8
CORE, X, Y = 1, 2, 4
KROWS = 32
TOP = 14.0
PAIR_LANES = 32
F32 = jnp.float32
BF16 = jnp.bfloat16
VMEM = pl.BlockSpec(memory_space=pltpu.VMEM)
HBM = pl.BlockSpec(memory_space=pltpu.HBM)


def call(kernel, outs, scratch=(), aliases=None, ins=None, flops=0):
    def run(*args):
        return pl.pallas_call(
            kernel,
            out_shape=outs,
            in_specs=[VMEM] * len(args) if ins is None else ins,
            out_specs=jax.tree.map(lambda _: VMEM, outs),
            scratch_shapes=list(scratch),
            input_output_aliases=aliases or {},
            compiler_params=pltpu.CompilerParams(vmem_limit_bytes=32 * 1024 * 1024),
            cost_estimate=pl.CostEstimate(
                flops=flops, bytes_accessed=1_000_000, transcendentals=0
            ),
        )(*args)

    return run


def shape(dims, dtype=F32):
    return jax.ShapeDtypeStruct(dims, dtype)


def place():
    me = lax.axis_index("mode")
    return lax.rem(me, GROUP), lax.div(me, GROUP)


def flip(values, mask, count):
    return lax.ppermute(values, "mode", [(i, i ^ mask) for i in range(count)])


def payload_kernel(basis, region, index, table, out, region_s, index_s, table_s, sems):
    copies = [
        pltpu.make_async_copy(basis, out.at[KROWS:], sems.at[0]),
        pltpu.make_async_copy(region, region_s, sems.at[1]),
        pltpu.make_async_copy(index, index_s, sems.at[2]),
        pltpu.make_async_copy(table, table_s, sems.at[3]),
    ]
    for copy in copies:
        copy.start()
    for copy in copies[1:]:
        copy.wait()
    slabs = region.shape[0]
    width = out.shape[1] // slabs
    terms = index.shape[0]
    entries = table.shape[0]
    row = lax.broadcasted_iota(jnp.int32, (KROWS, width), 0)
    for s in range(slabs):
        reg = region_s[s]
        block = jnp.zeros((KROWS, width), F32)
        for q in range(terms):
            at = index_s[q, reg]
            kappa = jnp.where(at < entries, table_s[jnp.minimum(at, entries - 1)], 0.0)
            block = jnp.where(lax.div(row, 3) == q, kappa, block)
        high = block.astype(BF16).astype(F32)
        mid = (block - high).astype(BF16).astype(F32)
        low = block - high - mid
        part = lax.rem(row, 3)
        block = jnp.where(part == 0, high, jnp.where(part == 1, mid, low))
        out[0:KROWS, s * width : (s + 1) * width] = block.astype(BF16)
    copies[0].wait()


def payload(basis, region, index, table):
    rows, cells = basis.shape
    return call(
        payload_kernel,
        shape((rows + KROWS, cells), BF16),
        [
            pltpu.SMEM(region.shape, jnp.int32),
            pltpu.SMEM(index.shape[::-1], jnp.int32),
            pltpu.SMEM(table.shape, F32),
            pltpu.SemaphoreType.DMA((4,)),
        ],
        ins=[HBM] * 4,
    )(basis, region, index.T, table)


def selector(own, rows, planes):
    j, a = place()
    line = lax.broadcasted_iota(jnp.int32, (planes * own, rows), 0)
    column = lax.broadcasted_iota(jnp.int32, (planes * own, rows), 1)
    shift = jnp.zeros((planes * own, rows), jnp.int32)
    for k in range(planes):
        start = lax.rem(a + k, planes) * (GROUP * own) + j * own - k * own
        shift = jnp.where(line >= k * own, start, shift)
    return jnp.where(column - line == shift, 1.0, 0.0).astype(BF16)


def across(width):
    line = lax.broadcasted_iota(jnp.int32, (width, width), 0)
    column = lax.broadcasted_iota(jnp.int32, (width, width), 1)
    same = jnp.where(line == column, 1.0, 0.0)
    beside = jnp.where(jnp.abs(line - column) == 1, 1.0, 0.0)
    mirror = jnp.where(line + column == width - 1, 1.0, 0.0)
    return jnp.concatenate([2.0 * same - beside, same - mirror], axis=1).astype(BF16)


def act(triples, stencil, side, right, left, squares, base, rows, terms):
    total, width = triples[0][1].shape
    own = total - rows
    for n, (before, here, after, weight) in enumerate(triples):
        lanes = pl.ds(base + n * width, width)
        side[...] = jnp.dot(here[...], stencil, preferred_element_type=F32)
        table = weight[...].astype(F32)
        kappas = []
        for q in range(terms):
            one = (table[3 * q : 3 * q + 1] + table[3 * q + 1 : 3 * q + 2]) + table[
                3 * q + 2 : 3 * q + 3
            ]
            kappas.append(jnp.broadcast_to(one, (8, width))[None])
        sums = [jnp.zeros((8, width), F32) for _ in range(terms)]
        for start in range(0, total, own):
            part = slice(start, start + own)
            value = here[part, :].astype(F32)
            back = value - before[part, :].astype(F32)
            ahead = value - after[part, :].astype(F32)
            shapes = (
                back + ahead,
                side[part, 0:width],
                back,
                ahead,
                side[part, width : 2 * width],
                value,
            )
            for q in range(terms):
                action = shapes[q].reshape(own // 8, 8, width) * kappas[q]
                action = action.reshape(own, width).astype(BF16)
                if start < rows:
                    right[q, part, lanes] = action
                    rounded = action.astype(F32).reshape(own // 8, 8, width)
                    sums[q] += jnp.sum(rounded * rounded, axis=0)
                else:
                    left[q * own : (q + 1) * own, lanes] = action
        for q in range(terms):
            squares[q] += sums[q]


def contract(left, right, total, own, terms, depth, first=False):
    offset = 0
    for k in range(terms):
        lines = own * (k + 1)
        product = lax.dot_general(
            left[0:lines, 0:depth],
            right[k, :, 0:depth],
            (((1,), (1,)), ((), ())),
            preferred_element_type=F32,
        )
        if first:
            total[offset : offset + lines, :] = product
        else:
            total[offset : offset + lines, :] += product
        offset += lines


def spread(pieces, pick, field, weights, rows):
    j, _ = place()
    width = field.shape[2]
    for flipped, piece in enumerate(pieces):
        core = jnp.bitwise_xor(jnp.bitwise_and(j, 1), flipped)
        slabs = piece[0].shape[1] // width
        for s in range(slabs):
            lanes = slice(s * width, (s + 1) * width)
            at = core * slabs + s
            weights[at] = piece[0][0:KROWS, lanes]
            start = KROWS
            done = 0
            for part in piece:
                size = part.shape[0] - start
                field[at, done : done + size] = part[start:, lanes]
                done += size
                start = 0
            field[at, rows:] = jnp.dot(
                pick, field[at, 0:rows], preferred_element_type=F32
            ).astype(BF16)


def inner(field, weights, stencil, side, right, left, squares, base, rows, terms):
    slabs, _, width = field.shape

    @pl.loop(0, (slabs - 2) // 2)
    def _(t):
        s = 2 * t + 1
        triples = [
            (field.at[s + n - 1], field.at[s + n], field.at[s + n + 1], weights.at[s + n])
            for n in range(2)
        ]
        start = pl.multiple_of(base + 2 * t * width, width)
        act(triples, stencil, side, right, left, squares, start, rows, terms)


def pick_into(ends, at, field, slot, taken):
    @pl.when(taken)
    def _():
        ends[at] = field[slot]


def seam(ours, theirs, ends, seam_weights, field_weights, mine_first):
    slabs = ours.shape[0]
    for taken, (one, two) in (
        (mine_first, (0, 1)),
        (jnp.logical_not(mine_first), (1, 0)),
    ):

        @pl.when(taken)
        def _():
            fields = (ours, theirs)
            ends[0] = fields[one][slabs - 2]
            ends[1] = fields[one][slabs - 1]
            ends[2] = fields[two][0]
            ends[3] = fields[two][1]
            seam_weights[0] = field_weights[one][slabs - 1]
            seam_weights[1] = field_weights[two][0]


def own_kernel(rows, terms, own, planes, *refs):
    mine, other, field, weights, total, squares, side, right, left = refs
    squares[...] = jnp.zeros_like(squares)
    spread([[mine], [other]], selector(own, rows, planes), field, weights, rows)
    inner(field, weights, across(field.shape[2]), side, right, left, squares, 0, rows, terms)
    depth = (field.shape[0] - 2) * field.shape[2]
    contract(left, right, total, planes * own, terms, depth, first=True)


def middle_kernel(rows, terms, own, planes, *refs):
    (by_x, by_y, others, own_field, own_weights, total_in, squares_in,
     field_x, weights_x, field_y, weights_y, total, squares,
     side, right, left, ends, end_weights) = refs
    j, _ = place()
    width = field_x.shape[2]
    stencil = across(width)
    pick = selector(own, rows, planes)
    height = by_x.shape[0]
    squares[...] = squares_in[...]
    spread([[by_x], [others.at[:height]]], pick, field_x, weights_x, rows)
    spread([[by_y], [others.at[height:]]], pick, field_y, weights_y, rows)
    depth = (field_x.shape[0] - 2) * width
    inner(field_x, weights_x, stencil, side, right, left, squares, 0, rows, terms)
    inner(field_y, weights_y, stencil, side, right, left, squares, depth, rows, terms)
    first = jnp.bitwise_and(j, X) == 0
    seam(own_field, field_x, ends, end_weights, (own_weights, weights_x), first)
    triples = [(ends.at[n], ends.at[n + 1], ends.at[n + 2], end_weights.at[n]) for n in range(2)]
    act(triples, stencil, side, right, left, squares, 2 * depth, rows, terms)
    total[...] = total_in[...]
    contract(left, right, total, planes * own, terms, 2 * depth + 2 * width)


def edge_kernel(*refs):
    pieces, strip = refs[:-1], refs[-1]
    j, _ = place()
    lines, cells = strip.shape
    parts = (pieces[0].shape[0] - KROWS) // lines
    width = cells // parts
    for piece, flips in zip(pieces, (0, CORE, X, Y)):
        for here, lanes in ((0, slice(0, width)), (GROUP - 1, slice(cells - width, cells))):

            @pl.when(jnp.bitwise_xor(j, flips) == here)
            def _():
                for n in range(parts):
                    strip[:, n * width : (n + 1) * width] = piece[
                        KROWS + n * lines : KROWS + (n + 1) * lines, lanes
                    ]


def last_kernel(rows, terms, own, planes, *refs):
    (one, two, strip, others_in, *rest) = refs
    fields, field_weights, rest = list(rest[:3]), list(rest[3:6]), rest[6:]
    (total_in, squares_in, mine, others, levels,
     field, weights, total, squares, side, right, left, ends, end_weights) = rest
    fields.append(field)
    field_weights.append(weights)
    slabs, every, width = field.shape
    lines = every - rows
    j, _ = place()
    chip = lax.div(j, 2)
    stencil = across(width)
    pick = selector(own, rows, planes)
    squares[...] = squares_in[...]
    height = one.shape[0] + two.shape[0]
    even = jnp.bitwise_and(j, CORE) == 0
    size = strip.shape[0]
    other = others_in[height:, :]
    first_core = jnp.where(even, strip[...], other)
    second_core = jnp.where(even, other, strip[...])
    for at, source in ((0, second_core), (5, first_core)):
        for n in range(rows // size):
            ends[at, n * size : (n + 1) * size] = source[:, n * width : (n + 1) * width]
        ends[at, rows:] = jnp.dot(pick, ends[at, 0:rows], preferred_element_type=F32).astype(BF16)
    spread([[one, two], [others_in.at[0:height]]], pick, field, weights, rows)
    inner(field, weights, stencil, side, right, left, squares, 0, rows, terms)
    for n, source in enumerate(fields):
        for number, at, slots, weight in (
            (0, 1, (0, 1), 0),
            (3, 3, (slabs - 2, slabs - 1), 1),
            (1, 6, (slabs - 2, slabs - 1), 2),
            (2, 8, (0, 1), 3),
        ):

            @pl.when(jnp.bitwise_xor(chip, n) == number)
            def _():
                ends[at] = source[slots[0]]
                ends[at + 1] = source[slots[1]]
                end_weights[weight] = field_weights[n][slots[1] if slots[0] else 0]

    first = jnp.bitwise_and(j, X) == 0
    seam(fields[2], field, ends.at[10:14], end_weights.at[4:6], (field_weights[2], weights), first)
    triples = [
        (ends.at[n - 1], ends.at[n], ends.at[n + 1], end_weights.at[m])
        for m, n in enumerate((1, 4, 7, 8, 11, 12))
    ]
    depth = (slabs - 2) * width
    for n in range(0, 6, 2):
        act(triples[n : n + 2], stencil, side, right, left, squares, depth + n * width, rows, terms)
    total[...] = total_in[...]
    contract(left, right, total, lines, terms, depth + 6 * width)
    lane = lax.broadcasted_iota(jnp.int32, (8, rows), 1)
    line = lax.broadcasted_iota(jnp.int32, (8, rows), 0)
    spare = jnp.zeros((8, rows), F32)
    for q in range(terms):
        level = jnp.sum(squares[q], keepdims=True)
        levels[q : q + 1, :] = jnp.broadcast_to(level, (1, levels.shape[1]))
        power = jnp.ceil(jnp.log2(jnp.maximum(level, 1e-30)))
        level = level * jnp.exp2(-power)
        high = jnp.floor(level * 2.0**10) * 2.0**-10
        low = (level - high) * 2.0**10
        low = jnp.floor(low * 2.0**10) * 2.0**-10
        for n, value in enumerate((power, high, low)):
            here = jnp.logical_and(line == 0, lane == PAIR_LANES + 3 * q + n)
            spare = jnp.where(here, value, spare)
    levels[terms:, :] = jnp.zeros((levels.shape[0] - terms, levels.shape[1]), F32)
    offset = 0
    for k in range(terms):
        for q in range(k + 1):
            pair = q * terms - q * (q - 1) // 2 + k - q
            at = offset + q * lines
            block = total[at : at + lines, :]
            largest = jnp.max(jnp.abs(block), keepdims=True)
            power = jnp.ceil(jnp.log2(jnp.maximum(largest, 1e-30)))
            spare = jnp.where(jnp.logical_and(line == 0, lane == pair), power, spare)
            scale = jnp.exp2(TOP - power)
            for z in range(planes):
                part = total[at + z * own : at + (z + 1) * own, :]
                if z == 0:
                    mine[pair * own : (pair + 1) * own, :] = part
                else:
                    others[z - 1, pair * own : (pair + 1) * own, :] = part * scale
        offset += (k + 1) * lines
    end = terms * (terms + 1) // 2 * own
    for z in range(1, planes):
        others[z - 1, end:, :] = spare[0 : others.shape[1] - end]


def finish_kernel(own, terms, cells, *refs):
    parts, (levels, out) = refs[:-2], refs[-2:]
    rows = parts[0].shape[1]
    pairs = terms * (terms + 1) // 2
    spares = [part[pairs * own : pairs * own + 1, 0:128] for part in parts[1:]]
    norms = []
    for q in range(terms):
        level = levels[q : q + 1, 0:1]
        for spare in spares:
            power, high, low = (
                spare[:, PAIR_LANES + 3 * q + n : PAIR_LANES + 3 * q + n + 1] for n in range(3)
            )
            level = level + (high + low * 2.0**-10) * jnp.exp2(power)
        norms.append(lax.rsqrt(level / (rows * cells) + 1e-06) * cells**-0.5)
    powers = [jnp.exp2(spare - TOP) for spare in spares]
    pair = 0
    for q in range(terms):
        for k in range(q, terms):
            here = slice(pair * own, (pair + 1) * own)
            total = parts[0][here, :]
            for part, power in zip(parts[1:], powers):
                total = total + part[here, :] * power[:, pair : pair + 1]
            out[:, pair, :] = total * (norms[q] * norms[k])
            pair += 1


def per_device(basis, slab_region, coef_index, coef_table):
    terms = coef_index.shape[1]
    rows, cells = basis.shape
    width = cells // slab_region.shape[0]
    count = lax.axis_size("mode")
    planes = count // GROUP
    own = rows // count
    lines = planes * own
    every = rows + lines
    pairs = terms * (terms + 1) // 2
    slabs = 2 * slab_region.shape[0]
    sizes = (rows, terms, own, planes)
    flops = 20_000_000_000

    chip = (shape((slabs, every, width), BF16), shape((slabs, KROWS, width), BF16))
    sums = (shape((pairs * lines, rows)), shape((terms, 8, width)))

    def scratch(number):
        return [
            pltpu.VMEM((every, 2 * width), F32),
            pltpu.VMEM((terms, rows, number * width), BF16),
            pltpu.VMEM((terms * lines, number * width), BF16),
        ]

    def ends(number, borders):
        return [pltpu.VMEM((number, every, width), BF16), pltpu.VMEM((borders, KROWS, width), BF16)]

    block = payload(basis, slab_region, coef_index, coef_table)
    by_x = flip(block, X, count)
    by_y = flip(block, Y, count)
    by_core = flip(block, CORE, count)
    field, weights, total, squares = call(
        functools.partial(own_kernel, *sizes), chip + sums, scratch(slabs - 2), flops=flops // 8
    )(block, by_core)
    by_x, by_y, total = lax.optimization_barrier((by_x, by_y, total))

    half = block.shape[0] // 2
    one = flip(by_x[:half], Y, count)
    two = flip(by_y[half:], X, count)
    by_xy_core = flip(jnp.concatenate([by_x, by_y], axis=0), CORE, count)
    strip = call(edge_kernel, shape((rows * width // cells, cells), BF16))(
        block, by_core, by_x, by_y
    )
    pairs_of = []
    for i in range(count):
        here = i % GROUP
        if here in (0, 1, 2, 4):
            to = (i - here - GROUP) % count + (6 if here == 1 else here)
        else:
            to = (i - here + GROUP) % count + (1 if here == 6 else here)
        pairs_of.append((i, to))
    strip = lax.ppermute(strip, "mode", pairs_of)
    x_field, x_weights, y_field, y_weights, total, squares = call(
        functools.partial(middle_kernel, *sizes),
        chip + chip + sums,
        scratch(2 * slabs - 2) + ends(4, 2),
        flops=flops // 4,
    )(by_x, by_y, by_xy_core, field, weights, total, squares)

    diagonal = flip(jnp.concatenate([one, two, strip], axis=0), CORE, count)
    high_rows = pairs * own + 8 - (pairs * own) % 8
    mine, others, levels = call(
        functools.partial(last_kernel, *sizes),
        (shape((high_rows, rows)), shape((planes - 1, high_rows, rows)), shape((8, 128))),
        [pltpu.VMEM(o.shape, o.dtype) for o in chip + sums] + scratch(slabs + 4) + ends(14, 6),
        flops=flops // 4,
    )(
        one, two, strip, diagonal, field, x_field, y_field, weights, x_weights, y_weights,
        total, squares,
    )

    parts = [mine]
    others = others.astype(jnp.float16)
    for z in range(1, planes):
        there = [(i, (i + z * GROUP) % count) for i in range(count)]
        parts.append(lax.ppermute(others[z - 1], "mode", there).astype(F32))
    out = call(
        functools.partial(finish_kernel, own, terms, cells * count), shape((own, pairs, rows))
    )(*parts, levels)
    return jnp.transpose(out, (1, 0, 2))


def solution(mesh):
    return jax.shard_map(
        per_device,
        mesh=mesh,
        in_specs=(P("groups", "mode"), P(("groups", "mode")), P("groups", None), P("groups")),
        out_specs=P(None, ("groups", "mode"), None),
        check_vma=False,
    )
```

time: 245 us -> 65.6 us (0.27)
  the two profiles are of different devices: /device:TPU:0 before, /device:TPU:15 now
where the time goes in v3:
time: 65.6 us; the launch traced here: 65.4 us
  waiting for transfers between devices  27.9 us (43%)
  Pallas kernels  21.7 us (33%)
  starting transfers between devices  12.4 us (19%)
  local copies, waits for them, and re-layouts  3.14 us (5%)
    pallas_call x6, Pallas kernels, run(): pl.pallas_call(kernel, out_shape=outs, in_specs=[VMEM] * len(args) if ins...  21.7 us
    ppermute x3, waiting for transfers between devices, per_device(): parts.append(lax.ppermute(others[z - 1], 'mode', there).astype(F32))  16.6 us
    ppermute x7, waiting for transfers between devices, flip(): return lax.ppermute(values, 'mode', [(i, i ^ mask) for i in range(count)])  8.83 us
    ppermute x7, starting transfers between devices, flip(): return lax.ppermute(values, 'mode', [(i, i ^ mask) for i in range(count)])  5.58 us
    ppermute x3, starting transfers between devices, per_device(): parts.append(lax.ppermute(others[z - 1], 'mode', there).astype(F32))  5.49 us
    unnamed x8, local copies, waits for them, and re-layouts  2.99 us
    ppermute x1, waiting for transfers between devices, per_device(): strip = lax.ppermute(strip, 'mode', pairs_of)  2.47 us
    ppermute x1, starting transfers between devices, per_device(): strip = lax.ppermute(strip, 'mode', pairs_of)  1.35 us
  transfers between devices with their start and end apart: 11, of which 7 were waited for; matrix products, arithmetic and copies ran while one was open for 0% of the time, Pallas kernels for 19%

profile of v3, /device:TPU:15, one launch (start us, length us, event | category | flops | bytes accessed | tf_op | source)
XLA Modules:
  0.0 65.4 jit_solution(10873655519273407924)
XLA Ops:
  0.0 0.0 copy-start
  0.0 1.0 %copy-done = bf16[384,512]{1,0:T(8,128)(2,1)S(1)} copy-done((bf16[384,512]{1,0:T(8,128)(2,1)S(1)}, bf16[384,512]{1,0:T(8,128)(2,1)}, u32[]{:S(2)}) %copy-start) | copy-done | bytes 393240
  1.0 0.0 copy-start.1
  1.0 0.7 %copy-done.1 = s32[9,6]{0,1:T(8,128)S(1)} copy-done((s32[9,6]{0,1:T(8,128)S(1)}, s32[9,6]{0,1:T(8,128)}, u32[]{:S(2)}) %copy-start.1) | copy-done | bytes 240
  1.7 0.0 copy-start.2
  1.7 0.7 copy-done.2
  2.3 0.0 copy-start.3
  2.3 0.7 copy-done.3
  3.0 0.9 %shard_map.46.refs_0_ = bf16[416,512]{1,0:T(8,128)(2,1)S(1)} custom-call(bf16[384,512]{1,0:T(8,128)(2,1)S(1)} %copy-done, s32[4]{0:T(128)S(1)} %copy-done.2, s32[6,9]{1,0:T(8,128)S(1)} %bitcast.8, f32[8]{0:T(128)S(1)} %copy-done.3), custom_call_target="tpu_custom_call" | custom-call | bytes 1000000 | tf_op jit(solution)/shard_map/pallas_call | solution.py:23
  3.9 0.7 %collective-permute-start.2 = (bf16[416,512]{1,0:T(8,128)(2,1)S(1)}, bf16[416,512]{1,0:T(8,128)(2,1)S(1)}, u32[]{:S(2)}, u32[]{:S(2)}) collective-permute-start(bf16[416,512]{1,0:T(8,128)(2,1)S(1)} %shard_map.46.refs_0_), channel_id=1, source_target_pairs={{0,1},{1,0},{2,3},{3,2},{4,5},{5,4},{6,7},{7,6},{8,9},{9,8},{10,11... | collective-permute-start | bytes 1277960 | tf_op jit(solution)/shard_map/ppermute | solution.py:49
  4.6 0.3 collective-permute-start
  4.9 0.2 collective-permute-start.1
  5.1 0.9 %collective-permute-done.2.refs_1_ = bf16[416,512]{1,0:T(8,128)(2,1)S(1)} collective-permute-done((bf16[416,512]{1,0:T(8,128)(2,1)S(1)}, bf16[416,512]{1,0:T(8,128)(2,1)S(1)}, u32[]{:S(2)}, u32[]{:S(2)}) %collective-permute-start.2) | collective-permute-done | bytes 426016 | tf_op jit(solution)/shard_map/ppermute | solution.py:49
  6.0 4.0 %shard_map.47 = (bf16[8,432,128]{2,1,0:T(8,128)(2,1)S(1)}, bf16[8,32,128]{2,1,0:T(8,128)(2,1)S(1)}, f32[1008,384]{1,0:T(8,128)S(1)}, f32[6,8,128]{2,1,0:T(8,128)S(1)}) custom-call(bf16[416,512]{1,0:T(8,128)(2,1)S(1)} %shard_map.46.refs_0_, bf16[416,512]{1,0:T(8,128)(2,1)S(1)} %collective-permute-done.2.refs_1_), custom_call_target="tpu_custom_call" | custom-call | flops 2500000000 | bytes 1000000 | tf_op jit(solution)/shard_map/pallas_call | solution.py:23
  10.0 6.0 %collective-permute-done.refs_2_.refs_0_ = bf16[416,512]{1,0:T(8,128)(2,1)S(1)} collective-permute-done((bf16[416,512]{1,0:T(8,128)(2,1)S(1)}, bf16[416,512]{1,0:T(8,128)(2,1)S(1)}, u32[]{:S(2)}, u32[]{:S(2)}) %collective-permute-start) | collective-permute-done | bytes 426016 | tf_op jit(solution)/shard_map/ppermute | solution.py:49
  16.0 0.0 collective-permute-done.1.refs_3_.refs_1_
  16.0 0.1 pad_maximum_fusion
  16.1 1.2 %collective-permute-start.7 = (bf16[832,512]{1,0:T(8,128)(2,1)S(1)}, bf16[832,512]{1,0:T(8,128)(2,1)S(1)}, u32[]{:S(2)}, u32[]{:S(2)}) collective-permute-start(bf16[832,512]{1,0:T(8,128)(2,1)S(1)} %pad_maximum_fusion), channel_id=1, source_target_pairs={{0,1},{1,0},{2,3},{3,2},{4,5},{5,4},{6,7},{7,6},{8,9},{9,8},{10,11... | collective-permute-start | bytes 2555912 | tf_op jit(solution)/shard_map/ppermute | solution.py:49
  17.3 0.3 collective-permute-start.3
  17.6 1.2 %collective-permute-start.4 = (bf16[208,512]{1,0:T(8,128)(2,1)S(1)}, bf16[208,512]{1,0:T(8,128)(2,1)S(1)}, u32[]{:S(2)}, u32[]{:S(2)}) collective-permute-start(bf16[208,512]{1,0:T(8,128)(2,1)S(1)} %slice.16), channel_id=1, source_target_pairs={{0,2},{1,3},{2,0},{3,1},{4,6},{5,7},{6,4},{7,5},{8,10},{9,11},{10,... | collective-permute-start | bytes 638984 | tf_op jit(solution)/shard_map/ppermute | solution.py:49
  18.9 1.3 %collective-permute-start.5 = (bf16[96,512]{1,0:T(8,128)(2,1)S(1)}, bf16[96,512]{1,0:T(8,128)(2,1)S(1)}, u32[]{:S(2)}, u32[]{:S(2)}) collective-permute-start(bf16[96,512]{1,0:T(8,128)(2,1)S(1)} %shard_map.48), channel_id=1, source_target_pairs={{0,24},{1,30},{2,26},{3,11},{4,28},{5,13},{6,9},{7,15},{8,0},{9,6}... | collective-permute-start | bytes 294920 | tf_op jit(solution)/shard_map/ppermute | solution.py:450
  20.2 2.5 %collective-permute-done.5.refs_2_ = bf16[96,512]{1,0:T(8,128)(2,1)S(1)} collective-permute-done((bf16[96,512]{1,0:T(8,128)(2,1)S(1)}, bf16[96,512]{1,0:T(8,128)(2,1)S(1)}, u32[]{:S(2)}, u32[]{:S(2)}) %collective-permute-start.5) | collective-permute-done | bytes 98336 | tf_op jit(solution)/shard_map/ppermute | solution.py:450
  22.7 1.9 %collective-permute-done.3.refs_0_ = bf16[208,512]{1,0:T(8,128)(2,1)S(1)} collective-permute-done((bf16[208,512]{1,0:T(8,128)(2,1)S(1)}, bf16[208,512]{1,0:T(8,128)(2,1)S(1)}, u32[]{:S(2)}, u32[]{:S(2)}) %collective-permute-start.3) | collective-permute-done | bytes 213024 | tf_op jit(solution)/shard_map/ppermute | solution.py:49
  24.6 0.0 collective-permute-done.4.refs_1_
  24.6 1.7 %collective-permute-start.6 = (bf16[512,512]{1,0:T(8,128)(2,1)S(1)}, bf16[512,512]{1,0:T(8,128)(2,1)S(1)}, u32[]{:S(2)}, u32[]{:S(2)}) collective-permute-start(bf16[512,512]{1,0:T(8,128)(2,1)S(1)} %pad_maximum_fusion.1), channel_id=1, source_target_pairs={{0,1},{1,0},{2,3},{3,2},{4,5},{5,4},{6,7},{7,6},{8,9},{9,8},{10,11... | collective-permute-start | bytes 1572872 | tf_op jit(solution)/shard_map/ppermute | solution.py:49
  26.3 0.0 collective-permute-done.7.refs_2_
  26.3 8.2 %shard_map.49 = (bf16[8,432,128]{2,1,0:T(8,128)(2,1)S(1)}, bf16[8,32,128]{2,1,0:T(8,128)(2,1)S(1)}, bf16[8,432,128]{2,1,0:T(8,128)(2,1)S(1)}, bf16[8,32,128]{2,1...) custom-call(bf16[416,512]{1,0:T(8,128)(2,1)S(1)} %collective-permute-done.refs_2_.refs_0_, ...), custom_call_target="tpu_custom_call" | custom-call | flops 5000000000 | bytes 1000000 | tf_op jit(solution)/shard_map/pallas_call | solution.py:23
  34.5 0.0 collective-permute-done.6.refs_3_
  34.6 7.4 %shard_map.50 = (f32[256,384]{1,0:T(8,128)S(1)}, f32[3,256,384]{2,1,0:T(8,128)S(1)}, f32[8,128]{1,0:T(8,128)S(1)}) custom-call(bf16[208,512]{1,0:T(8,128)(2,1)S(1)} %collective-permute-done.3.refs_0_, bf16[208,512]{1,0:T(8,128)(2,1)S(1)} %collective-permute-done.4.refs_1_, bf16[96,512]{1,0:T(8,128)(2,1)S(1)} %collective-permute-done.5.refs_2_, ...), custom_call_target="tpu_custom_call" | custom-call | flops 5000000000 | bytes 1000000 | tf_op jit(solution)/shard_map/pallas_call | solution.py:23
  41.9 0.1 convert_element_type.12
  42.0 0.1 slice_bitcast_fusion
  42.1 1.4 %collective-permute-start.8 = (f16[256,384]{1,0:T(8,128)(2,1)S(1)}, f16[256,384]{1,0:T(8,128)(2,1)S(1)}, u32[]{:S(2)}, u32[]{:S(2)}) collective-permute-start(f16[256,384]{1,0:T(8,128)(2,1)S(1)} %get-tuple-element.39), channel_id=1, source_target_pairs={{0,8},{1,9},{2,10},{3,11},{4,12},{5,13},{6,14},{7,15},{8,16},{9,17... | collective-permute-start | bytes 589832 | tf_op jit(solution)/shard_map/ppermute | solution.py:474
  43.5 2.8 %collective-permute-start.9 = (f16[256,384]{1,0:T(8,128)(2,1)S(1)}, f16[256,384]{1,0:T(8,128)(2,1)S(1)}, u32[]{:S(2)}, u32[]{:S(2)}) collective-permute-start(f16[256,384]{1,0:T(8,128)(2,1)S(1)} %get-tuple-element.38), channel_id=1, source_target_pairs={{0,16},{1,17},{2,18},{3,19},{4,20},{5,21},{6,22},{7,23},{8,24},{9,... | collective-permute-start | bytes 589832 | tf_op jit(solution)/shard_map/ppermute | solution.py:474
  46.2 1.4 %collective-permute-start.10 = (f16[256,384]{1,0:T(8,128)(2,1)S(1)}, f16[256,384]{1,0:T(8,128)(2,1)S(1)}, u32[]{:S(2)}, u32[]{:S(2)}) collective-permute-start(f16[256,384]{1,0:T(8,128)(2,1)S(1)} %get-tuple-element.37), channel_id=1, source_target_pairs={{0,24},{1,25},{2,26},{3,27},{4,28},{5,29},{6,30},{7,31},{8,0},{9,1... | collective-permute-start | bytes 589832 | tf_op jit(solution)/shard_map/ppermute | solution.py:474
  47.6 1.1 %collective-permute-done.8 = f16[256,384]{1,0:T(8,128)(2,1)S(1)} collective-permute-done((f16[256,384]{1,0:T(8,128)(2,1)S(1)}, f16[256,384]{1,0:T(8,128)(2,1)S(1)}, u32[]{:S(2)}, u32[]{:S(2)}) %collective-permute-start.8) | collective-permute-done | bytes 196640 | tf_op jit(solution)/shard_map/ppermute | solution.py:474
  48.7 11.7 %collective-permute-done.9 = f16[256,384]{1,0:T(8,128)(2,1)S(1)} collective-permute-done((f16[256,384]{1,0:T(8,128)(2,1)S(1)}, f16[256,384]{1,0:T(8,128)(2,1)S(1)}, u32[]{:S(2)}, u32[]{:S(2)}) %collective-permute-start.9) | collective-permute-done | bytes 196640 | tf_op jit(solution)/shard_map/ppermute | solution.py:474
  60.5 3.8 %collective-permute-done.10 = f16[256,384]{1,0:T(8,128)(2,1)S(1)} collective-permute-done((f16[256,384]{1,0:T(8,128)(2,1)S(1)}, f16[256,384]{1,0:T(8,128)(2,1)S(1)}, u32[]{:S(2)}, u32[]{:S(2)}) %collective-permute-start.10) | collective-permute-done | bytes 196640 | tf_op jit(solution)/shard_map/ppermute | solution.py:474
  64.3 1.2 %shard_map.51 = f32[12,21,384]{2,1,0:T(8,128)} custom-call(f32[256,384]{1,0:T(8,128)S(1)} %get-tuple-element.34.refs_0_, f32[256,384]{1,0:T(8,128)S(1)} %convert_element_type.13.refs_1_, f32[256,384]{1,0:T(8,128)S(1)} %convert_element_type.14.refs_2_, f32[256,384]{1,0:T(8,128)S(1)} %convert_element_type.15.refs_3_, f32[8,128]{1,0:T(8,128)S(1)} %get-tuple-element.36.refs_4_), custom_call_target="tpu_custom_call" | custom-call | bytes 1000000 | tf_op jit(solution)/shard_map/pallas_call | solution.py:23
  (7 shorter events, 0.2 us)
Async XLA Ops:
  0.0 1.0 %copy-start = (bf16[384,512]{1,0:T(8,128)(2,1)S(1)}, bf16[384,512]{1,0:T(8,128)(2,1)}, u32[]{:S(2)}) copy-start(bf16[384,512]{1,0:T(8,128)(2,1)} %basis.1) | copy-start | bytes 1179652
  1.0 0.7 %copy-start.1 = (s32[9,6]{0,1:T(8,128)S(1)}, s32[9,6]{0,1:T(8,128)}, u32[]{:S(2)}) copy-start(s32[9,6]{0,1:T(8,128)} %param.6) | copy-start | bytes 652
  1.7 0.7 %copy-start.2 = (s32[4]{0:T(128)S(1)}, s32[4]{0:T(128)}, u32[]{:S(2)}) copy-start(s32[4]{0:T(128)} %region.1) | copy-start | bytes 52
  2.3 0.7 %copy-start.3 = (f32[8]{0:T(128)S(1)}, f32[8]{0:T(128)}, u32[]{:S(2)}) copy-start(f32[8]{0:T(128)} %table.1) | copy-start | bytes 100
  3.9 2.1 %collective-permute-start.2 = (bf16[416,512]{1,0:T(8,128)(2,1)S(1)}, bf16[416,512]{1,0:T(8,128)(2,1)S(1)}, u32[]{:S(2)}, u32[]{:S(2)}) collective-permute-start(bf16[416,512]{1,0:T(8,128)(2,1)S(1)} %shard_map.46.refs_0_), channel_id=1, source_target_pairs={{0,1},{1,0},{2,3},{3,2},{4,5},{5,4},{6,7},{7,6},{8,9},{9,8},{10,11... | collective-permute-start | bytes 1277960 | tf_op jit(solution)/shard_map/ppermute | solution.py:49
  4.6 11.4 %collective-permute-start = (bf16[416,512]{1,0:T(8,128)(2,1)S(1)}, bf16[416,512]{1,0:T(8,128)(2,1)S(1)}, u32[]{:S(2)}, u32[]{:S(2)}) collective-permute-start(bf16[416,512]{1,0:T(8,128)(2,1)S(1)} %shard_map.46.refs_0_), channel_id=1, source_target_pairs={{0,2},{1,3},{2,0},{3,1},{4,6},{5,7},{6,4},{7,5},{8,10},{9,11},{10,... | collective-permute-start | bytes 1277960 | tf_op jit(solution)/shard_map/ppermute | solution.py:49
  4.9 11.1 %collective-permute-start.1 = (bf16[416,512]{1,0:T(8,128)(2,1)S(1)}, bf16[416,512]{1,0:T(8,128)(2,1)S(1)}, u32[]{:S(2)}, u32[]{:S(2)}) collective-permute-start(bf16[416,512]{1,0:T(8,128)(2,1)S(1)} %shard_map.46.refs_0_), channel_id=1, source_target_pairs={{0,4},{1,5},{2,6},{3,7},{4,0},{5,1},{6,2},{7,3},{8,12},{9,13},{10,... | collective-permute-start | bytes 1277960 | tf_op jit(solution)/shard_map/ppermute | solution.py:49
  16.1 10.2 %collective-permute-start.7 = (bf16[832,512]{1,0:T(8,128)(2,1)S(1)}, bf16[832,512]{1,0:T(8,128)(2,1)S(1)}, u32[]{:S(2)}, u32[]{:S(2)}) collective-permute-start(bf16[832,512]{1,0:T(8,128)(2,1)S(1)} %pad_maximum_fusion), channel_id=1, source_target_pairs={{0,1},{1,0},{2,3},{3,2},{4,5},{5,4},{6,7},{7,6},{8,9},{9,8},{10,11... | collective-permute-start | bytes 2555912 | tf_op jit(solution)/shard_map/ppermute | solution.py:49
  17.3 7.3 %collective-permute-start.3 = (bf16[208,512]{1,0:T(8,128)(2,1)S(1)}, bf16[208,512]{1,0:T(8,128)(2,1)S(1)}, u32[]{:S(2)}, u32[]{:S(2)}) collective-permute-start(bf16[208,512]{1,0:T(8,128)(2,1)S(1)} %slice.15), channel_id=1, source_target_pairs={{0,4},{1,5},{2,6},{3,7},{4,0},{5,1},{6,2},{7,3},{8,12},{9,13},{10,... | collective-permute-start | bytes 638984 | tf_op jit(solution)/shard_map/ppermute | solution.py:49
  17.6 7.0 %collective-permute-start.4 = (bf16[208,512]{1,0:T(8,128)(2,1)S(1)}, bf16[208,512]{1,0:T(8,128)(2,1)S(1)}, u32[]{:S(2)}, u32[]{:S(2)}) collective-permute-start(bf16[208,512]{1,0:T(8,128)(2,1)S(1)} %slice.16), channel_id=1, source_target_pairs={{0,2},{1,3},{2,0},{3,1},{4,6},{5,7},{6,4},{7,5},{8,10},{9,11},{10,... | collective-permute-start | bytes 638984 | tf_op jit(solution)/shard_map/ppermute | solution.py:49
  18.9 3.8 %collective-permute-start.5 = (bf16[96,512]{1,0:T(8,128)(2,1)S(1)}, bf16[96,512]{1,0:T(8,128)(2,1)S(1)}, u32[]{:S(2)}, u32[]{:S(2)}) collective-permute-start(bf16[96,512]{1,0:T(8,128)(2,1)S(1)} %shard_map.48), channel_id=1, source_target_pairs={{0,24},{1,30},{2,26},{3,11},{4,28},{5,13},{6,9},{7,15},{8,0},{9,6}... | collective-permute-start | bytes 294920 | tf_op jit(solution)/shard_map/ppermute | solution.py:450
  24.6 9.9 %collective-permute-start.6 = (bf16[512,512]{1,0:T(8,128)(2,1)S(1)}, bf16[512,512]{1,0:T(8,128)(2,1)S(1)}, u32[]{:S(2)}, u32[]{:S(2)}) collective-permute-start(bf16[512,512]{1,0:T(8,128)(2,1)S(1)} %pad_maximum_fusion.1), channel_id=1, source_target_pairs={{0,1},{1,0},{2,3},{3,2},{4,5},{5,4},{6,7},{7,6},{8,9},{9,8},{10,11... | collective-permute-start | bytes 1572872 | tf_op jit(solution)/shard_map/ppermute | solution.py:49
  42.1 6.6 %collective-permute-start.8 = (f16[256,384]{1,0:T(8,128)(2,1)S(1)}, f16[256,384]{1,0:T(8,128)(2,1)S(1)}, u32[]{:S(2)}, u32[]{:S(2)}) collective-permute-start(f16[256,384]{1,0:T(8,128)(2,1)S(1)} %get-tuple-element.39), channel_id=1, source_target_pairs={{0,8},{1,9},{2,10},{3,11},{4,12},{5,13},{6,14},{7,15},{8,16},{9,17... | collective-permute-start | bytes 589832 | tf_op jit(solution)/shard_map/ppermute | solution.py:474
  43.5 17.0 %collective-permute-start.9 = (f16[256,384]{1,0:T(8,128)(2,1)S(1)}, f16[256,384]{1,0:T(8,128)(2,1)S(1)}, u32[]{:S(2)}, u32[]{:S(2)}) collective-permute-start(f16[256,384]{1,0:T(8,128)(2,1)S(1)} %get-tuple-element.38), channel_id=1, source_target_pairs={{0,16},{1,17},{2,18},{3,19},{4,20},{5,21},{6,22},{7,23},{8,24},{9,... | collective-permute-start | bytes 589832 | tf_op jit(solution)/shard_map/ppermute | solution.py:474
  46.2 18.0 %collective-permute-start.10 = (f16[256,384]{1,0:T(8,128)(2,1)S(1)}, f16[256,384]{1,0:T(8,128)(2,1)S(1)}, u32[]{:S(2)}, u32[]{:S(2)}) collective-permute-start(f16[256,384]{1,0:T(8,128)(2,1)S(1)} %get-tuple-element.37), channel_id=1, source_target_pairs={{0,24},{1,25},{2,26},{3,27},{4,28},{5,29},{6,30},{7,31},{8,0},{9,1... | collective-permute-start | bytes 589832 | tf_op jit(solution)/shard_map/ppermute | solution.py:474

commit v4 on v3

--- a/solution.py
+++ b/solution.py
@@ -18,7 +18,7 @@
 HBM = pl.BlockSpec(memory_space=pltpu.HBM)
 
 
-def call(kernel, outs, scratch=(), aliases=None, ins=None, flops=0):
+def call(kernel, outs, scratch=(), aliases=None, ins=None):
     def run(*args):
         return pl.pallas_call(
             kernel,
@@ -28,9 +28,7 @@
             scratch_shapes=list(scratch),
             input_output_aliases=aliases or {},
             compiler_params=pltpu.CompilerParams(vmem_limit_bytes=32 * 1024 * 1024),
-            cost_estimate=pl.CostEstimate(
-                flops=flops, bytes_accessed=1_000_000, transcendentals=0
-            ),
+            cost_estimate=pl.CostEstimate(flops=0, bytes_accessed=0, transcendentals=0),
         )(*args)
 
     return run
@@ -49,16 +47,15 @@
     return lax.ppermute(values, "mode", [(i, i ^ mask) for i in range(count)])
 
 
-def payload_kernel(basis, region, index, table, out, region_s, index_s, table_s, sems):
+def weight_kernel(region, index, table, out, region_s, index_s, table_s, sems):
     copies = [
-        pltpu.make_async_copy(basis, out.at[KROWS:], sems.at[0]),
-        pltpu.make_async_copy(region, region_s, sems.at[1]),
-        pltpu.make_async_copy(index, index_s, sems.at[2]),
-        pltpu.make_async_copy(table, table_s, sems.at[3]),
+        pltpu.make_async_copy(region, region_s, sems.at[0]),
+        pltpu.make_async_copy(index, index_s, sems.at[1]),
+        pltpu.make_async_copy(table, table_s, sems.at[2]),
     ]
     for copy in copies:
         copy.start()
-    for copy in copies[1:]:
+    for copy in copies:
         copy.wait()
     slabs = region.shape[0]
     width = out.shape[1] // slabs
@@ -77,23 +74,21 @@
         low = block - high - mid
         part = lax.rem(row, 3)
         block = jnp.where(part == 0, high, jnp.where(part == 1, mid, low))
-        out[0:KROWS, s * width : (s + 1) * width] = block.astype(BF16)
-    copies[0].wait()
-
-
-def payload(basis, region, index, table):
-    rows, cells = basis.shape
+        out[:, s * width : (s + 1) * width] = block.astype(BF16)
+
+
+def weight_rows(cells, region, index, table):
     return call(
-        payload_kernel,
-        shape((rows + KROWS, cells), BF16),
+        weight_kernel,
+        shape((KROWS, cells), BF16),
         [
             pltpu.SMEM(region.shape, jnp.int32),
             pltpu.SMEM(index.shape[::-1], jnp.int32),
             pltpu.SMEM(table.shape, F32),
-            pltpu.SemaphoreType.DMA((4,)),
+            pltpu.SemaphoreType.DMA((3,)),
         ],
-        ins=[HBM] * 4,
-    )(basis, region, index.T, table)
+        ins=[HBM] * 3,
+    )(region, index.T, table)
 
 
 def selector(own, rows, planes):
@@ -156,7 +151,7 @@
             squares[q] += sums[q]
 
 
-def contract(left, right, total, own, terms, depth, first=False):
+def contract(left, right, total, own, terms, depth, before=None):
     offset = 0
     for k in range(terms):
         lines = own * (k + 1)
@@ -166,33 +161,34 @@
             (((1,), (1,)), ((), ())),
             preferred_element_type=F32,
         )
-        if first:
-            total[offset : offset + lines, :] = product
-        else:
-            total[offset : offset + lines, :] += product
+        if before is not None:
+            product = before[offset : offset + lines, :] + product
+        total[offset : offset + lines, :] = product
         offset += lines
 
 
 def spread(pieces, pick, field, weights, rows):
     j, _ = place()
     width = field.shape[2]
-    for flipped, piece in enumerate(pieces):
+    for flipped, (table, *parts) in enumerate(pieces):
         core = jnp.bitwise_xor(jnp.bitwise_and(j, 1), flipped)
-        slabs = piece[0].shape[1] // width
+        slabs = table.shape[1] // width
         for s in range(slabs):
             lanes = slice(s * width, (s + 1) * width)
             at = core * slabs + s
-            weights[at] = piece[0][0:KROWS, lanes]
-            start = KROWS
+            weights[at] = table[:, lanes]
             done = 0
-            for part in piece:
-                size = part.shape[0] - start
-                field[at, done : done + size] = part[start:, lanes]
+            for part in parts:
+                size = part.shape[0]
+                field[at, done : done + size] = part[:, lanes]
                 done += size
-                start = 0
             field[at, rows:] = jnp.dot(
                 pick, field[at, 0:rows], preferred_element_type=F32
             ).astype(BF16)
+
+
+def split(ref, start, rows):
+    return [ref.at[start + rows : start + rows + KROWS], ref.at[start : start + rows]]
 
 
 def inner(field, weights, stencil, side, right, left, squares, base, rows, terms):
@@ -234,42 +230,50 @@
 
 
 def own_kernel(rows, terms, own, planes, *refs):
-    mine, other, field, weights, total, squares, side, right, left = refs
+    (mine, table, other, other_table,
+     field, weights, total, squares, side, right, left) = refs
     squares[...] = jnp.zeros_like(squares)
-    spread([[mine], [other]], selector(own, rows, planes), field, weights, rows)
+    pick = selector(own, rows, planes)
+    spread([[table, mine], [other_table, other]], pick, field, weights, rows)
     inner(field, weights, across(field.shape[2]), side, right, left, squares, 0, rows, terms)
     depth = (field.shape[0] - 2) * field.shape[2]
-    contract(left, right, total, planes * own, terms, depth, first=True)
-
-
-def middle_kernel(rows, terms, own, planes, *refs):
-    (by_x, by_y, others, own_field, own_weights, total_in, squares_in,
-     field_x, weights_x, field_y, weights_y, total, squares,
-     side, right, left, ends, end_weights) = refs
+    contract(left, right, total, planes * own, terms, depth)
+
+
+def row_kernel(rows, terms, own, planes, *refs):
+    (mine, table, other, own_field, own_weights, total_in, squares_in,
+     field, weights, total, squares, side, right, left, ends, end_weights) = refs
     j, _ = place()
-    width = field_x.shape[2]
+    width = field.shape[2]
     stencil = across(width)
+    squares[...] = squares_in[...]
     pick = selector(own, rows, planes)
-    height = by_x.shape[0]
+    spread([[table, mine], split(other, 0, rows)], pick, field, weights, rows)
+    depth = (field.shape[0] - 2) * width
+    inner(field, weights, stencil, side, right, left, squares, 0, rows, terms)
+    first = jnp.bitwise_and(j, X) == 0
+    seam(own_field, field, ends, end_weights, (own_weights, weights), first)
+    triples = [(ends.at[n], ends.at[n + 1], ends.at[n + 2], end_weights.at[n]) for n in range(2)]
+    act(triples, stencil, side, right, left, squares, depth, rows, terms)
+    contract(left, right, total, planes * own, terms, depth + 2 * width, total_in)
+
+
+def lone_kernel(rows, terms, own, planes, *refs):
+    (mine, table, other, total_in, squares_in,
+     field, weights, total, squares, side, right, left) = refs
     squares[...] = squares_in[...]
-    spread([[by_x], [others.at[:height]]], pick, field_x, weights_x, rows)
-    spread([[by_y], [others.at[height:]]], pick, field_y, weights_y, rows)
-    depth = (field_x.shape[0] - 2) * width
-    inner(field_x, weights_x, stencil, side, right, left, squares, 0, rows, terms)
-    inner(field_y, weights_y, stencil, side, right, left, squares, depth, rows, terms)
-    first = jnp.bitwise_and(j, X) == 0
-    seam(own_field, field_x, ends, end_weights, (own_weights, weights_x), first)
-    triples = [(ends.at[n], ends.at[n + 1], ends.at[n + 2], end_weights.at[n]) for n in range(2)]
-    act(triples, stencil, side, right, left, squares, 2 * depth, rows, terms)
-    total[...] = total_in[...]
-    contract(left, right, total, planes * own, terms, 2 * depth + 2 * width)
+    pick = selector(own, rows, planes)
+    spread([[table, mine], split(other, rows + KROWS, rows)], pick, field, weights, rows)
+    inner(field, weights, across(field.shape[2]), side, right, left, squares, 0, rows, terms)
+    depth = (field.shape[0] - 2) * field.shape[2]
+    contract(left, right, total, planes * own, terms, depth, total_in)
 
 
 def edge_kernel(*refs):
     pieces, strip = refs[:-1], refs[-1]
     j, _ = place()
     lines, cells = strip.shape
-    parts = (pieces[0].shape[0] - KROWS) // lines
+    parts = pieces[0].shape[0] // lines
     width = cells // parts
     for piece, flips in zip(pieces, (0, CORE, X, Y)):
         for here, lanes in ((0, slice(0, width)), (GROUP - 1, slice(cells - width, cells))):
@@ -278,7 +282,7 @@
             def _():
                 for n in range(parts):
                     strip[:, n * width : (n + 1) * width] = piece[
-                        KROWS + n * lines : KROWS + (n + 1) * lines, lanes
+                        n * lines : (n + 1) * lines, lanes
                     ]
 
 
@@ -306,7 +310,18 @@
         for n in range(rows // size):
             ends[at, n * size : (n + 1) * size] = source[:, n * width : (n + 1) * width]
         ends[at, rows:] = jnp.dot(pick, ends[at, 0:rows], preferred_element_type=F32).astype(BF16)
-    spread([[one, two], [others_in.at[0:height]]], pick, field, weights, rows)
+    part = one.shape[0] - KROWS
+    there = others_in.at
+    spread(
+        [
+            [one.at[part:], one.at[0:part], two],
+            [there[part : part + KROWS], there[0:part], there[part + KROWS : height]],
+        ],
+        pick,
+        field,
+        weights,
+        rows,
+    )
     inner(field, weights, stencil, side, right, left, squares, 0, rows, terms)
     for n, source in enumerate(fields):
         for number, at, slots, weight in (
@@ -331,8 +346,7 @@
     depth = (slabs - 2) * width
     for n in range(0, 6, 2):
         act(triples[n : n + 2], stencil, side, right, left, squares, depth + n * width, rows, terms)
-    total[...] = total_in[...]
-    contract(left, right, total, lines, terms, depth + 6 * width)
+    contract(left, right, total, lines, terms, depth + 6 * width, total_in)
     lane = lax.broadcasted_iota(jnp.int32, (8, rows), 1)
     line = lax.broadcasted_iota(jnp.int32, (8, rows), 0)
     spare = jnp.zeros((8, rows), F32)
@@ -408,7 +422,6 @@
     pairs = terms * (terms + 1) // 2
     slabs = 2 * slab_region.shape[0]
     sizes = (rows, terms, own, planes)
-    flops = 20_000_000_000
 
     chip = (shape((slabs, every, width), BF16), shape((slabs, KROWS, width), BF16))
     sums = (shape((pairs * lines, rows)), shape((terms, 8, width)))
@@ -423,21 +436,27 @@
     def ends(number, borders):
         return [pltpu.VMEM((number, every, width), BF16), pltpu.VMEM((borders, KROWS, width), BF16)]
 
-    block = payload(basis, slab_region, coef_index, coef_table)
-    by_x = flip(block, X, count)
-    by_y = flip(block, Y, count)
-    by_core = flip(block, CORE, count)
+    by_x = flip(basis, X, count)
+    by_y = flip(basis, Y, count)
+    by_core = flip(basis, CORE, count)
+    by_core, slab_region = lax.optimization_barrier((by_core, slab_region))
+    table = weight_rows(cells, slab_region, coef_index, coef_table)
+    table_core = flip(table, CORE, count)
+    table_x = flip(table, X, count)
+    table_y = flip(table, Y, count)
     field, weights, total, squares = call(
-        functools.partial(own_kernel, *sizes), chip + sums, scratch(slabs - 2), flops=flops // 8
-    )(block, by_core)
-    by_x, by_y, total = lax.optimization_barrier((by_x, by_y, total))
-
-    half = block.shape[0] // 2
-    one = flip(by_x[:half], Y, count)
+        functools.partial(own_kernel, *sizes), chip + sums, scratch(slabs - 2)
+    )(basis, table, by_core, table_core)
+    by_x, by_y, table_x, table_y, total = lax.optimization_barrier(
+        (by_x, by_y, table_x, table_y, total)
+    )
+
+    half = (rows - KROWS) // 2
+    one = flip(jnp.concatenate([by_x[:half], table_x], axis=0), Y, count)
     two = flip(by_y[half:], X, count)
-    by_xy_core = flip(jnp.concatenate([by_x, by_y], axis=0), CORE, count)
+    others = flip(jnp.concatenate([by_x, table_x, by_y, table_y], axis=0), CORE, count)
     strip = call(edge_kernel, shape((rows * width // cells, cells), BF16))(
-        block, by_core, by_x, by_y
+        basis, by_core, by_x, by_y
     )
     pairs_of = []
     for i in range(count):
@@ -448,20 +467,24 @@
             to = (i - here + GROUP) % count + (1 if here == 6 else here)
         pairs_of.append((i, to))
     strip = lax.ppermute(strip, "mode", pairs_of)
-    x_field, x_weights, y_field, y_weights, total, squares = call(
-        functools.partial(middle_kernel, *sizes),
-        chip + chip + sums,
-        scratch(2 * slabs - 2) + ends(4, 2),
-        flops=flops // 4,
-    )(by_x, by_y, by_xy_core, field, weights, total, squares)
+    x_field, x_weights, total, squares = call(
+        functools.partial(row_kernel, *sizes),
+        chip + sums,
+        scratch(slabs) + ends(4, 2),
+    )(by_x, table_x, others, field, weights, total, squares)
+    one, two, strip, total = lax.optimization_barrier((one, two, strip, total))
 
     diagonal = flip(jnp.concatenate([one, two, strip], axis=0), CORE, count)
+    y_field, y_weights, total, squares = call(
+        functools.partial(lone_kernel, *sizes), chip + sums, scratch(slabs - 2)
+    )(by_y, table_y, others, total, squares)
+    diagonal, total = lax.optimization_barrier((diagonal, total))
+
     high_rows = pairs * own + 8 - (pairs * own) % 8
     mine, others, levels = call(
         functools.partial(last_kernel, *sizes),
         (shape((high_rows, rows)), shape((planes - 1, high_rows, rows)), shape((8, 128))),
         [pltpu.VMEM(o.shape, o.dtype) for o in chip + sums] + scratch(slabs + 4) + ends(14, 6),
-        flops=flops // 4,
     )(
         one, two, strip, diagonal, field, x_field, y_field, weights, x_weights, y_weights,
         total, squares,

time: 65.6 us -> 59.5 us (0.907)
  the two profiles are of different devices: /device:TPU:15 before, /device:TPU:0 now
where the time goes in v4:
time: 59.5 us; the launch traced here: 59.3 us
  Pallas kernels  22.3 us (37%)
  waiting for transfers between devices  17.1 us (29%)
  starting transfers between devices  16.2 us (27%)
  local copies, waits for them, and re-layouts  3.14 us (5%)
    pallas_call x7, Pallas kernels, run(): pl.pallas_call(kernel, out_shape=outs, in_specs=[VMEM] * len(args) if ins...  22.3 us
    ppermute x3, waiting for transfers between devices, per_device(): parts.append(lax.ppermute(others[z - 1], 'mode', there).astype(F32))  16.3 us
    ppermute x10, starting transfers between devices, flip(): return lax.ppermute(values, 'mode', [(i, i ^ mask) for i in range(count)])  9.82 us
    ppermute x1, starting transfers between devices, per_device(): strip = lax.ppermute(strip, 'mode', pairs_of)  3.65 us
    unnamed x10, local copies, waits for them, and re-layouts  3 us
    ppermute x3, starting transfers between devices, per_device(): parts.append(lax.ppermute(others[z - 1], 'mode', there).astype(F32))  2.76 us
  transfers between devices with their start and end apart: 14, of which 4 were waited for; matrix products, arithmetic and copies ran while one was open for 0% of the time, Pallas kernels for 23%

profile of v4, /device:TPU:0, one launch (start us, length us, event | category | flops | bytes accessed | tf_op | source)
XLA Modules:
  0.0 59.3 jit_solution(6669423162234848039)
XLA Ops:
  0.0 0.5 collective-permute-start.2
  0.5 2.5 %collective-permute-start.1 = (bf16[384,512]{1,0:T(8,128)(2,1)}, bf16[384,512]{1,0:T(8,128)(2,1)S(1)}, u32[]{:S(2)}, u32[]{:S(2)}) collective-permute-start(bf16[384,512]{1,0:T(8,128)(2,1)} %refs_0_.3), channel_id=1, source_target_pairs={{0,4},{1,5},{2,6},{3,7},{4,0},{5,1},{6,2},{7,3},{8,12},{9,13},{10,... | collective-permute-start | bytes 1179656 | tf_op jit(solution)/shard_map/ppermute | solution.py:47
  3.0 1.5 %collective-permute-start = (bf16[384,512]{1,0:T(8,128)(2,1)}, bf16[384,512]{1,0:T(8,128)(2,1)S(1)}, u32[]{:S(2)}, u32[]{:S(2)}) collective-permute-start(bf16[384,512]{1,0:T(8,128)(2,1)} %refs_0_.3), channel_id=1, source_target_pairs={{0,2},{1,3},{2,0},{3,1},{4,6},{5,7},{6,4},{7,5},{8,10},{9,11},{10,... | collective-permute-start | bytes 1179656 | tf_op jit(solution)/shard_map/ppermute | solution.py:47
  4.5 0.0 collective-permute-done.2.refs_2_.refs_1_
  4.5 0.0 copy-start.2
  4.5 0.7 %copy-done.2 = s32[9,6]{0,1:T(8,128)S(1)} copy-done((s32[9,6]{0,1:T(8,128)S(1)}, s32[9,6]{0,1:T(8,128)}, u32[]{:S(2)}) %copy-start.2) | copy-done | bytes 240
  5.2 0.0 copy-start.3
  5.2 0.7 %copy-done.3 = s32[4]{0:T(128)S(1)} copy-done((s32[4]{0:T(128)S(1)}, s32[4]{0:T(128)}, u32[]{:S(2)}) %copy-start.3) | copy-done | bytes 40
  5.8 0.0 copy-start.4
  5.8 0.7 %copy-done.4 = f32[8]{0:T(128)S(1)} copy-done((f32[8]{0:T(128)S(1)}, f32[8]{0:T(128)}, u32[]{:S(2)}) %copy-start.4) | copy-done | bytes 56
  6.5 0.7 %shard_map.46.refs_1_ = bf16[32,512]{1,0:T(8,128)(2,1)S(1)} custom-call(s32[4]{0:T(128)S(1)} %copy-done.3, s32[6,9]{1,0:T(8,128)S(1)} %bitcast.8, f32[8]{0:T(128)S(1)} %copy-done.4), custom_call_target="tpu_custom_call" | custom-call | tf_op jit(solution)/shard_map/pallas_call | solution.py:23
  7.2 0.1 collective-permute-start.5
  7.2 0.6 collective-permute-start.4
  7.8 1.5 %collective-permute-start.3 = (bf16[32,512]{1,0:T(8,128)(2,1)S(1)}, bf16[32,512]{1,0:T(8,128)(2,1)S(1)}, u32[]{:S(2)}, u32[]{:S(2)}) collective-permute-start(bf16[32,512]{1,0:T(8,128)(2,1)S(1)} %shard_map.46.refs_1_), channel_id=1, source_target_pairs={{0,2},{1,3},{2,0},{3,1},{4,6},{5,7},{6,4},{7,5},{8,10},{9,11},{10,... | collective-permute-start | bytes 98312 | tf_op jit(solution)/shard_map/ppermute | solution.py:47
  9.3 0.0 collective-permute-done.5.refs_3_
  9.3 0.0 copy-start
  9.3 1.0 %copy-done = bf16[384,512]{1,0:T(8,128)(2,1)S(1)} copy-done((bf16[384,512]{1,0:T(8,128)(2,1)S(1)}, bf16[384,512]{1,0:T(8,128)(2,1)}, u32[]{:S(2)}) %copy-start) | copy-done | bytes 393240
  10.3 4.0 %shard_map.47 = (bf16[8,432,128]{2,1,0:T(8,128)(2,1)S(1)}, bf16[8,32,128]{2,1,0:T(8,128)(2,1)S(1)}, f32[1008,384]{1,0:T(8,128)S(1)}, f32[6,8,128]{2,1,0:T(8,128)S(1)}) custom-call(bf16[384,512]{1,0:T(8,128)(2,1)S(1)} %copy-done, bf16[32,512]{1,0:T(8,128)(2,1)S(1)} %shard_map.46.refs_1_, bf16[384,512]{1,0:T(8,128)(2,1)S(1)} %collective-permute-done.2.refs_2_.refs_1_, ...), custom_call_target="tpu_custom_call" | custom-call | tf_op jit(solution)/shard_map/pallas_call | solution.py:23
  14.3 0.0 copy-start.1
  14.3 0.0 collective-permute-done.1.refs_3_.refs_0_
  14.3 0.4 collective-permute-done.refs_2_.refs_0_
  14.8 0.0 collective-permute-done.4.refs_1_
  14.8 0.3 collective-permute-done.3.refs_1_
  15.1 0.1 pad_maximum_fusion
  15.2 0.1 collective-permute-start.9
  15.3 1.6 %collective-permute-start.7 = (bf16[208,512]{1,0:T(8,128)(2,1)S(1)}, bf16[208,512]{1,0:T(8,128)(2,1)S(1)}, u32[]{:S(2)}, u32[]{:S(2)}) collective-permute-start(bf16[208,512]{1,0:T(8,128)(2,1)S(1)} %slice.16), channel_id=1, source_target_pairs={{0,2},{1,3},{2,0},{3,1},{4,6},{5,7},{6,4},{7,5},{8,10},{9,11},{10,... | collective-permute-start | bytes 638984 | tf_op jit(solution)/shard_map/ppermute | solution.py:47
  16.9 0.5 collective-permute-start.6
  17.4 0.0 copy-done.1
  17.5 3.7 %collective-permute-start.8 = (bf16[96,512]{1,0:T(8,128)(2,1)S(1)}, bf16[96,512]{1,0:T(8,128)(2,1)S(1)}, u32[]{:S(2)}, u32[]{:S(2)}) collective-permute-start(bf16[96,512]{1,0:T(8,128)(2,1)S(1)} %shard_map.48), channel_id=1, source_target_pairs={{0,24},{1,30},{2,26},{3,11},{4,28},{5,13},{6,9},{7,15},{8,0},{9,6}... | collective-permute-start | bytes 294920 | tf_op jit(solution)/shard_map/ppermute | solution.py:469
  21.1 0.0 collective-permute-done.9.refs_2_
  21.1 5.1 %shard_map.49 = (bf16[8,432,128]{2,1,0:T(8,128)(2,1)S(1)}, bf16[8,32,128]{2,1,0:T(8,128)(2,1)S(1)}, f32[1008,384]{1,0:T(8,128)S(1)}, f32[6,8,128]{2,1,0:T(8,128)S(1)}) custom-call(bf16[384,512]{1,0:T(8,128)(2,1)S(1)} %collective-permute-done.refs_2_.refs_0_, bf16[32,512]{1,0:T(8,128)(2,1)S(1)} %collective-permute-done.3.refs_1_, ...), custom_call_target="tpu_custom_call" | custom-call | tf_op jit(solution)/shard_map/pallas_call | solution.py:23
  26.2 0.0 collective-permute-done.8.refs_2_
  26.2 0.0 collective-permute-done.7.refs_1_
  26.2 0.0 collective-permute-done.6.refs_0_
  26.3 1.1 %collective-permute-start.10 = (bf16[512,512]{1,0:T(8,128)(2,1)S(1)}, bf16[512,512]{1,0:T(8,128)(2,1)S(1)}, u32[]{:S(2)}, u32[]{:S(2)}) collective-permute-start(bf16[512,512]{1,0:T(8,128)(2,1)S(1)} %pad_maximum_fusion.1), channel_id=1, source_target_pairs={{0,1},{1,0},{2,3},{3,2},{4,5},{5,4},{6,7},{7,6},{8,9},{9,8},{10,11... | collective-permute-start | bytes 1572872 | tf_op jit(solution)/shard_map/ppermute | solution.py:47
  27.4 4.0 %shard_map.50 = (bf16[8,432,128]{2,1,0:T(8,128)(2,1)S(1)}, bf16[8,32,128]{2,1,0:T(8,128)(2,1)S(1)}, f32[1008,384]{1,0:T(8,128)S(1)}, f32[6,8,128]{2,1,0:T(8,128)S(1)}) custom-call(bf16[384,512]{1,0:T(8,128)(2,1)S(1)} %collective-permute-done.1.refs_3_.refs_0_, bf16[32,512]{1,0:T(8,128)(2,1)S(1)} %collective-permute-done.4.refs_1_, ...), custom_call_target="tpu_custom_call" | custom-call | tf_op jit(solution)/shard_map/pallas_call | solution.py:23
  31.4 0.0 collective-permute-done.10.refs_3_
  31.4 7.3 %shard_map.51 = (f32[256,384]{1,0:T(8,128)S(1)}, f32[3,256,384]{2,1,0:T(8,128)S(1)}, f32[8,128]{1,0:T(8,128)S(1)}) custom-call(bf16[208,512]{1,0:T(8,128)(2,1)S(1)} %collective-permute-done.6.refs_0_, bf16[208,512]{1,0:T(8,128)(2,1)S(1)} %collective-permute-done.7.refs_1_, bf16[96,512]{1,0:T(8,128)(2,1)S(1)} %collective-permute-done.8.refs_2_, ...), custom_call_target="tpu_custom_call" | custom-call | tf_op jit(solution)/shard_map/pallas_call | solution.py:23
  38.7 0.1 convert_element_type.12
  38.8 0.1 slice_bitcast_fusion
  39.0 1.7 %collective-permute-start.13 = (f16[256,384]{1,0:T(8,128)(2,1)S(1)}, f16[256,384]{1,0:T(8,128)(2,1)S(1)}, u32[]{:S(2)}, u32[]{:S(2)}) collective-permute-start(f16[256,384]{1,0:T(8,128)(2,1)S(1)} %get-tuple-element.61), channel_id=1, source_target_pairs={{0,24},{1,25},{2,26},{3,27},{4,28},{5,29},{6,30},{7,31},{8,0},{9,1... | collective-permute-start | bytes 589832 | tf_op jit(solution)/shard_map/ppermute | solution.py:497
  40.7 0.0 collective-permute-start.12
  40.7 1.0 %collective-permute-start.11 = (f16[256,384]{1,0:T(8,128)(2,1)S(1)}, f16[256,384]{1,0:T(8,128)(2,1)S(1)}, u32[]{:S(2)}, u32[]{:S(2)}) collective-permute-start(f16[256,384]{1,0:T(8,128)(2,1)S(1)} %get-tuple-element.63), channel_id=1, source_target_pairs={{0,8},{1,9},{2,10},{3,11},{4,12},{5,13},{6,14},{7,15},{8,16},{9,17... | collective-permute-start | bytes 589832 | tf_op jit(solution)/shard_map/ppermute | solution.py:497
  41.7 5.3 %collective-permute-done.13 = f16[256,384]{1,0:T(8,128)(2,1)S(1)} collective-permute-done((f16[256,384]{1,0:T(8,128)(2,1)S(1)}, f16[256,384]{1,0:T(8,128)(2,1)S(1)}, u32[]{:S(2)}, u32[]{:S(2)}) %collective-permute-start.13) | collective-permute-done | bytes 196640 | tf_op jit(solution)/shard_map/ppermute | solution.py:497
  47.0 11.1 %collective-permute-done.12 = f16[256,384]{1,0:T(8,128)(2,1)S(1)} collective-permute-done((f16[256,384]{1,0:T(8,128)(2,1)S(1)}, f16[256,384]{1,0:T(8,128)(2,1)S(1)}, u32[]{:S(2)}, u32[]{:S(2)}) %collective-permute-start.12) | collective-permute-done | bytes 196640 | tf_op jit(solution)/shard_map/ppermute | solution.py:497
  58.1 0.0 collective-permute-done.11
  58.1 1.2 %shard_map.52 = f32[12,21,384]{2,1,0:T(8,128)} custom-call(f32[256,384]{1,0:T(8,128)S(1)} %get-tuple-element.58.refs_0_, f32[256,384]{1,0:T(8,128)S(1)} %convert_element_type.13.refs_1_, f32[256,384]{1,0:T(8,128)S(1)} %convert_element_type.14.refs_2_, f32[256,384]{1,0:T(8,128)S(1)} %convert_element_type.15.refs_3_, f32[8,128]{1,0:T(8,128)S(1)} %get-tuple-element.60.refs_4_), custom_call_target="tpu_custom_call" | custom-call | tf_op jit(solution)/shard_map/pallas_call | solution.py:23
  (8 shorter events, 0.2 us)
Async XLA Ops:
  0.0 4.5 %collective-permute-start.2 = (bf16[384,512]{1,0:T(8,128)(2,1)}, bf16[384,512]{1,0:T(8,128)(2,1)S(1)}, u32[]{:S(2)}, u32[]{:S(2)}) collective-permute-start(bf16[384,512]{1,0:T(8,128)(2,1)} %refs_0_.3), channel_id=1, source_target_pairs={{0,1},{1,0},{2,3},{3,2},{4,5},{5,4},{6,7},{7,6},{8,9},{9,8},{10,11... | collective-permute-start | bytes 1179656 | tf_op jit(solution)/shard_map/ppermute | solution.py:47
  0.5 13.9 %collective-permute-start.1 = (bf16[384,512]{1,0:T(8,128)(2,1)}, bf16[384,512]{1,0:T(8,128)(2,1)S(1)}, u32[]{:S(2)}, u32[]{:S(2)}) collective-permute-start(bf16[384,512]{1,0:T(8,128)(2,1)} %refs_0_.3), channel_id=1, source_target_pairs={{0,4},{1,5},{2,6},{3,7},{4,0},{5,1},{6,2},{7,3},{8,12},{9,13},{10,... | collective-permute-start | bytes 1179656 | tf_op jit(solution)/shard_map/ppermute | solution.py:47
  3.0 11.8 %collective-permute-start = (bf16[384,512]{1,0:T(8,128)(2,1)}, bf16[384,512]{1,0:T(8,128)(2,1)S(1)}, u32[]{:S(2)}, u32[]{:S(2)}) collective-permute-start(bf16[384,512]{1,0:T(8,128)(2,1)} %refs_0_.3), channel_id=1, source_target_pairs={{0,2},{1,3},{2,0},{3,1},{4,6},{5,7},{6,4},{7,5},{8,10},{9,11},{10,... | collective-permute-start | bytes 1179656 | tf_op jit(solution)/shard_map/ppermute | solution.py:47
  4.5 0.7 %copy-start.2 = (s32[9,6]{0,1:T(8,128)S(1)}, s32[9,6]{0,1:T(8,128)}, u32[]{:S(2)}) copy-start(s32[9,6]{0,1:T(8,128)} %param.6) | copy-start | bytes 652
  5.2 0.7 %copy-start.3 = (s32[4]{0:T(128)S(1)}, s32[4]{0:T(128)}, u32[]{:S(2)}) copy-start(s32[4]{0:T(128)} %region) | copy-start | bytes 52
  5.8 0.7 %copy-start.4 = (f32[8]{0:T(128)S(1)}, f32[8]{0:T(128)}, u32[]{:S(2)}) copy-start(f32[8]{0:T(128)} %table.1) | copy-start | bytes 100
  7.2 2.1 %collective-permute-start.5 = (bf16[32,512]{1,0:T(8,128)(2,1)S(1)}, bf16[32,512]{1,0:T(8,128)(2,1)S(1)}, u32[]{:S(2)}, u32[]{:S(2)}) collective-permute-start(bf16[32,512]{1,0:T(8,128)(2,1)S(1)} %shard_map.46.refs_1_), channel_id=1, source_target_pairs={{0,1},{1,0},{2,3},{3,2},{4,5},{5,4},{6,7},{7,6},{8,9},{9,8},{10,11... | collective-permute-start | bytes 98312 | tf_op jit(solution)/shard_map/ppermute | solution.py:47
  7.2 7.5 %collective-permute-start.4 = (bf16[32,512]{1,0:T(8,128)(2,1)S(1)}, bf16[32,512]{1,0:T(8,128)(2,1)S(1)}, u32[]{:S(2)}, u32[]{:S(2)}) collective-permute-start(bf16[32,512]{1,0:T(8,128)(2,1)S(1)} %shard_map.46.refs_1_), channel_id=1, source_target_pairs={{0,4},{1,5},{2,6},{3,7},{4,0},{5,1},{6,2},{7,3},{8,12},{9,13},{10,... | collective-permute-start | bytes 98312 | tf_op jit(solution)/shard_map/ppermute | solution.py:47
  7.8 7.3 %collective-permute-start.3 = (bf16[32,512]{1,0:T(8,128)(2,1)S(1)}, bf16[32,512]{1,0:T(8,128)(2,1)S(1)}, u32[]{:S(2)}, u32[]{:S(2)}) collective-permute-start(bf16[32,512]{1,0:T(8,128)(2,1)S(1)} %shard_map.46.refs_1_), channel_id=1, source_target_pairs={{0,2},{1,3},{2,0},{3,1},{4,6},{5,7},{6,4},{7,5},{8,10},{9,11},{10,... | collective-permute-start | bytes 98312 | tf_op jit(solution)/shard_map/ppermute | solution.py:47
  9.3 1.0 %copy-start = (bf16[384,512]{1,0:T(8,128)(2,1)S(1)}, bf16[384,512]{1,0:T(8,128)(2,1)}, u32[]{:S(2)}) copy-start(bf16[384,512]{1,0:T(8,128)(2,1)} %refs_0_.3) | copy-start | bytes 1179652
  14.3 3.1 %copy-start.1 = (bf16[384,512]{1,0:T(8,128)(2,1)S(1)}, bf16[384,512]{1,0:T(8,128)(2,1)}, u32[]{:S(2)}) copy-start(bf16[384,512]{1,0:T(8,128)(2,1)} %refs_0_.3) | copy-start | bytes 1179652
  15.2 5.9 %collective-permute-start.9 = (bf16[832,512]{1,0:T(8,128)(2,1)S(1)}, bf16[832,512]{1,0:T(8,128)(2,1)S(1)}, u32[]{:S(2)}, u32[]{:S(2)}) collective-permute-start(bf16[832,512]{1,0:T(8,128)(2,1)S(1)} %pad_maximum_fusion), channel_id=1, source_target_pairs={{0,1},{1,0},{2,3},{3,2},{4,5},{5,4},{6,7},{7,6},{8,9},{9,8},{10,11... | collective-permute-start | bytes 2555912 | tf_op jit(solution)/shard_map/ppermute | solution.py:47
  15.3 10.9 %collective-permute-start.7 = (bf16[208,512]{1,0:T(8,128)(2,1)S(1)}, bf16[208,512]{1,0:T(8,128)(2,1)S(1)}, u32[]{:S(2)}, u32[]{:S(2)}) collective-permute-start(bf16[208,512]{1,0:T(8,128)(2,1)S(1)} %slice.16), channel_id=1, source_target_pairs={{0,2},{1,3},{2,0},{3,1},{4,6},{5,7},{6,4},{7,5},{8,10},{9,11},{10,... | collective-permute-start | bytes 638984 | tf_op jit(solution)/shard_map/ppermute | solution.py:47
  16.9 9.3 %collective-permute-start.6 = (bf16[208,512]{1,0:T(8,128)(2,1)S(1)}, bf16[208,512]{1,0:T(8,128)(2,1)S(1)}, u32[]{:S(2)}, u32[]{:S(2)}) collective-permute-start(bf16[208,512]{1,0:T(8,128)(2,1)S(1)} %pad_maximum_fusion.2), channel_id=1, source_target_pairs={{0,4},{1,5},{2,6},{3,7},{4,0},{5,1},{6,2},{7,3},{8,12},{9,13},{10,... | collective-permute-start | bytes 638984 | tf_op jit(solution)/shard_map/ppermute | solution.py:47
  17.5 8.7 %collective-permute-start.8 = (bf16[96,512]{1,0:T(8,128)(2,1)S(1)}, bf16[96,512]{1,0:T(8,128)(2,1)S(1)}, u32[]{:S(2)}, u32[]{:S(2)}) collective-permute-start(bf16[96,512]{1,0:T(8,128)(2,1)S(1)} %shard_map.48), channel_id=1, source_target_pairs={{0,24},{1,30},{2,26},{3,11},{4,28},{5,13},{6,9},{7,15},{8,0},{9,6}... | collective-permute-start | bytes 294920 | tf_op jit(solution)/shard_map/ppermute | solution.py:469
  26.3 5.1 %collective-permute-start.10 = (bf16[512,512]{1,0:T(8,128)(2,1)S(1)}, bf16[512,512]{1,0:T(8,128)(2,1)S(1)}, u32[]{:S(2)}, u32[]{:S(2)}) collective-permute-start(bf16[512,512]{1,0:T(8,128)(2,1)S(1)} %pad_maximum_fusion.1), channel_id=1, source_target_pairs={{0,1},{1,0},{2,3},{3,2},{4,5},{5,4},{6,7},{7,6},{8,9},{9,8},{10,11... | collective-permute-start | bytes 1572872 | tf_op jit(solution)/shard_map/ppermute | solution.py:47
  39.0 8.0 %collective-permute-start.13 = (f16[256,384]{1,0:T(8,128)(2,1)S(1)}, f16[256,384]{1,0:T(8,128)(2,1)S(1)}, u32[]{:S(2)}, u32[]{:S(2)}) collective-permute-start(f16[256,384]{1,0:T(8,128)(2,1)S(1)} %get-tuple-element.61), channel_id=1, source_target_pairs={{0,24},{1,25},{2,26},{3,27},{4,28},{5,29},{6,30},{7,31},{8,0},{9,1... | collective-permute-start | bytes 589832 | tf_op jit(solution)/shard_map/ppermute | solution.py:497
  40.7 17.4 %collective-permute-start.12 = (f16[256,384]{1,0:T(8,128)(2,1)S(1)}, f16[256,384]{1,0:T(8,128)(2,1)S(1)}, u32[]{:S(2)}, u32[]{:S(2)}) collective-permute-start(f16[256,384]{1,0:T(8,128)(2,1)S(1)} %get-tuple-element.62), channel_id=1, source_target_pairs={{0,16},{1,17},{2,18},{3,19},{4,20},{5,21},{6,22},{7,23},{8,24},{9,... | collective-permute-start | bytes 589832 | tf_op jit(solution)/shard_map/ppermute | solution.py:497
  40.7 17.4 %collective-permute-start.11 = (f16[256,384]{1,0:T(8,128)(2,1)S(1)}, f16[256,384]{1,0:T(8,128)(2,1)S(1)}, u32[]{:S(2)}, u32[]{:S(2)}) collective-permute-start(f16[256,384]{1,0:T(8,128)(2,1)S(1)} %get-tuple-element.63), channel_id=1, source_target_pairs={{0,8},{1,9},{2,10},{3,11},{4,12},{5,13},{6,14},{7,15},{8,16},{9,17... | collective-permute-start | bytes 589832 | tf_op jit(solution)/shard_map/ppermute | solution.py:497

commit v5 on v4

--- a/solution.py
+++ b/solution.py
@@ -111,11 +111,12 @@
     return jnp.concatenate([2.0 * same - beside, same - mirror], axis=1).astype(BF16)
 
 
-def act(triples, stencil, side, right, left, squares, base, rows, terms):
+def act(triples, stencil, sides, right, left, squares, base, rows, terms):
     total, width = triples[0][1].shape
     own = total - rows
     for n, (before, here, after, weight) in enumerate(triples):
-        lanes = pl.ds(base + n * width, width)
+        lanes = slice(base + n * width, base + (n + 1) * width)
+        side = sides.at[n % 2]
         side[...] = jnp.dot(here[...], stencil, preferred_element_type=F32)
         table = weight[...].astype(F32)
         kappas = []
@@ -173,6 +174,8 @@
     for flipped, (table, *parts) in enumerate(pieces):
         core = jnp.bitwise_xor(jnp.bitwise_and(j, 1), flipped)
         slabs = table.shape[1] // width
+        block = jnp.concatenate([part[...] for part in parts], axis=0)
+        picked = jnp.dot(pick, block, preferred_element_type=F32).astype(BF16)
         for s in range(slabs):
             lanes = slice(s * width, (s + 1) * width)
             at = core * slabs + s
@@ -182,9 +185,7 @@
                 size = part.shape[0]
                 field[at, done : done + size] = part[:, lanes]
                 done += size
-            field[at, rows:] = jnp.dot(
-                pick, field[at, 0:rows], preferred_element_type=F32
-            ).astype(BF16)
+            field[at, rows:] = picked[:, lanes]
 
 
 def split(ref, start, rows):
@@ -192,23 +193,11 @@
 
 
 def inner(field, weights, stencil, side, right, left, squares, base, rows, terms):
-    slabs, _, width = field.shape
-
-    @pl.loop(0, (slabs - 2) // 2)
-    def _(t):
-        s = 2 * t + 1
-        triples = [
-            (field.at[s + n - 1], field.at[s + n], field.at[s + n + 1], weights.at[s + n])
-            for n in range(2)
-        ]
-        start = pl.multiple_of(base + 2 * t * width, width)
-        act(triples, stencil, side, right, left, squares, start, rows, terms)
-
-
-def pick_into(ends, at, field, slot, taken):
-    @pl.when(taken)
-    def _():
-        ends[at] = field[slot]
+    triples = [
+        (field.at[s - 1], field.at[s], field.at[s + 1], weights.at[s])
+        for s in range(1, field.shape[0] - 1)
+    ]
+    act(triples, stencil, side, right, left, squares, base, rows, terms)
 
 
 def seam(ours, theirs, ends, seam_weights, field_weights, mine_first):
@@ -428,7 +417,7 @@
 
     def scratch(number):
         return [
-            pltpu.VMEM((every, 2 * width), F32),
+            pltpu.VMEM((2, every, 2 * width), F32),
             pltpu.VMEM((terms, rows, number * width), BF16),
             pltpu.VMEM((terms * lines, number * width), BF16),
         ]

time: 59.5 us -> 57.4 us (0.965)
  Pallas kernels: 22.3 us -> 18 us
  waiting for transfers between devices: 17.1 us -> 18.5 us
  starting transfers between devices: 16.2 us -> 17 us
    pallas_call x7, Pallas kernels: 22.3 us -> 18 us  [run(): pl.pallas_call(kernel, out_shape=outs, in_specs=[VMEM] * len(args) if ins...]
    ppermute x10, waiting for transfers between devices: 0.81 us -> 2.2 us  [flip(): return lax.ppermute(values, 'mode', [(i, i ^ mask) for i in range(count)])]
    ppermute x3, starting transfers between devices: 2.76 us -> 3.52 us  [per_device(): parts.append(lax.ppermute(others[z - 1], 'mode', there).astype(F32))]
  transfers between devices with their start and end apart: 14 -> 14, of which waited for: 4 -> 5; matrix products, arithmetic and copies ran while one was open for 0% -> 0% of each run, Pallas kernels for 23% -> 18%
where the time goes in v5:
time: 57.4 us; the launch traced here: 57.2 us
  waiting for transfers between devices  18.5 us (32%)
  Pallas kernels  18 us (31%)
  starting transfers between devices  17 us (30%)
  local copies, waits for them, and re-layouts  3.14 us (5%)
    pallas_call x7, Pallas kernels, run(): pl.pallas_call(kernel, out_shape=outs, in_specs=[VMEM] * len(args) if ins...  18 us
    ppermute x3, waiting for transfers between devices, per_device(): parts.append(lax.ppermute(others[z - 1], 'mode', there).astype(F32))  16.3 us
    ppermute x10, starting transfers between devices, flip(): return lax.ppermute(values, 'mode', [(i, i ^ mask) for i in range(count)])  9.84 us
    ppermute x1, starting transfers between devices, per_device(): strip = lax.ppermute(strip, 'mode', pairs_of)  3.65 us
    ppermute x3, starting transfers between devices, per_device(): parts.append(lax.ppermute(others[z - 1], 'mode', there).astype(F32))  3.52 us
    unnamed x10, local copies, waits for them, and re-layouts  3 us
    ppermute x10, waiting for transfers between devices, flip(): return lax.ppermute(values, 'mode', [(i, i ^ mask) for i in range(count)])  2.2 us
  transfers between devices with their start and end apart: 14, of which 5 were waited for; matrix products, arithmetic and copies ran while one was open for 0% of the time, Pallas kernels for 18%

profile of v5, /device:TPU:0, one launch (start us, length us, event | category | flops | bytes accessed | tf_op | source)
XLA Modules:
  0.0 57.2 jit_solution(12655050405108096026)
XLA Ops:
  0.0 0.5 collective-permute-start.2
  0.5 2.5 %collective-permute-start.1 = (bf16[384,512]{1,0:T(8,128)(2,1)}, bf16[384,512]{1,0:T(8,128)(2,1)S(1)}, u32[]{:S(2)}, u32[]{:S(2)}) collective-permute-start(bf16[384,512]{1,0:T(8,128)(2,1)} %refs_0_.3), channel_id=1, source_target_pairs={{0,4},{1,5},{2,6},{3,7},{4,0},{5,1},{6,2},{7,3},{8,12},{9,13},{10,... | collective-permute-start | bytes 1179656 | tf_op jit(solution)/shard_map/ppermute | solution.py:47
  3.0 1.5 %collective-permute-start = (bf16[384,512]{1,0:T(8,128)(2,1)}, bf16[384,512]{1,0:T(8,128)(2,1)S(1)}, u32[]{:S(2)}, u32[]{:S(2)}) collective-permute-start(bf16[384,512]{1,0:T(8,128)(2,1)} %refs_0_.3), channel_id=1, source_target_pairs={{0,2},{1,3},{2,0},{3,1},{4,6},{5,7},{6,4},{7,5},{8,10},{9,11},{10,... | collective-permute-start | bytes 1179656 | tf_op jit(solution)/shard_map/ppermute | solution.py:47
  4.5 0.0 collective-permute-done.2.refs_2_.refs_1_
  4.5 0.0 copy-start.2
  4.5 0.7 %copy-done.2 = s32[9,6]{0,1:T(8,128)S(1)} copy-done((s32[9,6]{0,1:T(8,128)S(1)}, s32[9,6]{0,1:T(8,128)}, u32[]{:S(2)}) %copy-start.2) | copy-done | bytes 240
  5.2 0.0 copy-start.3
  5.2 0.7 %copy-done.3 = s32[4]{0:T(128)S(1)} copy-done((s32[4]{0:T(128)S(1)}, s32[4]{0:T(128)}, u32[]{:S(2)}) %copy-start.3) | copy-done | bytes 40
  5.8 0.0 copy-start.4
  5.8 0.7 %copy-done.4 = f32[8]{0:T(128)S(1)} copy-done((f32[8]{0:T(128)S(1)}, f32[8]{0:T(128)}, u32[]{:S(2)}) %copy-start.4) | copy-done | bytes 56
  6.5 0.7 %shard_map.46.refs_1_ = bf16[32,512]{1,0:T(8,128)(2,1)S(1)} custom-call(s32[4]{0:T(128)S(1)} %copy-done.3, s32[6,9]{1,0:T(8,128)S(1)} %bitcast.8, f32[8]{0:T(128)S(1)} %copy-done.4), custom_call_target="tpu_custom_call" | custom-call | tf_op jit(solution)/shard_map/pallas_call | solution.py:23
  7.2 0.1 collective-permute-start.5
  7.2 0.6 %collective-permute-start.4 = (bf16[32,512]{1,0:T(8,128)(2,1)S(1)}, bf16[32,512]{1,0:T(8,128)(2,1)S(1)}, u32[]{:S(2)}, u32[]{:S(2)}) collective-permute-start(bf16[32,512]{1,0:T(8,128)(2,1)S(1)} %shard_map.46.refs_1_), channel_id=1, source_target_pairs={{0,4},{1,5},{2,6},{3,7},{4,0},{5,1},{6,2},{7,3},{8,12},{9,13},{10,... | collective-permute-start | bytes 98312 | tf_op jit(solution)/shard_map/ppermute | solution.py:47
  7.8 1.5 %collective-permute-start.3 = (bf16[32,512]{1,0:T(8,128)(2,1)S(1)}, bf16[32,512]{1,0:T(8,128)(2,1)S(1)}, u32[]{:S(2)}, u32[]{:S(2)}) collective-permute-start(bf16[32,512]{1,0:T(8,128)(2,1)S(1)} %shard_map.46.refs_1_), channel_id=1, source_target_pairs={{0,2},{1,3},{2,0},{3,1},{4,6},{5,7},{6,4},{7,5},{8,10},{9,11},{10,... | collective-permute-start | bytes 98312 | tf_op jit(solution)/shard_map/ppermute | solution.py:47
  9.3 0.0 collective-permute-done.5.refs_3_
  9.3 0.0 copy-start
  9.3 1.0 %copy-done = bf16[384,512]{1,0:T(8,128)(2,1)S(1)} copy-done((bf16[384,512]{1,0:T(8,128)(2,1)S(1)}, bf16[384,512]{1,0:T(8,128)(2,1)}, u32[]{:S(2)}) %copy-start) | copy-done | bytes 393240
  10.3 2.6 %shard_map.47 = (bf16[8,432,128]{2,1,0:T(8,128)(2,1)S(1)}, bf16[8,32,128]{2,1,0:T(8,128)(2,1)S(1)}, f32[1008,384]{1,0:T(8,128)S(1)}, f32[6,8,128]{2,1,0:T(8,128)S(1)}) custom-call(bf16[384,512]{1,0:T(8,128)(2,1)S(1)} %copy-done, bf16[32,512]{1,0:T(8,128)(2,1)S(1)} %shard_map.46.refs_1_, bf16[384,512]{1,0:T(8,128)(2,1)S(1)} %collective-permute-done.2.refs_2_.refs_1_, ...), custom_call_target="tpu_custom_call" | custom-call | tf_op jit(solution)/shard_map/pallas_call | solution.py:23
  12.9 0.0 copy-start.1
  12.9 0.2 collective-permute-done.1.refs_3_.refs_0_
  13.1 1.6 %collective-permute-done.refs_2_.refs_0_ = bf16[384,512]{1,0:T(8,128)(2,1)S(1)} collective-permute-done((bf16[384,512]{1,0:T(8,128)(2,1)}, bf16[384,512]{1,0:T(8,128)(2,1)S(1)}, u32[]{:S(2)}, u32[]{:S(2)}) %collective-permute-start) | collective-permute-done | bytes 393248 | tf_op jit(solution)/shard_map/ppermute | solution.py:47
  14.8 0.0 collective-permute-done.4.refs_1_
  14.8 0.3 collective-permute-done.3.refs_1_
  15.1 0.1 pad_maximum_fusion
  15.2 0.1 collective-permute-start.9
  15.3 1.6 %collective-permute-start.7 = (bf16[208,512]{1,0:T(8,128)(2,1)S(1)}, bf16[208,512]{1,0:T(8,128)(2,1)S(1)}, u32[]{:S(2)}, u32[]{:S(2)}) collective-permute-start(bf16[208,512]{1,0:T(8,128)(2,1)S(1)} %slice.16), channel_id=1, source_target_pairs={{0,2},{1,3},{2,0},{3,1},{4,6},{5,7},{6,4},{7,5},{8,10},{9,11},{10,... | collective-permute-start | bytes 638984 | tf_op jit(solution)/shard_map/ppermute | solution.py:47
  16.9 0.5 collective-permute-start.6
  17.4 0.0 copy-done.1
  17.5 3.7 %collective-permute-start.8 = (bf16[96,512]{1,0:T(8,128)(2,1)S(1)}, bf16[96,512]{1,0:T(8,128)(2,1)S(1)}, u32[]{:S(2)}, u32[]{:S(2)}) collective-permute-start(bf16[96,512]{1,0:T(8,128)(2,1)S(1)} %shard_map.48), channel_id=1, source_target_pairs={{0,24},{1,30},{2,26},{3,11},{4,28},{5,13},{6,9},{7,15},{8,0},{9,6}... | collective-permute-start | bytes 294920 | tf_op jit(solution)/shard_map/ppermute | solution.py:458
  21.1 0.0 collective-permute-done.9.refs_2_
  21.1 4.3 %shard_map.49 = (bf16[8,432,128]{2,1,0:T(8,128)(2,1)S(1)}, bf16[8,32,128]{2,1,0:T(8,128)(2,1)S(1)}, f32[1008,384]{1,0:T(8,128)S(1)}, f32[6,8,128]{2,1,0:T(8,128)S(1)}) custom-call(bf16[384,512]{1,0:T(8,128)(2,1)S(1)} %collective-permute-done.refs_2_.refs_0_, bf16[32,512]{1,0:T(8,128)(2,1)S(1)} %collective-permute-done.3.refs_1_, ...), custom_call_target="tpu_custom_call" | custom-call | tf_op jit(solution)/shard_map/pallas_call | solution.py:23
  25.4 0.0 collective-permute-done.8.refs_2_
  25.4 0.0 collective-permute-done.7.refs_1_
  25.4 0.0 collective-permute-done.6.refs_0_
  25.5 1.1 %collective-permute-start.10 = (bf16[512,512]{1,0:T(8,128)(2,1)S(1)}, bf16[512,512]{1,0:T(8,128)(2,1)S(1)}, u32[]{:S(2)}, u32[]{:S(2)}) collective-permute-start(bf16[512,512]{1,0:T(8,128)(2,1)S(1)} %pad_maximum_fusion.1), channel_id=1, source_target_pairs={{0,1},{1,0},{2,3},{3,2},{4,5},{5,4},{6,7},{7,6},{8,9},{9,8},{10,11... | collective-permute-start | bytes 1572872 | tf_op jit(solution)/shard_map/ppermute | solution.py:47
  26.6 2.7 %shard_map.50 = (bf16[8,432,128]{2,1,0:T(8,128)(2,1)S(1)}, bf16[8,32,128]{2,1,0:T(8,128)(2,1)S(1)}, f32[1008,384]{1,0:T(8,128)S(1)}, f32[6,8,128]{2,1,0:T(8,128)S(1)}) custom-call(bf16[384,512]{1,0:T(8,128)(2,1)S(1)} %collective-permute-done.1.refs_3_.refs_0_, bf16[32,512]{1,0:T(8,128)(2,1)S(1)} %collective-permute-done.4.refs_1_, ...), custom_call_target="tpu_custom_call" | custom-call | tf_op jit(solution)/shard_map/pallas_call | solution.py:23
  29.3 0.0 collective-permute-done.10.refs_3_
  29.3 6.5 %shard_map.51 = (f32[256,384]{1,0:T(8,128)S(1)}, f32[3,256,384]{2,1,0:T(8,128)S(1)}, f32[8,128]{1,0:T(8,128)S(1)}) custom-call(bf16[208,512]{1,0:T(8,128)(2,1)S(1)} %collective-permute-done.6.refs_0_, bf16[208,512]{1,0:T(8,128)(2,1)S(1)} %collective-permute-done.7.refs_1_, bf16[96,512]{1,0:T(8,128)(2,1)S(1)} %collective-permute-done.8.refs_2_, ...), custom_call_target="tpu_custom_call" | custom-call | tf_op jit(solution)/shard_map/pallas_call | solution.py:23
  35.8 0.1 convert_element_type.12
  35.9 0.1 slice_bitcast_fusion
  36.1 2.5 %collective-permute-start.13 = (f16[256,384]{1,0:T(8,128)(2,1)S(1)}, f16[256,384]{1,0:T(8,128)(2,1)S(1)}, u32[]{:S(2)}, u32[]{:S(2)}) collective-permute-start(f16[256,384]{1,0:T(8,128)(2,1)S(1)} %get-tuple-element.61), channel_id=1, source_target_pairs={{0,24},{1,25},{2,26},{3,27},{4,28},{5,29},{6,30},{7,31},{8,0},{9,1... | collective-permute-start | bytes 589832 | tf_op jit(solution)/shard_map/ppermute | solution.py:486
  38.6 0.0 collective-permute-start.12
  38.6 1.0 %collective-permute-start.11 = (f16[256,384]{1,0:T(8,128)(2,1)S(1)}, f16[256,384]{1,0:T(8,128)(2,1)S(1)}, u32[]{:S(2)}, u32[]{:S(2)}) collective-permute-start(f16[256,384]{1,0:T(8,128)(2,1)S(1)} %get-tuple-element.63), channel_id=1, source_target_pairs={{0,8},{1,9},{2,10},{3,11},{4,12},{5,13},{6,14},{7,15},{8,16},{9,17... | collective-permute-start | bytes 589832 | tf_op jit(solution)/shard_map/ppermute | solution.py:486
  39.6 4.3 %collective-permute-done.13 = f16[256,384]{1,0:T(8,128)(2,1)S(1)} collective-permute-done((f16[256,384]{1,0:T(8,128)(2,1)S(1)}, f16[256,384]{1,0:T(8,128)(2,1)S(1)}, u32[]{:S(2)}, u32[]{:S(2)}) %collective-permute-start.13) | collective-permute-done | bytes 196640 | tf_op jit(solution)/shard_map/ppermute | solution.py:486
  43.9 12.0 %collective-permute-done.12 = f16[256,384]{1,0:T(8,128)(2,1)S(1)} collective-permute-done((f16[256,384]{1,0:T(8,128)(2,1)S(1)}, f16[256,384]{1,0:T(8,128)(2,1)S(1)}, u32[]{:S(2)}, u32[]{:S(2)}) %collective-permute-start.12) | collective-permute-done | bytes 196640 | tf_op jit(solution)/shard_map/ppermute | solution.py:486
  55.9 0.0 collective-permute-done.11
  56.0 1.2 %shard_map.52 = f32[12,21,384]{2,1,0:T(8,128)} custom-call(f32[256,384]{1,0:T(8,128)S(1)} %get-tuple-element.58.refs_0_, f32[256,384]{1,0:T(8,128)S(1)} %convert_element_type.13.refs_1_, f32[256,384]{1,0:T(8,128)S(1)} %convert_element_type.14.refs_2_, f32[256,384]{1,0:T(8,128)S(1)} %convert_element_type.15.refs_3_, f32[8,128]{1,0:T(8,128)S(1)} %get-tuple-element.60.refs_4_), custom_call_target="tpu_custom_call" | custom-call | tf_op jit(solution)/shard_map/pallas_call | solution.py:23
  (8 shorter events, 0.2 us)
Async XLA Ops:
  0.0 4.5 %collective-permute-start.2 = (bf16[384,512]{1,0:T(8,128)(2,1)}, bf16[384,512]{1,0:T(8,128)(2,1)S(1)}, u32[]{:S(2)}, u32[]{:S(2)}) collective-permute-start(bf16[384,512]{1,0:T(8,128)(2,1)} %refs_0_.3), channel_id=1, source_target_pairs={{0,1},{1,0},{2,3},{3,2},{4,5},{5,4},{6,7},{7,6},{8,9},{9,8},{10,11... | collective-permute-start | bytes 1179656 | tf_op jit(solution)/shard_map/ppermute | solution.py:47
  0.5 12.7 %collective-permute-start.1 = (bf16[384,512]{1,0:T(8,128)(2,1)}, bf16[384,512]{1,0:T(8,128)(2,1)S(1)}, u32[]{:S(2)}, u32[]{:S(2)}) collective-permute-start(bf16[384,512]{1,0:T(8,128)(2,1)} %refs_0_.3), channel_id=1, source_target_pairs={{0,4},{1,5},{2,6},{3,7},{4,0},{5,1},{6,2},{7,3},{8,12},{9,13},{10,... | collective-permute-start | bytes 1179656 | tf_op jit(solution)/shard_map/ppermute | solution.py:47
  3.0 11.8 %collective-permute-start = (bf16[384,512]{1,0:T(8,128)(2,1)}, bf16[384,512]{1,0:T(8,128)(2,1)S(1)}, u32[]{:S(2)}, u32[]{:S(2)}) collective-permute-start(bf16[384,512]{1,0:T(8,128)(2,1)} %refs_0_.3), channel_id=1, source_target_pairs={{0,2},{1,3},{2,0},{3,1},{4,6},{5,7},{6,4},{7,5},{8,10},{9,11},{10,... | collective-permute-start | bytes 1179656 | tf_op jit(solution)/shard_map/ppermute | solution.py:47
  4.5 0.7 %copy-start.2 = (s32[9,6]{0,1:T(8,128)S(1)}, s32[9,6]{0,1:T(8,128)}, u32[]{:S(2)}) copy-start(s32[9,6]{0,1:T(8,128)} %param.6) | copy-start | bytes 652
  5.2 0.7 %copy-start.3 = (s32[4]{0:T(128)S(1)}, s32[4]{0:T(128)}, u32[]{:S(2)}) copy-start(s32[4]{0:T(128)} %region) | copy-start | bytes 52
  5.8 0.7 %copy-start.4 = (f32[8]{0:T(128)S(1)}, f32[8]{0:T(128)}, u32[]{:S(2)}) copy-start(f32[8]{0:T(128)} %table.1) | copy-start | bytes 100
  7.2 2.1 %collective-permute-start.5 = (bf16[32,512]{1,0:T(8,128)(2,1)S(1)}, bf16[32,512]{1,0:T(8,128)(2,1)S(1)}, u32[]{:S(2)}, u32[]{:S(2)}) collective-permute-start(bf16[32,512]{1,0:T(8,128)(2,1)S(1)} %shard_map.46.refs_1_), channel_id=1, source_target_pairs={{0,1},{1,0},{2,3},{3,2},{4,5},{5,4},{6,7},{7,6},{8,9},{9,8},{10,11... | collective-permute-start | bytes 98312 | tf_op jit(solution)/shard_map/ppermute | solution.py:47
  7.2 7.5 %collective-permute-start.4 = (bf16[32,512]{1,0:T(8,128)(2,1)S(1)}, bf16[32,512]{1,0:T(8,128)(2,1)S(1)}, u32[]{:S(2)}, u32[]{:S(2)}) collective-permute-start(bf16[32,512]{1,0:T(8,128)(2,1)S(1)} %shard_map.46.refs_1_), channel_id=1, source_target_pairs={{0,4},{1,5},{2,6},{3,7},{4,0},{5,1},{6,2},{7,3},{8,12},{9,13},{10,... | collective-permute-start | bytes 98312 | tf_op jit(solution)/shard_map/ppermute | solution.py:47
  7.8 7.3 %collective-permute-start.3 = (bf16[32,512]{1,0:T(8,128)(2,1)S(1)}, bf16[32,512]{1,0:T(8,128)(2,1)S(1)}, u32[]{:S(2)}, u32[]{:S(2)}) collective-permute-start(bf16[32,512]{1,0:T(8,128)(2,1)S(1)} %shard_map.46.refs_1_), channel_id=1, source_target_pairs={{0,2},{1,3},{2,0},{3,1},{4,6},{5,7},{6,4},{7,5},{8,10},{9,11},{10,... | collective-permute-start | bytes 98312 | tf_op jit(solution)/shard_map/ppermute | solution.py:47
  9.3 1.0 %copy-start = (bf16[384,512]{1,0:T(8,128)(2,1)S(1)}, bf16[384,512]{1,0:T(8,128)(2,1)}, u32[]{:S(2)}) copy-start(bf16[384,512]{1,0:T(8,128)(2,1)} %refs_0_.3) | copy-start | bytes 1179652
  12.9 4.5 %copy-start.1 = (bf16[384,512]{1,0:T(8,128)(2,1)S(1)}, bf16[384,512]{1,0:T(8,128)(2,1)}, u32[]{:S(2)}) copy-start(bf16[384,512]{1,0:T(8,128)(2,1)} %refs_0_.3) | copy-start | bytes 1179652
  15.2 5.9 %collective-permute-start.9 = (bf16[832,512]{1,0:T(8,128)(2,1)S(1)}, bf16[832,512]{1,0:T(8,128)(2,1)S(1)}, u32[]{:S(2)}, u32[]{:S(2)}) collective-permute-start(bf16[832,512]{1,0:T(8,128)(2,1)S(1)} %pad_maximum_fusion), channel_id=1, source_target_pairs={{0,1},{1,0},{2,3},{3,2},{4,5},{5,4},{6,7},{7,6},{8,9},{9,8},{10,11... | collective-permute-start | bytes 2555912 | tf_op jit(solution)/shard_map/ppermute | solution.py:47
  15.3 10.1 %collective-permute-start.7 = (bf16[208,512]{1,0:T(8,128)(2,1)S(1)}, bf16[208,512]{1,0:T(8,128)(2,1)S(1)}, u32[]{:S(2)}, u32[]{:S(2)}) collective-permute-start(bf16[208,512]{1,0:T(8,128)(2,1)S(1)} %slice.16), channel_id=1, source_target_pairs={{0,2},{1,3},{2,0},{3,1},{4,6},{5,7},{6,4},{7,5},{8,10},{9,11},{10,... | collective-permute-start | bytes 638984 | tf_op jit(solution)/shard_map/ppermute | solution.py:47
  16.9 8.5 %collective-permute-start.6 = (bf16[208,512]{1,0:T(8,128)(2,1)S(1)}, bf16[208,512]{1,0:T(8,128)(2,1)S(1)}, u32[]{:S(2)}, u32[]{:S(2)}) collective-permute-start(bf16[208,512]{1,0:T(8,128)(2,1)S(1)} %pad_maximum_fusion.2), channel_id=1, source_target_pairs={{0,4},{1,5},{2,6},{3,7},{4,0},{5,1},{6,2},{7,3},{8,12},{9,13},{10,... | collective-permute-start | bytes 638984 | tf_op jit(solution)/shard_map/ppermute | solution.py:47
  17.5 7.9 %collective-permute-start.8 = (bf16[96,512]{1,0:T(8,128)(2,1)S(1)}, bf16[96,512]{1,0:T(8,128)(2,1)S(1)}, u32[]{:S(2)}, u32[]{:S(2)}) collective-permute-start(bf16[96,512]{1,0:T(8,128)(2,1)S(1)} %shard_map.48), channel_id=1, source_target_pairs={{0,24},{1,30},{2,26},{3,11},{4,28},{5,13},{6,9},{7,15},{8,0},{9,6}... | collective-permute-start | bytes 294920 | tf_op jit(solution)/shard_map/ppermute | solution.py:458
  25.5 3.8 %collective-permute-start.10 = (bf16[512,512]{1,0:T(8,128)(2,1)S(1)}, bf16[512,512]{1,0:T(8,128)(2,1)S(1)}, u32[]{:S(2)}, u32[]{:S(2)}) collective-permute-start(bf16[512,512]{1,0:T(8,128)(2,1)S(1)} %pad_maximum_fusion.1), channel_id=1, source_target_pairs={{0,1},{1,0},{2,3},{3,2},{4,5},{5,4},{6,7},{7,6},{8,9},{9,8},{10,11... | collective-permute-start | bytes 1572872 | tf_op jit(solution)/shard_map/ppermute | solution.py:47
  36.1 7.8 %collective-permute-start.13 = (f16[256,384]{1,0:T(8,128)(2,1)S(1)}, f16[256,384]{1,0:T(8,128)(2,1)S(1)}, u32[]{:S(2)}, u32[]{:S(2)}) collective-permute-start(f16[256,384]{1,0:T(8,128)(2,1)S(1)} %get-tuple-element.61), channel_id=1, source_target_pairs={{0,24},{1,25},{2,26},{3,27},{4,28},{5,29},{6,30},{7,31},{8,0},{9,1... | collective-permute-start | bytes 589832 | tf_op jit(solution)/shard_map/ppermute | solution.py:486
  38.6 17.4 %collective-permute-start.12 = (f16[256,384]{1,0:T(8,128)(2,1)S(1)}, f16[256,384]{1,0:T(8,128)(2,1)S(1)}, u32[]{:S(2)}, u32[]{:S(2)}) collective-permute-start(f16[256,384]{1,0:T(8,128)(2,1)S(1)} %get-tuple-element.62), channel_id=1, source_target_pairs={{0,16},{1,17},{2,18},{3,19},{4,20},{5,21},{6,22},{7,23},{8,24},{9,... | collective-permute-start | bytes 589832 | tf_op jit(solution)/shard_map/ppermute | solution.py:486
  38.6 17.4 %collective-permute-start.11 = (f16[256,384]{1,0:T(8,128)(2,1)S(1)}, f16[256,384]{1,0:T(8,128)(2,1)S(1)}, u32[]{:S(2)}, u32[]{:S(2)}) collective-permute-start(f16[256,384]{1,0:T(8,128)(2,1)S(1)} %get-tuple-element.63), channel_id=1, source_target_pairs={{0,8},{1,9},{2,10},{3,11},{4,12},{5,13},{6,14},{7,15},{8,16},{9,17... | collective-permute-start | bytes 589832 | tf_op jit(solution)/shard_map/ppermute | solution.py:486

commit v6 on v5

v6 whole, which is shorter than its diff:
```python
import functools

import jax
import jax.numpy as jnp
from jax import lax
from jax.experimental import pallas as pl
from jax.experimental.pallas import tpu as pltpu
from jax.sharding import PartitionSpec as P

GROUP = 8
CORE, X, Y = 1, 2, 4
KROWS = 32
TOP = 14.0
F32 = jnp.float32
BF16 = jnp.bfloat16
VMEM = pl.BlockSpec(memory_space=pltpu.VMEM)
HBM = pl.BlockSpec(memory_space=pltpu.HBM)


def call(kernel, outs, scratch=(), aliases=None, ins=None):
    def run(*args):
        return pl.pallas_call(
            kernel,
            out_shape=outs,
            in_specs=[VMEM] * len(args) if ins is None else ins,
            out_specs=jax.tree.map(lambda _: VMEM, outs),
            scratch_shapes=list(scratch),
            input_output_aliases=aliases or {},
            compiler_params=pltpu.CompilerParams(vmem_limit_bytes=32 * 1024 * 1024),
            cost_estimate=pl.CostEstimate(flops=0, bytes_accessed=0, transcendentals=0),
        )(*args)

    return run


def shape(dims, dtype=F32):
    return jax.ShapeDtypeStruct(dims, dtype)


def place():
    me = lax.axis_index("mode")
    return lax.rem(me, GROUP), lax.div(me, GROUP)


def flip(values, mask, count):
    return lax.ppermute(values, "mode", [(i, i ^ mask) for i in range(count)])


def weight_kernel(region, index, table, out, region_s, index_s, table_s, sems):
    copies = [
        pltpu.make_async_copy(region, region_s, sems.at[0]),
        pltpu.make_async_copy(index, index_s, sems.at[1]),
        pltpu.make_async_copy(table, table_s, sems.at[2]),
    ]
    for copy in copies:
        copy.start()
    for copy in copies:
        copy.wait()
    slabs = region.shape[0]
    width = out.shape[1] // slabs
    terms = index.shape[0]
    entries = table.shape[0]
    row = lax.broadcasted_iota(jnp.int32, (KROWS, width), 0)
    for s in range(slabs):
        reg = region_s[s]
        block = jnp.zeros((KROWS, width), F32)
        for q in range(terms):
            at = index_s[q, reg]
            kappa = jnp.where(at < entries, table_s[jnp.minimum(at, entries - 1)], 0.0)
            block = jnp.where(lax.div(row, 3) == q, kappa, block)
        high = block.astype(BF16).astype(F32)
        mid = (block - high).astype(BF16).astype(F32)
        low = block - high - mid
        part = lax.rem(row, 3)
        block = jnp.where(part == 0, high, jnp.where(part == 1, mid, low))
        out[:, s * width : (s + 1) * width] = block.astype(BF16)


def weight_rows(cells, region, index, table):
    return call(
        weight_kernel,
        shape((KROWS, cells), BF16),
        [
            pltpu.SMEM(region.shape, jnp.int32),
            pltpu.SMEM(index.shape[::-1], jnp.int32),
            pltpu.SMEM(table.shape, F32),
            pltpu.SemaphoreType.DMA((3,)),
        ],
        ins=[HBM] * 3,
    )(region, index.T, table)


def selector(own, rows, planes):
    j, a = place()
    line = lax.broadcasted_iota(jnp.int32, (planes * own, rows), 0)
    column = lax.broadcasted_iota(jnp.int32, (planes * own, rows), 1)
    shift = jnp.zeros((planes * own, rows), jnp.int32)
    for k in range(planes):
        start = lax.rem(a + k, planes) * (GROUP * own) + j * own - k * own
        shift = jnp.where(line >= k * own, start, shift)
    return jnp.where(column - line == shift, 1.0, 0.0).astype(BF16)


def across(width):
    line = lax.broadcasted_iota(jnp.int32, (width, width), 0)
    column = lax.broadcasted_iota(jnp.int32, (width, width), 1)
    same = jnp.where(line == column, 1.0, 0.0)
    beside = jnp.where(jnp.abs(line - column) == 1, 1.0, 0.0)
    mirror = jnp.where(line + column == width - 1, 1.0, 0.0)
    return jnp.concatenate([2.0 * same - beside, same - mirror], axis=1).astype(BF16)


def act(triples, stencil, sides, right, left, squares, rows, terms):
    total, width = triples[0][1].shape
    own = total - rows
    for n, (before, here, after, weight) in enumerate(triples):
        lanes = slice(n * width, (n + 1) * width)
        side = sides.at[n % 2]
        side[...] = jnp.dot(here[...], stencil, preferred_element_type=F32)
        table = weight[...].astype(F32)
        kappas = []
        for q in range(terms):
            one = (table[3 * q : 3 * q + 1] + table[3 * q + 1 : 3 * q + 2]) + table[
                3 * q + 2 : 3 * q + 3
            ]
            kappas.append(jnp.broadcast_to(one, (8, width))[None])
        sums = [jnp.zeros((8, width), F32) for _ in range(terms)]
        for start in range(0, total, own):
            part = slice(start, start + own)
            value = here[part, :].astype(F32)
            back = value - before[part, :].astype(F32)
            ahead = value - after[part, :].astype(F32)
            shapes = (
                back + ahead,
                side[part, 0:width],
                back,
                ahead,
                side[part, width : 2 * width],
                value,
            )
            for q in range(terms):
                action = shapes[q].reshape(own // 8, 8, width) * kappas[q]
                action = action.reshape(own, width).astype(BF16)
                if start < rows:
                    right[q, part, lanes] = action
                    rounded = action.astype(F32).reshape(own // 8, 8, width)
                    sums[q] += jnp.sum(rounded * rounded, axis=0)
                else:
                    left[q * own : (q + 1) * own, lanes] = action
        for q in range(terms):
            squares[q] += sums[q]


def contract(left, right, own, terms, depth, before, store):
    offset = 0
    for k in range(terms):
        lines = own * (k + 1)
        product = lax.dot_general(
            left[0:lines, 0:depth],
            right[k, :, 0:depth],
            (((1,), (1,)), ((), ())),
            preferred_element_type=F32,
        )
        if before is not None:
            product = before[offset : offset + lines, :] + product
        store(offset, k, product)
        offset += lines


def keep(total):
    def store(offset, _, product):
        total[offset : offset + product.shape[0], :] = product

    return store


def spread(chip, pieces, pick, field, weights, rows):
    j, _ = place()
    width = field.shape[2]
    for flipped, (table, *parts) in enumerate(pieces):
        core = jnp.bitwise_xor(jnp.bitwise_and(j, 1), flipped)
        slabs = table.shape[1] // width
        block = jnp.concatenate([part[...] for part in parts], axis=0)
        picked = jnp.dot(pick, block, preferred_element_type=F32).astype(BF16)
        for s in range(slabs):
            lanes = slice(s * width, (s + 1) * width)
            at = (2 * chip + core) * slabs + s
            weights[at] = table[:, lanes]
            field[at + 1, 0:rows] = block[:, lanes]
            field[at + 1, rows:] = picked[:, lanes]


def split(ref, start, rows):
    return [ref.at[start + rows : start + rows + KROWS], ref.at[start : start + rows]]


def around(field, weights, spots):
    return [(field.at[s], field.at[s + 1], field.at[s + 2], weights.at[s]) for s in spots]


def inside(chip, weights):
    slabs = weights.shape[0] // 4
    return [chip * slabs + s for s in range(1, slabs - 1)]


def seam(chip, weights):
    middle = (2 * lax.div(chip, 2) + 1) * (weights.shape[0] // 4)
    return [middle - 1, middle]


def chip_kernel(sizes, mask, at, border, *refs):
    rows, terms, own, planes = sizes
    if mask:
        mine, table, other, *refs = refs
        _, _, total_in, squares_in, *refs = refs
        pieces = [[table, mine], split(other, at, rows)]
    else:
        mine, table, other, other_table, *refs = refs
        pieces = [[table, mine], [other_table, other]]
        total_in = None
    field, weights, total, squares, sides, right, left = refs
    j, _ = place()
    chip = jnp.bitwise_xor(lax.div(j, 2), mask)
    squares[...] = squares_in[...] if mask else jnp.zeros_like(squares)
    spread(chip, pieces, selector(own, rows, planes), field, weights, rows)
    spots = inside(chip, weights) + (seam(chip, weights) if border else [])
    act(around(field, weights, spots), across(field.shape[2]), sides, right, left, squares, rows, terms)
    depth = len(spots) * field.shape[2]
    contract(left, right, planes * own, terms, depth, total_in, keep(total))


def edge_kernel(*refs):
    pieces, strip = refs[:-1], refs[-1]
    j, _ = place()
    lines, cells = strip.shape
    parts = pieces[0].shape[0] // lines
    width = cells // parts
    for piece, flips in zip(pieces, (0, CORE, X, Y)):
        for here, lanes in ((0, slice(0, width)), (GROUP - 1, slice(cells - width, cells))):

            @pl.when(jnp.bitwise_xor(j, flips) == here)
            def _():
                for n in range(parts):
                    strip[:, n * width : (n + 1) * width] = piece[
                        n * lines : (n + 1) * lines, lanes
                    ]


def last_kernel(sizes, *refs):
    rows, terms, own, planes = sizes
    (one, two, strip, others_in, _, _, total_in, squares_in,
     field, weights, mine, others, levels, squares, sides, right, left) = refs
    slots, every, width = field.shape
    slabs = slots - 2
    lines = every - rows
    j, _ = place()
    chip = jnp.bitwise_xor(lax.div(j, 2), 3)
    pick = selector(own, rows, planes)
    squares[...] = squares_in[...]
    height = one.shape[0] + two.shape[0]
    even = jnp.bitwise_and(j, CORE) == 0
    size = strip.shape[0]
    other = others_in[height:, :]
    first_core = jnp.where(even, strip[...], other)
    second_core = jnp.where(even, other, strip[...])
    for at, source in ((0, second_core), (slots - 1, first_core)):
        for n in range(rows // size):
            field[at, n * size : (n + 1) * size] = source[:, n * width : (n + 1) * width]
        field[at, rows:] = jnp.dot(pick, field[at, 0:rows], preferred_element_type=F32).astype(BF16)
    part = one.shape[0] - KROWS
    there = others_in.at
    pieces = [
        [one.at[part:], one.at[0:part], two],
        [there[part : part + KROWS], there[0:part], there[part + KROWS : height]],
    ]
    spread(chip, pieces, pick, field, weights, rows)
    spots = inside(chip, weights) + seam(chip, weights)
    spots += [0, slabs // 2 - 1, slabs // 2, slabs - 1]
    act(around(field, weights, spots), across(width), sides, right, left, squares, rows, terms)
    lane = lax.broadcasted_iota(jnp.int32, (8, rows), 1)
    spare = jnp.zeros((8, rows), F32)
    powers = []
    for q in range(terms):
        level = jnp.sum(squares[q], keepdims=True)
        levels[q : q + 1, :] = jnp.broadcast_to(level, (1, levels.shape[1]))
        power = jnp.ceil(jnp.log2(jnp.maximum(level, 1e-30)))
        powers.append(power)
        level = level * jnp.exp2(-power)
        high = jnp.floor(level * 2.0**10) * 2.0**-10
        low = (level - high) * 2.0**10
        low = jnp.floor(low * 2.0**10) * 2.0**-10
        for n, value in enumerate((power, high, low)):
            spare = jnp.where(lane == 3 * q + n, value, spare)
    levels[terms:, :] = jnp.zeros((levels.shape[0] - terms, levels.shape[1]), F32)
    end = terms * (terms + 1) // 2 * own
    for z in range(1, planes):
        others[z - 1, end:, :] = spare[0 : others.shape[1] - end]

    def store(_, k, product):
        for q in range(k + 1):
            pair = q * terms - q * (q - 1) // 2 + k - q
            here = slice(pair * own, (pair + 1) * own)
            scale = jnp.exp2(TOP - jnp.ceil(0.5 * (powers[q] + powers[k])))
            for z in range(planes):
                block = product[q * lines + z * own : q * lines + (z + 1) * own, :]
                if z == 0:
                    mine[here, :] = block
                else:
                    others[z - 1, here, :] = block * scale

    contract(left, right, lines, terms, len(spots) * width, total_in, store)


def finish_kernel(own, terms, cells, *refs):
    parts, (levels, out) = refs[:-2], refs[-2:]
    rows = parts[0].shape[1]
    pairs = terms * (terms + 1) // 2
    spares = [part[pairs * own : pairs * own + 1, 0:128] for part in parts[1:]]
    norms = []
    powers = []
    for q in range(terms):
        level = levels[q : q + 1, 0:1]
        powers.append([])
        for spare in spares:
            power, high, low = (spare[:, 3 * q + n : 3 * q + n + 1] for n in range(3))
            level = level + (high + low * 2.0**-10) * jnp.exp2(power)
            powers[q].append(power)
        norms.append(lax.rsqrt(level / (rows * cells) + 1e-06) * cells**-0.5)
    pair = 0
    for q in range(terms):
        for k in range(q, terms):
            here = slice(pair * own, (pair + 1) * own)
            total = parts[0][here, :]
            for n, part in enumerate(parts[1:]):
                power = jnp.ceil(0.5 * (powers[q][n] + powers[k][n])) - TOP
                total = total + part[here, :] * jnp.exp2(power)
            out[:, pair, :] = total * (norms[q] * norms[k])
            pair += 1


def per_device(basis, slab_region, coef_index, coef_table):
    terms = coef_index.shape[1]
    rows, cells = basis.shape
    width = cells // slab_region.shape[0]
    count = lax.axis_size("mode")
    planes = count // GROUP
    own = rows // count
    lines = planes * own
    every = rows + lines
    pairs = terms * (terms + 1) // 2
    slabs = 2 * slab_region.shape[0]
    sizes = (rows, terms, own, planes)

    plane = (
        shape((GROUP // 2 * slabs + 2, every, width), BF16),
        shape((GROUP // 2 * slabs, KROWS, width), BF16),
    )
    sums = (shape((pairs * lines, rows)), shape((terms, 8, width)))

    def scratch(number):
        return [
            pltpu.VMEM((2, every, 2 * width), F32),
            pltpu.VMEM((terms, rows, number * width), BF16),
            pltpu.VMEM((terms * lines, number * width), BF16),
        ]

    def chip(mask, at, border):
        return call(
            functools.partial(chip_kernel, sizes, mask, at, border),
            plane + sums,
            scratch(slabs if border else slabs - 2),
            aliases={3: 0, 4: 1} if mask else None,
        )

    by_x = flip(basis, X, count)
    by_y = flip(basis, Y, count)
    by_core = flip(basis, CORE, count)
    by_core, slab_region = lax.optimization_barrier((by_core, slab_region))
    table = weight_rows(cells, slab_region, coef_index, coef_table)
    table_core = flip(table, CORE, count)
    table_x = flip(table, X, count)
    table_y = flip(table, Y, count)
    field, weights, total, squares = chip(0, 0, False)(basis, table, by_core, table_core)
    by_x, by_y, table_x, table_y, total = lax.optimization_barrier(
        (by_x, by_y, table_x, table_y, total)
    )

    half = (rows - KROWS) // 2
    one = flip(jnp.concatenate([by_x[:half], table_x], axis=0), Y, count)
    two = flip(by_y[half:], X, count)
    others = flip(jnp.concatenate([by_x, table_x, by_y, table_y], axis=0), CORE, count)
    strip = call(edge_kernel, shape((rows * width // cells, cells), BF16))(
        basis, by_core, by_x, by_y
    )
    pairs_of = []
    for i in range(count):
        here = i % GROUP
        if here in (0, 1, 2, 4):
            to = (i - here - GROUP) % count + (6 if here == 1 else here)
        else:
            to = (i - here + GROUP) % count + (1 if here == 6 else here)
        pairs_of.append((i, to))
    strip = lax.ppermute(strip, "mode", pairs_of)
    field, weights, total, squares = chip(1, 0, True)(
        by_x, table_x, others, field, weights, total, squares
    )
    one, two, strip, total = lax.optimization_barrier((one, two, strip, total))

    diagonal = flip(jnp.concatenate([one, two, strip], axis=0), CORE, count)
    field, weights, total, squares = chip(2, rows + KROWS, False)(
        by_y, table_y, others, field, weights, total, squares
    )
    diagonal, total = lax.optimization_barrier((diagonal, total))

    height = pairs * own + 8 - (pairs * own) % 8
    _, _, mine, others, levels = call(
        functools.partial(last_kernel, sizes),
        plane + (shape((height, rows)), shape((planes - 1, height, rows)), shape((8, 128))),
        [pltpu.VMEM(sums[1].shape, F32)] + scratch(slabs + 4),
        aliases={4: 0, 5: 1},
    )(one, two, strip, diagonal, field, weights, total, squares)

    parts = [mine]
    others = others.astype(jnp.float16)
    for z in range(1, planes):
        there = [(i, (i + z * GROUP) % count) for i in range(count)]
        parts.append(lax.ppermute(others[z - 1], "mode", there).astype(F32))
    out = call(
        functools.partial(finish_kernel, own, terms, cells * count), shape((own, pairs, rows))
    )(*parts, levels)
    return jnp.transpose(out, (1, 0, 2))


def solution(mesh):
    return jax.shard_map(
        per_device,
        mesh=mesh,
        in_specs=(P("groups", "mode"), P(("groups", "mode")), P("groups", None), P("groups")),
        out_specs=P(None, ("groups", "mode"), None),
        check_vma=False,
    )
```

time: 57.4 us -> 55.2 us (0.962)
  the two profiles are of different devices: /device:TPU:0 before, /device:TPU:15 now
where the time goes in v6:
time: 55.2 us; the launch traced here: 55 us
  waiting for transfers between devices  19.7 us (36%)
  Pallas kernels  16.9 us (31%)
  starting transfers between devices  14.9 us (27%)
  local copies, waits for them, and re-layouts  3.14 us (6%)
    pallas_call x7, Pallas kernels, run(): pl.pallas_call(kernel, out_shape=outs, in_specs=[VMEM] * len(args) if ins...  16.9 us
    ppermute x3, waiting for transfers between devices, per_device(): parts.append(lax.ppermute(others[z - 1], 'mode', there).astype(F32))  16.6 us
    ppermute x10, starting transfers between devices, flip(): return lax.ppermute(values, 'mode', [(i, i ^ mask) for i in range(count)])  7.83 us
    ppermute x3, starting transfers between devices, per_device(): parts.append(lax.ppermute(others[z - 1], 'mode', there).astype(F32))  5.51 us
    ppermute x10, waiting for transfers between devices, flip(): return lax.ppermute(values, 'mode', [(i, i ^ mask) for i in range(count)])  3.11 us
    unnamed x10, local copies, waits for them, and re-layouts  3 us
    ppermute x1, starting transfers between devices, per_device(): strip = lax.ppermute(strip, 'mode', pairs_of)  1.53 us
  transfers between devices with their start and end apart: 14, of which 7 were waited for; matrix products, arithmetic and copies ran while one was open for 0% of the time, Pallas kernels for 18%

profile of v6, /device:TPU:15, one launch (start us, length us, event | category | flops | bytes accessed | tf_op | source)
XLA Modules:
  0.0 55.0 jit_solution(9961763665900390789)
XLA Ops:
  0.0 0.7 %collective-permute-start.2 = (bf16[384,512]{1,0:T(8,128)(2,1)}, bf16[384,512]{1,0:T(8,128)(2,1)S(1)}, u32[]{:S(2)}, u32[]{:S(2)}) collective-permute-start(bf16[384,512]{1,0:T(8,128)(2,1)} %refs_0_.3), channel_id=1, source_target_pairs={{0,1},{1,0},{2,3},{3,2},{4,5},{5,4},{6,7},{7,6},{8,9},{9,8},{10,11... | collective-permute-start | bytes 1179656 | tf_op jit(solution)/shard_map/ppermute | solution.py:46
  0.7 0.3 collective-permute-start
  0.9 0.2 collective-permute-start.1
  1.2 1.1 %collective-permute-done.2.refs_2_.refs_1_ = bf16[384,512]{1,0:T(8,128)(2,1)S(1)} collective-permute-done((bf16[384,512]{1,0:T(8,128)(2,1)}, bf16[384,512]{1,0:T(8,128)(2,1)S(1)}, u32[]{:S(2)}, u32[]{:S(2)}) %collective-permute-start.2) | collective-permute-done | bytes 393248 | tf_op jit(solution)/shard_map/ppermute | solution.py:46
  2.2 0.0 copy-start.2
  2.2 0.7 %copy-done.2 = s32[9,6]{0,1:T(8,128)S(1)} copy-done((s32[9,6]{0,1:T(8,128)S(1)}, s32[9,6]{0,1:T(8,128)}, u32[]{:S(2)}) %copy-start.2) | copy-done | bytes 240
  2.9 0.0 copy-start.3
  2.9 0.7 %copy-done.3 = s32[4]{0:T(128)S(1)} copy-done((s32[4]{0:T(128)S(1)}, s32[4]{0:T(128)}, u32[]{:S(2)}) %copy-start.3) | copy-done | bytes 40
  3.6 0.0 copy-start.4
  3.6 0.7 %copy-done.4 = f32[8]{0:T(128)S(1)} copy-done((f32[8]{0:T(128)S(1)}, f32[8]{0:T(128)}, u32[]{:S(2)}) %copy-start.4) | copy-done | bytes 56
  4.2 0.7 %shard_map.46.refs_1_ = bf16[32,512]{1,0:T(8,128)(2,1)S(1)} custom-call(s32[4]{0:T(128)S(1)} %copy-done.3, s32[6,9]{1,0:T(8,128)S(1)} %bitcast.8, f32[8]{0:T(128)S(1)} %copy-done.4), custom_call_target="tpu_custom_call" | custom-call | tf_op jit(solution)/shard_map/pallas_call | solution.py:22
  4.9 0.4 collective-permute-start.5
  5.4 0.3 collective-permute-start.3
  5.7 1.2 %collective-permute-start.4 = (bf16[32,512]{1,0:T(8,128)(2,1)S(1)}, bf16[32,512]{1,0:T(8,128)(2,1)S(1)}, u32[]{:S(2)}, u32[]{:S(2)}) collective-permute-start(bf16[32,512]{1,0:T(8,128)(2,1)S(1)} %shard_map.46.refs_1_), channel_id=1, source_target_pairs={{0,4},{1,5},{2,6},{3,7},{4,0},{5,1},{6,2},{7,3},{8,12},{9,13},{10,... | collective-permute-start | bytes 98312 | tf_op jit(solution)/shard_map/ppermute | solution.py:46
  7.0 0.0 collective-permute-done.5.refs_3_
  7.0 0.0 copy-start
  7.0 1.0 %copy-done = bf16[384,512]{1,0:T(8,128)(2,1)S(1)} copy-done((bf16[384,512]{1,0:T(8,128)(2,1)S(1)}, bf16[384,512]{1,0:T(8,128)(2,1)}, u32[]{:S(2)}) %copy-start) | copy-done | bytes 393240
  8.0 0.0 copy-start.1
  8.0 2.6 %shard_map.47 = (bf16[34,432,128]{2,1,0:T(8,128)(2,1)S(1)}, bf16[32,32,128]{2,1,0:T(8,128)(2,1)S(1)}, f32[1008,384]{1,0:T(8,128)S(1)}, f32[6,8,128]{2,1,0:T(8,128)S(1)}) custom-call(bf16[384,512]{1,0:T(8,128)(2,1)S(1)} %copy-done, bf16[32,512]{1,0:T(8,128)(2,1)S(1)} %shard_map.46.refs_1_, bf16[384,512]{1,0:T(8,128)(2,1)S(1)} %collective-permute-done.2.refs_2_.refs_1_, ...), custom_call_target="tpu_custom_call" | custom-call | tf_op jit(solution)/shard_map/pallas_call | solution.py:22
  10.6 1.1 %collective-permute-done.refs_2_.refs_0_ = bf16[384,512]{1,0:T(8,128)(2,1)S(1)} collective-permute-done((bf16[384,512]{1,0:T(8,128)(2,1)}, bf16[384,512]{1,0:T(8,128)(2,1)S(1)}, u32[]{:S(2)}, u32[]{:S(2)}) %collective-permute-start) | collective-permute-done | bytes 393248 | tf_op jit(solution)/shard_map/ppermute | solution.py:46
  11.6 0.0 collective-permute-done.1.refs_3_.refs_0_
  11.6 0.7 %collective-permute-done.3.refs_1_ = bf16[32,512]{1,0:T(8,128)(2,1)S(1)} collective-permute-done((bf16[32,512]{1,0:T(8,128)(2,1)S(1)}, bf16[32,512]{1,0:T(8,128)(2,1)S(1)}, u32[]{:S(2)}, u32[]{:S(2)}) %collective-permute-start.3) | collective-permute-done | bytes 32800 | tf_op jit(solution)/shard_map/ppermute | solution.py:46
  12.3 0.0 collective-permute-done.4.refs_1_
  12.3 0.1 pad_maximum_fusion
  12.4 1.1 %collective-permute-start.9 = (bf16[832,512]{1,0:T(8,128)(2,1)S(1)}, bf16[832,512]{1,0:T(8,128)(2,1)S(1)}, u32[]{:S(2)}, u32[]{:S(2)}) collective-permute-start(bf16[832,512]{1,0:T(8,128)(2,1)S(1)} %pad_maximum_fusion), channel_id=1, source_target_pairs={{0,1},{1,0},{2,3},{3,2},{4,5},{5,4},{6,7},{7,6},{8,9},{9,8},{10,11... | collective-permute-start | bytes 2555912 | tf_op jit(solution)/shard_map/ppermute | solution.py:46
  13.6 0.3 collective-permute-start.6
  13.9 1.2 %collective-permute-start.7 = (bf16[208,512]{1,0:T(8,128)(2,1)S(1)}, bf16[208,512]{1,0:T(8,128)(2,1)S(1)}, u32[]{:S(2)}, u32[]{:S(2)}) collective-permute-start(bf16[208,512]{1,0:T(8,128)(2,1)S(1)} %slice.16), channel_id=1, source_target_pairs={{0,2},{1,3},{2,0},{3,1},{4,6},{5,7},{6,4},{7,5},{8,10},{9,11},{10,... | collective-permute-start | bytes 638984 | tf_op jit(solution)/shard_map/ppermute | solution.py:46
  15.1 0.0 copy-done.1
  15.1 1.5 %collective-permute-start.8 = (bf16[96,512]{1,0:T(8,128)(2,1)S(1)}, bf16[96,512]{1,0:T(8,128)(2,1)S(1)}, u32[]{:S(2)}, u32[]{:S(2)}) collective-permute-start(bf16[96,512]{1,0:T(8,128)(2,1)S(1)} %shard_map.48), channel_id=1, source_target_pairs={{0,24},{1,30},{2,26},{3,11},{4,28},{5,13},{6,9},{7,15},{8,0},{9,6}... | collective-permute-start | bytes 294920 | tf_op jit(solution)/shard_map/ppermute | solution.py:403
  16.7 0.0 collective-permute-done.9.refs_2_
  16.7 3.7 %shard_map.49 = (bf16[34,432,128]{2,1,0:T(8,128)(2,1)S(1)}, bf16[32,32,128]{2,1,0:T(8,128)(2,1)S(1)}, f32[1008,384]{1,0:T(8,128)S(1)}, f32[6,8,128]{2,1,0:T(8,128)S(1)}) custom-call(bf16[384,512]{1,0:T(8,128)(2,1)S(1)} %collective-permute-done.refs_2_.refs_0_, ...), custom_call_target="tpu_custom_call", output_to_operand_aliasing={{0}: (3, {}), {1}: (4, {})} | custom-call | tf_op jit(solution)/shard_map/pallas_call | solution.py:22
  20.4 0.0 collective-permute-done.8.refs_2_
  20.4 0.3 collective-permute-done.6.refs_0_
  20.7 0.0 collective-permute-done.7.refs_1_
  20.7 2.0 %collective-permute-start.10 = (bf16[512,512]{1,0:T(8,128)(2,1)S(1)}, bf16[512,512]{1,0:T(8,128)(2,1)S(1)}, u32[]{:S(2)}, u32[]{:S(2)}) collective-permute-start(bf16[512,512]{1,0:T(8,128)(2,1)S(1)} %pad_maximum_fusion.1), channel_id=1, source_target_pairs={{0,1},{1,0},{2,3},{3,2},{4,5},{5,4},{6,7},{7,6},{8,9},{9,8},{10,11... | collective-permute-start | bytes 1572872 | tf_op jit(solution)/shard_map/ppermute | solution.py:46
  22.8 2.7 %shard_map.50 = (bf16[34,432,128]{2,1,0:T(8,128)(2,1)S(1)}, bf16[32,32,128]{2,1,0:T(8,128)(2,1)S(1)}, f32[1008,384]{1,0:T(8,128)S(1)}, f32[6,8,128]{2,1,0:T(8,128)S(1)}) custom-call(bf16[384,512]{1,0:T(8,128)(2,1)S(1)} %collective-permute-done.1.refs_3_.refs_0_, ...), custom_call_target="tpu_custom_call", output_to_operand_aliasing={{0}: (3, {}), {1}: (4, {})} | custom-call | tf_op jit(solution)/shard_map/pallas_call | solution.py:22
  25.4 0.0 collective-permute-done.10.refs_3_
  25.4 6.0 %shard_map.51 = (bf16[34,432,128]{2,1,0:T(8,128)(2,1)S(1)}, bf16[32,32,128]{2,1,0:T(8,128)(2,1)S(1)}, f32[256,384]{1,0:T(8,128)S(1)}, f32[3,256,384]{2,1,0:T(8,128)S(1)}, f32[8,128]{1,0:T(8,128)S(1)}) custom-call(bf16[208,512]{1,0:T(8,128)(2,1)S(1)} %collective-permute-done.6.refs_0_, ...), custom_call_target="tpu_custom_call", output_to_operand_aliasing={{0}: (4, {}), {1}: (5, {})} | custom-call | tf_op jit(solution)/shard_map/pallas_call | solution.py:22
  31.4 0.1 convert_element_type.12
  31.5 0.1 slice_bitcast_fusion
  31.6 1.3 %collective-permute-start.11 = (f16[256,384]{1,0:T(8,128)(2,1)S(1)}, f16[256,384]{1,0:T(8,128)(2,1)S(1)}, u32[]{:S(2)}, u32[]{:S(2)}) collective-permute-start(f16[256,384]{1,0:T(8,128)(2,1)S(1)} %get-tuple-element.63), channel_id=1, source_target_pairs={{0,8},{1,9},{2,10},{3,11},{4,12},{5,13},{6,14},{7,15},{8,16},{9,17... | collective-permute-start | bytes 589832 | tf_op jit(solution)/shard_map/ppermute | solution.py:427
  33.0 2.8 %collective-permute-start.12 = (f16[256,384]{1,0:T(8,128)(2,1)S(1)}, f16[256,384]{1,0:T(8,128)(2,1)S(1)}, u32[]{:S(2)}, u32[]{:S(2)}) collective-permute-start(f16[256,384]{1,0:T(8,128)(2,1)S(1)} %get-tuple-element.62), channel_id=1, source_target_pairs={{0,16},{1,17},{2,18},{3,19},{4,20},{5,21},{6,22},{7,23},{8,24},{9,... | collective-permute-start | bytes 589832 | tf_op jit(solution)/shard_map/ppermute | solution.py:427
  35.8 1.4 %collective-permute-start.13 = (f16[256,384]{1,0:T(8,128)(2,1)S(1)}, f16[256,384]{1,0:T(8,128)(2,1)S(1)}, u32[]{:S(2)}, u32[]{:S(2)}) collective-permute-start(f16[256,384]{1,0:T(8,128)(2,1)S(1)} %get-tuple-element.61), channel_id=1, source_target_pairs={{0,24},{1,25},{2,26},{3,27},{4,28},{5,29},{6,30},{7,31},{8,0},{9,1... | collective-permute-start | bytes 589832 | tf_op jit(solution)/shard_map/ppermute | solution.py:427
  37.1 1.1 %collective-permute-done.11 = f16[256,384]{1,0:T(8,128)(2,1)S(1)} collective-permute-done((f16[256,384]{1,0:T(8,128)(2,1)S(1)}, f16[256,384]{1,0:T(8,128)(2,1)S(1)}, u32[]{:S(2)}, u32[]{:S(2)}) %collective-permute-start.11) | collective-permute-done | bytes 196640 | tf_op jit(solution)/shard_map/ppermute | solution.py:427
  38.2 11.7 %collective-permute-done.12 = f16[256,384]{1,0:T(8,128)(2,1)S(1)} collective-permute-done((f16[256,384]{1,0:T(8,128)(2,1)S(1)}, f16[256,384]{1,0:T(8,128)(2,1)S(1)}, u32[]{:S(2)}, u32[]{:S(2)}) %collective-permute-start.12) | collective-permute-done | bytes 196640 | tf_op jit(solution)/shard_map/ppermute | solution.py:427
  50.0 3.8 %collective-permute-done.13 = f16[256,384]{1,0:T(8,128)(2,1)S(1)} collective-permute-done((f16[256,384]{1,0:T(8,128)(2,1)S(1)}, f16[256,384]{1,0:T(8,128)(2,1)S(1)}, u32[]{:S(2)}, u32[]{:S(2)}) %collective-permute-start.13) | collective-permute-done | bytes 196640 | tf_op jit(solution)/shard_map/ppermute | solution.py:427
  53.8 1.2 %shard_map.52 = f32[12,21,384]{2,1,0:T(8,128)} custom-call(f32[256,384]{1,0:T(8,128)S(1)} %get-tuple-element.58.refs_0_, f32[256,384]{1,0:T(8,128)S(1)} %convert_element_type.13.refs_1_, f32[256,384]{1,0:T(8,128)S(1)} %convert_element_type.14.refs_2_, f32[256,384]{1,0:T(8,128)S(1)} %convert_element_type.15.refs_3_, f32[8,128]{1,0:T(8,128)S(1)} %get-tuple-element.60.refs_4_), custom_call_target="tpu_custom_call" | custom-call | tf_op jit(solution)/shard_map/pallas_call | solution.py:22
  (8 shorter events, 0.2 us)
Async XLA Ops:
  0.0 2.2 %collective-permute-start.2 = (bf16[384,512]{1,0:T(8,128)(2,1)}, bf16[384,512]{1,0:T(8,128)(2,1)S(1)}, u32[]{:S(2)}, u32[]{:S(2)}) collective-permute-start(bf16[384,512]{1,0:T(8,128)(2,1)} %refs_0_.3), channel_id=1, source_target_pairs={{0,1},{1,0},{2,3},{3,2},{4,5},{5,4},{6,7},{7,6},{8,9},{9,8},{10,11... | collective-permute-start | bytes 1179656 | tf_op jit(solution)/shard_map/ppermute | solution.py:46
  0.7 11.0 %collective-permute-start = (bf16[384,512]{1,0:T(8,128)(2,1)}, bf16[384,512]{1,0:T(8,128)(2,1)S(1)}, u32[]{:S(2)}, u32[]{:S(2)}) collective-permute-start(bf16[384,512]{1,0:T(8,128)(2,1)} %refs_0_.3), channel_id=1, source_target_pairs={{0,2},{1,3},{2,0},{3,1},{4,6},{5,7},{6,4},{7,5},{8,10},{9,11},{10,... | collective-permute-start | bytes 1179656 | tf_op jit(solution)/shard_map/ppermute | solution.py:46
  0.9 10.7 %collective-permute-start.1 = (bf16[384,512]{1,0:T(8,128)(2,1)}, bf16[384,512]{1,0:T(8,128)(2,1)S(1)}, u32[]{:S(2)}, u32[]{:S(2)}) collective-permute-start(bf16[384,512]{1,0:T(8,128)(2,1)} %refs_0_.3), channel_id=1, source_target_pairs={{0,4},{1,5},{2,6},{3,7},{4,0},{5,1},{6,2},{7,3},{8,12},{9,13},{10,... | collective-permute-start | bytes 1179656 | tf_op jit(solution)/shard_map/ppermute | solution.py:46
  2.2 0.7 %copy-start.2 = (s32[9,6]{0,1:T(8,128)S(1)}, s32[9,6]{0,1:T(8,128)}, u32[]{:S(2)}) copy-start(s32[9,6]{0,1:T(8,128)} %param.6) | copy-start | bytes 652
  2.9 0.7 %copy-start.3 = (s32[4]{0:T(128)S(1)}, s32[4]{0:T(128)}, u32[]{:S(2)}) copy-start(s32[4]{0:T(128)} %region) | copy-start | bytes 52
  3.6 0.7 %copy-start.4 = (f32[8]{0:T(128)S(1)}, f32[8]{0:T(128)}, u32[]{:S(2)}) copy-start(f32[8]{0:T(128)} %table.1) | copy-start | bytes 100
  4.9 2.0 %collective-permute-start.5 = (bf16[32,512]{1,0:T(8,128)(2,1)S(1)}, bf16[32,512]{1,0:T(8,128)(2,1)S(1)}, u32[]{:S(2)}, u32[]{:S(2)}) collective-permute-start(bf16[32,512]{1,0:T(8,128)(2,1)S(1)} %shard_map.46.refs_1_), channel_id=1, source_target_pairs={{0,1},{1,0},{2,3},{3,2},{4,5},{5,4},{6,7},{7,6},{8,9},{9,8},{10,11... | collective-permute-start | bytes 98312 | tf_op jit(solution)/shard_map/ppermute | solution.py:46
  5.4 7.0 %collective-permute-start.3 = (bf16[32,512]{1,0:T(8,128)(2,1)S(1)}, bf16[32,512]{1,0:T(8,128)(2,1)S(1)}, u32[]{:S(2)}, u32[]{:S(2)}) collective-permute-start(bf16[32,512]{1,0:T(8,128)(2,1)S(1)} %shard_map.46.refs_1_), channel_id=1, source_target_pairs={{0,2},{1,3},{2,0},{3,1},{4,6},{5,7},{6,4},{7,5},{8,10},{9,11},{10,... | collective-permute-start | bytes 98312 | tf_op jit(solution)/shard_map/ppermute | solution.py:46
  5.7 6.6 %collective-permute-start.4 = (bf16[32,512]{1,0:T(8,128)(2,1)S(1)}, bf16[32,512]{1,0:T(8,128)(2,1)S(1)}, u32[]{:S(2)}, u32[]{:S(2)}) collective-permute-start(bf16[32,512]{1,0:T(8,128)(2,1)S(1)} %shard_map.46.refs_1_), channel_id=1, source_target_pairs={{0,4},{1,5},{2,6},{3,7},{4,0},{5,1},{6,2},{7,3},{8,12},{9,13},{10,... | collective-permute-start | bytes 98312 | tf_op jit(solution)/shard_map/ppermute | solution.py:46
  7.0 1.0 %copy-start = (bf16[384,512]{1,0:T(8,128)(2,1)S(1)}, bf16[384,512]{1,0:T(8,128)(2,1)}, u32[]{:S(2)}) copy-start(bf16[384,512]{1,0:T(8,128)(2,1)} %refs_0_.3) | copy-start | bytes 1179652
  8.0 7.1 %copy-start.1 = (bf16[384,512]{1,0:T(8,128)(2,1)S(1)}, bf16[384,512]{1,0:T(8,128)(2,1)}, u32[]{:S(2)}) copy-start(bf16[384,512]{1,0:T(8,128)(2,1)} %refs_0_.3) | copy-start | bytes 1179652
  12.4 4.3 %collective-permute-start.9 = (bf16[832,512]{1,0:T(8,128)(2,1)S(1)}, bf16[832,512]{1,0:T(8,128)(2,1)S(1)}, u32[]{:S(2)}, u32[]{:S(2)}) collective-permute-start(bf16[832,512]{1,0:T(8,128)(2,1)S(1)} %pad_maximum_fusion), channel_id=1, source_target_pairs={{0,1},{1,0},{2,3},{3,2},{4,5},{5,4},{6,7},{7,6},{8,9},{9,8},{10,11... | collective-permute-start | bytes 2555912 | tf_op jit(solution)/shard_map/ppermute | solution.py:46
  13.6 7.1 %collective-permute-start.6 = (bf16[208,512]{1,0:T(8,128)(2,1)S(1)}, bf16[208,512]{1,0:T(8,128)(2,1)S(1)}, u32[]{:S(2)}, u32[]{:S(2)}) collective-permute-start(bf16[208,512]{1,0:T(8,128)(2,1)S(1)} %pad_maximum_fusion.2), channel_id=1, source_target_pairs={{0,4},{1,5},{2,6},{3,7},{4,0},{5,1},{6,2},{7,3},{8,12},{9,13},{10,... | collective-permute-start | bytes 638984 | tf_op jit(solution)/shard_map/ppermute | solution.py:46
  13.9 6.8 %collective-permute-start.7 = (bf16[208,512]{1,0:T(8,128)(2,1)S(1)}, bf16[208,512]{1,0:T(8,128)(2,1)S(1)}, u32[]{:S(2)}, u32[]{:S(2)}) collective-permute-start(bf16[208,512]{1,0:T(8,128)(2,1)S(1)} %slice.16), channel_id=1, source_target_pairs={{0,2},{1,3},{2,0},{3,1},{4,6},{5,7},{6,4},{7,5},{8,10},{9,11},{10,... | collective-permute-start | bytes 638984 | tf_op jit(solution)/shard_map/ppermute | solution.py:46
  15.1 5.3 %collective-permute-start.8 = (bf16[96,512]{1,0:T(8,128)(2,1)S(1)}, bf16[96,512]{1,0:T(8,128)(2,1)S(1)}, u32[]{:S(2)}, u32[]{:S(2)}) collective-permute-start(bf16[96,512]{1,0:T(8,128)(2,1)S(1)} %shard_map.48), channel_id=1, source_target_pairs={{0,24},{1,30},{2,26},{3,11},{4,28},{5,13},{6,9},{7,15},{8,0},{9,6}... | collective-permute-start | bytes 294920 | tf_op jit(solution)/shard_map/ppermute | solution.py:403
  20.7 4.7 %collective-permute-start.10 = (bf16[512,512]{1,0:T(8,128)(2,1)S(1)}, bf16[512,512]{1,0:T(8,128)(2,1)S(1)}, u32[]{:S(2)}, u32[]{:S(2)}) collective-permute-start(bf16[512,512]{1,0:T(8,128)(2,1)S(1)} %pad_maximum_fusion.1), channel_id=1, source_target_pairs={{0,1},{1,0},{2,3},{3,2},{4,5},{5,4},{6,7},{7,6},{8,9},{9,8},{10,11... | collective-permute-start | bytes 1572872 | tf_op jit(solution)/shard_map/ppermute | solution.py:46
  31.6 6.6 %collective-permute-start.11 = (f16[256,384]{1,0:T(8,128)(2,1)S(1)}, f16[256,384]{1,0:T(8,128)(2,1)S(1)}, u32[]{:S(2)}, u32[]{:S(2)}) collective-permute-start(f16[256,384]{1,0:T(8,128)(2,1)S(1)} %get-tuple-element.63), channel_id=1, source_target_pairs={{0,8},{1,9},{2,10},{3,11},{4,12},{5,13},{6,14},{7,15},{8,16},{9,17... | collective-permute-start | bytes 589832 | tf_op jit(solution)/shard_map/ppermute | solution.py:427
  33.0 16.9 %collective-permute-start.12 = (f16[256,384]{1,0:T(8,128)(2,1)S(1)}, f16[256,384]{1,0:T(8,128)(2,1)S(1)}, u32[]{:S(2)}, u32[]{:S(2)}) collective-permute-start(f16[256,384]{1,0:T(8,128)(2,1)S(1)} %get-tuple-element.62), channel_id=1, source_target_pairs={{0,16},{1,17},{2,18},{3,19},{4,20},{5,21},{6,22},{7,23},{8,24},{9,... | collective-permute-start | bytes 589832 | tf_op jit(solution)/shard_map/ppermute | solution.py:427
  35.8 18.0 %collective-permute-start.13 = (f16[256,384]{1,0:T(8,128)(2,1)S(1)}, f16[256,384]{1,0:T(8,128)(2,1)S(1)}, u32[]{:S(2)}, u32[]{:S(2)}) collective-permute-start(f16[256,384]{1,0:T(8,128)(2,1)S(1)} %get-tuple-element.61), channel_id=1, source_target_pairs={{0,24},{1,25},{2,26},{3,27},{4,28},{5,29},{6,30},{7,31},{8,0},{9,1... | collective-permute-start | bytes 589832 | tf_op jit(solution)/shard_map/ppermute | solution.py:427

commit v7 on v6

--- a/solution.py
+++ b/solution.py
@@ -40,6 +40,21 @@
 def place():
     me = lax.axis_index("mode")
     return lax.rem(me, GROUP), lax.div(me, GROUP)
+
+
+def steps(planes):
+    if planes & (planes - 1):
+        return list(range(1, planes))
+    order = []
+    while planes > 1:
+        order += range(planes // 2, planes)
+        planes //= 2
+    return order
+
+
+def partner(a, k, planes):
+    step = ([0] + steps(planes))[k]
+    return (a + step) % planes if planes & (planes - 1) else a ^ step
 
 
 def flip(values, mask, count):
@@ -96,7 +111,7 @@
     column = lax.broadcasted_iota(jnp.int32, (planes * own, rows), 1)
     shift = jnp.zeros((planes * own, rows), jnp.int32)
     for k in range(planes):
-        start = lax.rem(a + k, planes) * (GROUP * own) + j * own - k * own
+        start = partner(a, k, planes) * (GROUP * own) + j * own - k * own
         shift = jnp.where(line >= k * own, start, shift)
     return jnp.where(column - line == shift, 1.0, 0.0).astype(BF16)
 
@@ -381,9 +396,7 @@
     table_x = flip(table, X, count)
     table_y = flip(table, Y, count)
     field, weights, total, squares = chip(0, 0, False)(basis, table, by_core, table_core)
-    by_x, by_y, table_x, table_y, total = lax.optimization_barrier(
-        (by_x, by_y, table_x, table_y, total)
-    )
+    by_x, by_y, total = lax.optimization_barrier((by_x, by_y, total))
 
     half = (rows - KROWS) // 2
     one = flip(jnp.concatenate([by_x[:half], table_x], axis=0), Y, count)
@@ -423,7 +436,7 @@
     parts = [mine]
     others = others.astype(jnp.float16)
     for z in range(1, planes):
-        there = [(i, (i + z * GROUP) % count) for i in range(count)]
+        there = [(i, partner(i // GROUP, z, planes) * GROUP + i % GROUP) for i in range(count)]
         parts.append(lax.ppermute(others[z - 1], "mode", there).astype(F32))
     out = call(
         functools.partial(finish_kernel, own, terms, cells * count), shape((own, pairs, rows))

time: 55.2 us -> 54.5 us (0.987)
  the two profiles are of different devices: /device:TPU:15 before, /device:TPU:0 now
where the time goes in v7:
time: 54.5 us; the launch traced here: 53.9 us
  starting transfers between devices  17.2 us (32%)
  Pallas kernels  16.9 us (31%)
  waiting for transfers between devices  16.2 us (30%)
  local copies, waits for them, and re-layouts  3.15 us (6%)
    pallas_call x7, Pallas kernels, run(): pl.pallas_call(kernel, out_shape=outs, in_specs=[VMEM] * len(args) if ins...  16.9 us
    ppermute x3, waiting for transfers between devices, per_device(): parts.append(lax.ppermute(others[z - 1], 'mode', there).astype(F32))  14 us
    ppermute x10, starting transfers between devices, flip(): return lax.ppermute(values, 'mode', [(i, i ^ mask) for i in range(count)])  9.82 us
    ppermute x1, starting transfers between devices, per_device(): strip = lax.ppermute(strip, 'mode', pairs_of)  3.83 us
    ppermute x3, starting transfers between devices, per_device(): parts.append(lax.ppermute(others[z - 1], 'mode', there).astype(F32))  3.55 us
    unnamed x10, local copies, waits for them, and re-layouts  3 us
    ppermute x10, waiting for transfers between devices, flip(): return lax.ppermute(values, 'mode', [(i, i ^ mask) for i in range(count)])  2.2 us
  transfers between devices with their start and end apart: 14, of which 5 were waited for; matrix products, arithmetic and copies ran while one was open for 0% of the time, Pallas kernels for 18%

profile of v7, /device:TPU:0, one launch (start us, length us, event | category | flops | bytes accessed | tf_op | source)
XLA Modules:
  0.0 53.9 jit_solution(11161345954343450744)
XLA Ops:
  0.0 0.5 collective-permute-start.2
  0.5 2.5 %collective-permute-start = (bf16[384,512]{1,0:T(8,128)(2,1)}, bf16[384,512]{1,0:T(8,128)(2,1)S(1)}, u32[]{:S(2)}, u32[]{:S(2)}) collective-permute-start(bf16[384,512]{1,0:T(8,128)(2,1)} %refs_0_.3), channel_id=1, source_target_pairs={{0,2},{1,3},{2,0},{3,1},{4,6},{5,7},{6,4},{7,5},{8,10},{9,11},{10,... | collective-permute-start | bytes 1179656 | tf_op jit(solution)/shard_map/ppermute | solution.py:61
  2.9 1.5 %collective-permute-start.1 = (bf16[384,512]{1,0:T(8,128)(2,1)}, bf16[384,512]{1,0:T(8,128)(2,1)S(1)}, u32[]{:S(2)}, u32[]{:S(2)}) collective-permute-start(bf16[384,512]{1,0:T(8,128)(2,1)} %refs_0_.3), channel_id=1, source_target_pairs={{0,4},{1,5},{2,6},{3,7},{4,0},{5,1},{6,2},{7,3},{8,12},{9,13},{10,... | collective-permute-start | bytes 1179656 | tf_op jit(solution)/shard_map/ppermute | solution.py:61
  4.5 0.0 collective-permute-done.2.refs_2_.refs_1_
  4.5 0.0 copy-start.2
  4.5 0.7 %copy-done.2 = s32[9,6]{0,1:T(8,128)S(1)} copy-done((s32[9,6]{0,1:T(8,128)S(1)}, s32[9,6]{0,1:T(8,128)}, u32[]{:S(2)}) %copy-start.2) | copy-done | bytes 240
  5.2 0.0 copy-start.3
  5.2 0.7 %copy-done.3 = s32[4]{0:T(128)S(1)} copy-done((s32[4]{0:T(128)S(1)}, s32[4]{0:T(128)}, u32[]{:S(2)}) %copy-start.3) | copy-done | bytes 40
  5.8 0.0 copy-start.4
  5.8 0.7 %copy-done.4 = f32[8]{0:T(128)S(1)} copy-done((f32[8]{0:T(128)S(1)}, f32[8]{0:T(128)}, u32[]{:S(2)}) %copy-start.4) | copy-done | bytes 56
  6.5 0.7 %shard_map.46.refs_1_ = bf16[32,512]{1,0:T(8,128)(2,1)S(1)} custom-call(s32[4]{0:T(128)S(1)} %copy-done.3, s32[6,9]{1,0:T(8,128)S(1)} %bitcast.8, f32[8]{0:T(128)S(1)} %copy-done.4), custom_call_target="tpu_custom_call" | custom-call | tf_op jit(solution)/shard_map/pallas_call | solution.py:22
  7.2 0.1 collective-permute-start.3
  7.2 0.6 %collective-permute-start.4 = (bf16[32,512]{1,0:T(8,128)(2,1)S(1)}, bf16[32,512]{1,0:T(8,128)(2,1)S(1)}, u32[]{:S(2)}, u32[]{:S(2)}) collective-permute-start(bf16[32,512]{1,0:T(8,128)(2,1)S(1)} %shard_map.46.refs_1_), channel_id=1, source_target_pairs={{0,2},{1,3},{2,0},{3,1},{4,6},{5,7},{6,4},{7,5},{8,10},{9,11},{10,... | collective-permute-start | bytes 98312 | tf_op jit(solution)/shard_map/ppermute | solution.py:61
  7.8 1.5 %collective-permute-start.8 = (bf16[32,512]{1,0:T(8,128)(2,1)S(1)}, bf16[32,512]{1,0:T(8,128)(2,1)S(1)}, u32[]{:S(2)}, u32[]{:S(2)}) collective-permute-start(bf16[32,512]{1,0:T(8,128)(2,1)S(1)} %shard_map.46.refs_1_), channel_id=1, source_target_pairs={{0,4},{1,5},{2,6},{3,7},{4,0},{5,1},{6,2},{7,3},{8,12},{9,13},{10,... | collective-permute-start | bytes 98312 | tf_op jit(solution)/shard_map/ppermute | solution.py:61
  9.3 0.0 collective-permute-done.3.refs_3_
  9.3 0.0 copy-start
  9.3 1.0 %copy-done = bf16[384,512]{1,0:T(8,128)(2,1)S(1)} copy-done((bf16[384,512]{1,0:T(8,128)(2,1)S(1)}, bf16[384,512]{1,0:T(8,128)(2,1)}, u32[]{:S(2)}) %copy-start) | copy-done | bytes 393240
  10.3 0.0 copy-start.1
  10.3 2.6 %shard_map.47 = (bf16[34,432,128]{2,1,0:T(8,128)(2,1)S(1)}, bf16[32,32,128]{2,1,0:T(8,128)(2,1)S(1)}, f32[1008,384]{1,0:T(8,128)S(1)}, f32[6,8,128]{2,1,0:T(8,128)S(1)}) custom-call(bf16[384,512]{1,0:T(8,128)(2,1)S(1)} %copy-done, bf16[32,512]{1,0:T(8,128)(2,1)S(1)} %shard_map.46.refs_1_, bf16[384,512]{1,0:T(8,128)(2,1)S(1)} %collective-permute-done.2.refs_2_.refs_1_, ...), custom_call_target="tpu_custom_call" | custom-call | tf_op jit(solution)/shard_map/pallas_call | solution.py:22
  12.9 0.2 collective-permute-done.refs_2_.refs_0_
  13.1 1.6 %collective-permute-done.1.refs_3_.refs_0_ = bf16[384,512]{1,0:T(8,128)(2,1)S(1)} collective-permute-done((bf16[384,512]{1,0:T(8,128)(2,1)}, bf16[384,512]{1,0:T(8,128)(2,1)S(1)}, u32[]{:S(2)}, u32[]{:S(2)}) %collective-permute-start.1) | collective-permute-done | bytes 393248 | tf_op jit(solution)/shard_map/ppermute | solution.py:61
  14.8 0.0 collective-permute-done.4.refs_1_
  14.8 0.3 collective-permute-done.8.refs_1_
  15.1 0.1 pad_maximum_fusion
  15.2 0.1 collective-permute-start.9
  15.3 1.6 %collective-permute-start.5 = (bf16[208,512]{1,0:T(8,128)(2,1)S(1)}, bf16[208,512]{1,0:T(8,128)(2,1)S(1)}, u32[]{:S(2)}, u32[]{:S(2)}) collective-permute-start(bf16[208,512]{1,0:T(8,128)(2,1)S(1)} %pad_maximum_fusion.2), channel_id=1, source_target_pairs={{0,4},{1,5},{2,6},{3,7},{4,0},{5,1},{6,2},{7,3},{8,12},{9,13},{10,... | collective-permute-start | bytes 638984 | tf_op jit(solution)/shard_map/ppermute | solution.py:61
  16.9 0.5 collective-permute-start.6
  17.4 0.0 copy-done.1
  17.5 3.8 %collective-permute-start.7 = (bf16[96,512]{1,0:T(8,128)(2,1)S(1)}, bf16[96,512]{1,0:T(8,128)(2,1)S(1)}, u32[]{:S(2)}, u32[]{:S(2)}) collective-permute-start(bf16[96,512]{1,0:T(8,128)(2,1)S(1)} %shard_map.48), channel_id=1, source_target_pairs={{0,24},{1,30},{2,26},{3,11},{4,28},{5,13},{6,9},{7,15},{8,0},{9,6}... | collective-permute-start | bytes 294920 | tf_op jit(solution)/shard_map/ppermute | solution.py:416
  21.3 0.0 collective-permute-done.9.refs_2_
  21.3 3.7 %shard_map.49 = (bf16[34,432,128]{2,1,0:T(8,128)(2,1)S(1)}, bf16[32,32,128]{2,1,0:T(8,128)(2,1)S(1)}, f32[1008,384]{1,0:T(8,128)S(1)}, f32[6,8,128]{2,1,0:T(8,128)S(1)}) custom-call(bf16[384,512]{1,0:T(8,128)(2,1)S(1)} %collective-permute-done.refs_2_.refs_0_, ...), custom_call_target="tpu_custom_call", output_to_operand_aliasing={{0}: (3, {}), {1}: (4, {})} | custom-call | tf_op jit(solution)/shard_map/pallas_call | solution.py:22
  25.1 0.0 collective-permute-done.7.refs_2_
  25.1 0.0 collective-permute-done.5.refs_0_
  25.1 0.0 collective-permute-done.6.refs_1_
  25.1 1.0 %collective-permute-start.10 = (bf16[512,512]{1,0:T(8,128)(2,1)S(1)}, bf16[512,512]{1,0:T(8,128)(2,1)S(1)}, u32[]{:S(2)}, u32[]{:S(2)}) collective-permute-start(bf16[512,512]{1,0:T(8,128)(2,1)S(1)} %pad_maximum_fusion.1), channel_id=1, source_target_pairs={{0,1},{1,0},{2,3},{3,2},{4,5},{5,4},{6,7},{7,6},{8,9},{9,8},{10,11... | collective-permute-start | bytes 1572872 | tf_op jit(solution)/shard_map/ppermute | solution.py:61
  26.2 2.7 %shard_map.50 = (bf16[34,432,128]{2,1,0:T(8,128)(2,1)S(1)}, bf16[32,32,128]{2,1,0:T(8,128)(2,1)S(1)}, f32[1008,384]{1,0:T(8,128)S(1)}, f32[6,8,128]{2,1,0:T(8,128)S(1)}) custom-call(bf16[384,512]{1,0:T(8,128)(2,1)S(1)} %collective-permute-done.1.refs_3_.refs_0_, ...), custom_call_target="tpu_custom_call", output_to_operand_aliasing={{0}: (3, {}), {1}: (4, {})} | custom-call | tf_op jit(solution)/shard_map/pallas_call | solution.py:22
  28.9 0.0 collective-permute-done.10.refs_3_
  28.9 6.0 %shard_map.51 = (bf16[34,432,128]{2,1,0:T(8,128)(2,1)S(1)}, bf16[32,32,128]{2,1,0:T(8,128)(2,1)S(1)}, f32[256,384]{1,0:T(8,128)S(1)}, f32[3,256,384]{2,1,0:T(8,128)S(1)}, f32[8,128]{1,0:T(8,128)S(1)}) custom-call(bf16[208,512]{1,0:T(8,128)(2,1)S(1)} %collective-permute-done.5.refs_0_, ...), custom_call_target="tpu_custom_call", output_to_operand_aliasing={{0}: (4, {}), {1}: (5, {})} | custom-call | tf_op jit(solution)/shard_map/pallas_call | solution.py:22
  34.8 0.1 convert_element_type.12
  34.9 0.1 slice_bitcast_fusion
  35.1 0.9 %collective-permute-start.11 = (f16[256,384]{1,0:T(8,128)(2,1)S(1)}, f16[256,384]{1,0:T(8,128)(2,1)S(1)}, u32[]{:S(2)}, u32[]{:S(2)}) collective-permute-start(f16[256,384]{1,0:T(8,128)(2,1)S(1)} %get-tuple-element.59), channel_id=1, source_target_pairs={{0,16},{1,17},{2,18},{3,19},{4,20},{5,21},{6,22},{7,23},{8,24},{9,... | collective-permute-start | bytes 589832 | tf_op jit(solution)/shard_map/ppermute | solution.py:440
  35.9 1.7 %collective-permute-start.12 = (f16[256,384]{1,0:T(8,128)(2,1)S(1)}, f16[256,384]{1,0:T(8,128)(2,1)S(1)}, u32[]{:S(2)}, u32[]{:S(2)}) collective-permute-start(f16[256,384]{1,0:T(8,128)(2,1)S(1)} %get-tuple-element.58), channel_id=1, source_target_pairs={{0,24},{1,25},{2,26},{3,27},{4,28},{5,29},{6,30},{7,31},{8,16},{9,... | collective-permute-start | bytes 589832 | tf_op jit(solution)/shard_map/ppermute | solution.py:440
  37.7 1.0 %collective-permute-start.13 = (f16[256,384]{1,0:T(8,128)(2,1)S(1)}, f16[256,384]{1,0:T(8,128)(2,1)S(1)}, u32[]{:S(2)}, u32[]{:S(2)}) collective-permute-start(f16[256,384]{1,0:T(8,128)(2,1)S(1)} %get-tuple-element.57), channel_id=1, source_target_pairs={{0,8},{1,9},{2,10},{3,11},{4,12},{5,13},{6,14},{7,15},{8,0},{9,1},... | collective-permute-start | bytes 589832 | tf_op jit(solution)/shard_map/ppermute | solution.py:440
  38.6 13.1 %collective-permute-done.11 = f16[256,384]{1,0:T(8,128)(2,1)S(1)} collective-permute-done((f16[256,384]{1,0:T(8,128)(2,1)S(1)}, f16[256,384]{1,0:T(8,128)(2,1)S(1)}, u32[]{:S(2)}, u32[]{:S(2)}) %collective-permute-start.11) | collective-permute-done | bytes 196640 | tf_op jit(solution)/shard_map/ppermute | solution.py:440
  51.7 0.0 collective-permute-done.12
  51.8 0.9 %collective-permute-done.13 = f16[256,384]{1,0:T(8,128)(2,1)S(1)} collective-permute-done((f16[256,384]{1,0:T(8,128)(2,1)S(1)}, f16[256,384]{1,0:T(8,128)(2,1)S(1)}, u32[]{:S(2)}, u32[]{:S(2)}) %collective-permute-start.13) | collective-permute-done | bytes 196640 | tf_op jit(solution)/shard_map/ppermute | solution.py:440
  52.7 1.2 %shard_map.52 = f32[12,21,384]{2,1,0:T(8,128)} custom-call(f32[256,384]{1,0:T(8,128)S(1)} %get-tuple-element.54.refs_0_, f32[256,384]{1,0:T(8,128)S(1)} %convert_element_type.13.refs_1_, f32[256,384]{1,0:T(8,128)S(1)} %convert_element_type.14.refs_2_, f32[256,384]{1,0:T(8,128)S(1)} %convert_element_type.15.refs_3_, f32[8,128]{1,0:T(8,128)S(1)} %get-tuple-element.56.refs_4_), custom_call_target="tpu_custom_call" | custom-call | tf_op jit(solution)/shard_map/pallas_call | solution.py:22
  (8 shorter events, 0.2 us)
Async XLA Ops:
  0.0 4.5 %collective-permute-start.2 = (bf16[384,512]{1,0:T(8,128)(2,1)}, bf16[384,512]{1,0:T(8,128)(2,1)S(1)}, u32[]{:S(2)}, u32[]{:S(2)}) collective-permute-start(bf16[384,512]{1,0:T(8,128)(2,1)} %refs_0_.3), channel_id=1, source_target_pairs={{0,1},{1,0},{2,3},{3,2},{4,5},{5,4},{6,7},{7,6},{8,9},{9,8},{10,11... | collective-permute-start | bytes 1179656 | tf_op jit(solution)/shard_map/ppermute | solution.py:61
  0.5 12.7 %collective-permute-start = (bf16[384,512]{1,0:T(8,128)(2,1)}, bf16[384,512]{1,0:T(8,128)(2,1)S(1)}, u32[]{:S(2)}, u32[]{:S(2)}) collective-permute-start(bf16[384,512]{1,0:T(8,128)(2,1)} %refs_0_.3), channel_id=1, source_target_pairs={{0,2},{1,3},{2,0},{3,1},{4,6},{5,7},{6,4},{7,5},{8,10},{9,11},{10,... | collective-permute-start | bytes 1179656 | tf_op jit(solution)/shard_map/ppermute | solution.py:61
  2.9 11.8 %collective-permute-start.1 = (bf16[384,512]{1,0:T(8,128)(2,1)}, bf16[384,512]{1,0:T(8,128)(2,1)S(1)}, u32[]{:S(2)}, u32[]{:S(2)}) collective-permute-start(bf16[384,512]{1,0:T(8,128)(2,1)} %refs_0_.3), channel_id=1, source_target_pairs={{0,4},{1,5},{2,6},{3,7},{4,0},{5,1},{6,2},{7,3},{8,12},{9,13},{10,... | collective-permute-start | bytes 1179656 | tf_op jit(solution)/shard_map/ppermute | solution.py:61
  4.5 0.7 %copy-start.2 = (s32[9,6]{0,1:T(8,128)S(1)}, s32[9,6]{0,1:T(8,128)}, u32[]{:S(2)}) copy-start(s32[9,6]{0,1:T(8,128)} %param.6) | copy-start | bytes 652
  5.2 0.7 %copy-start.3 = (s32[4]{0:T(128)S(1)}, s32[4]{0:T(128)}, u32[]{:S(2)}) copy-start(s32[4]{0:T(128)} %region) | copy-start | bytes 52
  5.8 0.7 %copy-start.4 = (f32[8]{0:T(128)S(1)}, f32[8]{0:T(128)}, u32[]{:S(2)}) copy-start(f32[8]{0:T(128)} %table.1) | copy-start | bytes 100
  7.2 2.1 %collective-permute-start.3 = (bf16[32,512]{1,0:T(8,128)(2,1)S(1)}, bf16[32,512]{1,0:T(8,128)(2,1)S(1)}, u32[]{:S(2)}, u32[]{:S(2)}) collective-permute-start(bf16[32,512]{1,0:T(8,128)(2,1)S(1)} %shard_map.46.refs_1_), channel_id=1, source_target_pairs={{0,1},{1,0},{2,3},{3,2},{4,5},{5,4},{6,7},{7,6},{8,9},{9,8},{10,11... | collective-permute-start | bytes 98312 | tf_op jit(solution)/shard_map/ppermute | solution.py:61
  7.2 7.5 %collective-permute-start.4 = (bf16[32,512]{1,0:T(8,128)(2,1)S(1)}, bf16[32,512]{1,0:T(8,128)(2,1)S(1)}, u32[]{:S(2)}, u32[]{:S(2)}) collective-permute-start(bf16[32,512]{1,0:T(8,128)(2,1)S(1)} %shard_map.46.refs_1_), channel_id=1, source_target_pairs={{0,2},{1,3},{2,0},{3,1},{4,6},{5,7},{6,4},{7,5},{8,10},{9,11},{10,... | collective-permute-start | bytes 98312 | tf_op jit(solution)/shard_map/ppermute | solution.py:61
  7.8 7.3 %collective-permute-start.8 = (bf16[32,512]{1,0:T(8,128)(2,1)S(1)}, bf16[32,512]{1,0:T(8,128)(2,1)S(1)}, u32[]{:S(2)}, u32[]{:S(2)}) collective-permute-start(bf16[32,512]{1,0:T(8,128)(2,1)S(1)} %shard_map.46.refs_1_), channel_id=1, source_target_pairs={{0,4},{1,5},{2,6},{3,7},{4,0},{5,1},{6,2},{7,3},{8,12},{9,13},{10,... | collective-permute-start | bytes 98312 | tf_op jit(solution)/shard_map/ppermute | solution.py:61
  9.3 1.0 %copy-start = (bf16[384,512]{1,0:T(8,128)(2,1)S(1)}, bf16[384,512]{1,0:T(8,128)(2,1)}, u32[]{:S(2)}) copy-start(bf16[384,512]{1,0:T(8,128)(2,1)} %refs_0_.3) | copy-start | bytes 1179652
  10.3 7.1 %copy-start.1 = (bf16[384,512]{1,0:T(8,128)(2,1)S(1)}, bf16[384,512]{1,0:T(8,128)(2,1)}, u32[]{:S(2)}) copy-start(bf16[384,512]{1,0:T(8,128)(2,1)} %refs_0_.3) | copy-start | bytes 1179652
  15.2 6.2 %collective-permute-start.9 = (bf16[832,512]{1,0:T(8,128)(2,1)S(1)}, bf16[832,512]{1,0:T(8,128)(2,1)S(1)}, u32[]{:S(2)}, u32[]{:S(2)}) collective-permute-start(bf16[832,512]{1,0:T(8,128)(2,1)S(1)} %pad_maximum_fusion), channel_id=1, source_target_pairs={{0,1},{1,0},{2,3},{3,2},{4,5},{5,4},{6,7},{7,6},{8,9},{9,8},{10,11... | collective-permute-start | bytes 2555912 | tf_op jit(solution)/shard_map/ppermute | solution.py:61
  15.3 9.8 %collective-permute-start.5 = (bf16[208,512]{1,0:T(8,128)(2,1)S(1)}, bf16[208,512]{1,0:T(8,128)(2,1)S(1)}, u32[]{:S(2)}, u32[]{:S(2)}) collective-permute-start(bf16[208,512]{1,0:T(8,128)(2,1)S(1)} %pad_maximum_fusion.2), channel_id=1, source_target_pairs={{0,4},{1,5},{2,6},{3,7},{4,0},{5,1},{6,2},{7,3},{8,12},{9,13},{10,... | collective-permute-start | bytes 638984 | tf_op jit(solution)/shard_map/ppermute | solution.py:61
  16.9 8.2 %collective-permute-start.6 = (bf16[208,512]{1,0:T(8,128)(2,1)S(1)}, bf16[208,512]{1,0:T(8,128)(2,1)S(1)}, u32[]{:S(2)}, u32[]{:S(2)}) collective-permute-start(bf16[208,512]{1,0:T(8,128)(2,1)S(1)} %slice.16), channel_id=1, source_target_pairs={{0,2},{1,3},{2,0},{3,1},{4,6},{5,7},{6,4},{7,5},{8,10},{9,11},{10,... | collective-permute-start | bytes 638984 | tf_op jit(solution)/shard_map/ppermute | solution.py:61
  17.5 7.6 %collective-permute-start.7 = (bf16[96,512]{1,0:T(8,128)(2,1)S(1)}, bf16[96,512]{1,0:T(8,128)(2,1)S(1)}, u32[]{:S(2)}, u32[]{:S(2)}) collective-permute-start(bf16[96,512]{1,0:T(8,128)(2,1)S(1)} %shard_map.48), channel_id=1, source_target_pairs={{0,24},{1,30},{2,26},{3,11},{4,28},{5,13},{6,9},{7,15},{8,0},{9,6}... | collective-permute-start | bytes 294920 | tf_op jit(solution)/shard_map/ppermute | solution.py:416
  25.1 3.7 %collective-permute-start.10 = (bf16[512,512]{1,0:T(8,128)(2,1)S(1)}, bf16[512,512]{1,0:T(8,128)(2,1)S(1)}, u32[]{:S(2)}, u32[]{:S(2)}) collective-permute-start(bf16[512,512]{1,0:T(8,128)(2,1)S(1)} %pad_maximum_fusion.1), channel_id=1, source_target_pairs={{0,1},{1,0},{2,3},{3,2},{4,5},{5,4},{6,7},{7,6},{8,9},{9,8},{10,11... | collective-permute-start | bytes 1572872 | tf_op jit(solution)/shard_map/ppermute | solution.py:61
  35.1 16.6 %collective-permute-start.11 = (f16[256,384]{1,0:T(8,128)(2,1)S(1)}, f16[256,384]{1,0:T(8,128)(2,1)S(1)}, u32[]{:S(2)}, u32[]{:S(2)}) collective-permute-start(f16[256,384]{1,0:T(8,128)(2,1)S(1)} %get-tuple-element.59), channel_id=1, source_target_pairs={{0,16},{1,17},{2,18},{3,19},{4,20},{5,21},{6,22},{7,23},{8,24},{9,... | collective-permute-start | bytes 589832 | tf_op jit(solution)/shard_map/ppermute | solution.py:440
  35.9 15.8 %collective-permute-start.12 = (f16[256,384]{1,0:T(8,128)(2,1)S(1)}, f16[256,384]{1,0:T(8,128)(2,1)S(1)}, u32[]{:S(2)}, u32[]{:S(2)}) collective-permute-start(f16[256,384]{1,0:T(8,128)(2,1)S(1)} %get-tuple-element.58), channel_id=1, source_target_pairs={{0,24},{1,25},{2,26},{3,27},{4,28},{5,29},{6,30},{7,31},{8,16},{9,... | collective-permute-start | bytes 589832 | tf_op jit(solution)/shard_map/ppermute | solution.py:440
  37.7 15.1 %collective-permute-start.13 = (f16[256,384]{1,0:T(8,128)(2,1)S(1)}, f16[256,384]{1,0:T(8,128)(2,1)S(1)}, u32[]{:S(2)}, u32[]{:S(2)}) collective-permute-start(f16[256,384]{1,0:T(8,128)(2,1)S(1)} %get-tuple-element.57), channel_id=1, source_target_pairs={{0,8},{1,9},{2,10},{3,11},{4,12},{5,13},{6,14},{7,15},{8,0},{9,1},... | collective-permute-start | bytes 589832 | tf_op jit(solution)/shard_map/ppermute | solution.py:440
